TPU v7x, 512 devices: a whole 4x8x8 slice. The times are simulated.
512 devices in a mesh: chol: 16 (over z_lo, x, core), occ: 32 (over y, z_hi).
Axes of the slice: x: 4, y: 8, z: 8 (z_hi: 4, z_lo: 2; z = z_hi * 2 + z_lo), core: 2. Of those that a mesh axis runs over, the one named last changes fastest.
Arguments:
- vectors: bfloat16 [128, 1536, 1536], P('chol', 'occ'), may hold values from -0.3984375 to 0.3984375
- coeffs: bfloat16 [2, 1536, 256], P(None, 'occ'), may hold values from -0.15625 to 0.15625
Outputs:
- exchange: float32 [2, 1536, 1536], P(None, 'occ', 'chol')
- coulomb: float32 [1536, 1536], P('occ', 'chol')
All inputs are finite; a program needn't handle non-finite values.
Results may differ from a plain program's by a relative error of at most 0.0028.
Values may be sent and summed in bfloat16 or wider, within the bound.
No kernel may reach another device: no remote copies, remote signals or barrier semaphores. Data moves between devices by JAX's collectives and lax.ppermute only.
A program may use at most 128 MiB of HBM per device.

v0:
```python
import jax
import jax.numpy as jnp
from jax import lax
from jax.sharding import PartitionSpec as P


def exchange_columns(own_slab, other_slab):
    real_part = jnp.einsum(
        "pcim,pcin->mn", own_slab, other_slab, preferred_element_type=jnp.float32
    )
    imag_part = jnp.einsum(
        "pim,pin->mn", own_slab[:, 1], other_slab[:, 0], preferred_element_type=jnp.float32
    ) - jnp.einsum(
        "pim,pin->mn", own_slab[:, 0], other_slab[:, 1], preferred_element_type=jnp.float32
    )
    return jnp.stack([real_part, imag_part])


def on_device(vectors, coeffs):
    full_coeffs = lax.all_gather(coeffs, "occ", axis=1, tiled=True)
    own_slab = jnp.einsum(
        "pnm,cmi->pcin", vectors, full_coeffs, preferred_element_type=jnp.float32
    ).astype(jnp.bfloat16)
    weight_terms = jnp.einsum(
        "cni,pcin->p", coeffs.astype(jnp.float32), own_slab.astype(jnp.float32)
    )
    vector_weight = lax.psum(weight_terms, "occ")
    exchange_part = exchange_columns(own_slab, lax.all_gather(own_slab, "occ", axis=3, tiled=True))
    coulomb_part = jnp.sum(vectors.astype(jnp.float32) * vector_weight[:, None, None], axis=0)[None]
    exchange_total, coulomb_total = lax.psum((exchange_part, coulomb_part), "chol")
    column_count = exchange_total.shape[2] // lax.axis_size("chol")
    column_start = lax.axis_index("chol") * column_count
    exchange = lax.dynamic_slice_in_dim(exchange_total, column_start, column_count, 2)
    coulomb = lax.dynamic_slice_in_dim(coulomb_total, column_start, column_count, 2)
    return (exchange, coulomb[0])


def solution(mesh):
    placed = (P("chol", "occ", None), P(None, "occ", None))
    return jax.shard_map(
        on_device,
        mesh=mesh,
        in_specs=placed,
        out_specs=(P(None, "occ", "chol"), P("occ", "chol")),
        check_vma=False,
    )
```

profile of v0, /device:TPU:6, one launch (start us, length us, event | category | flops | bytes accessed | tf_op | source)
XLA Modules:
  0.0 428.8 jit_solution(6514006979579966497)
XLA Ops:
  7.2 0.0 copy-start.3
  7.2 0.0 copy-start.2
  7.2 0.0 all-gather.3.cloned.1.call-start
  7.2 0.7 all-gather.3.cloned.1.call-update
  7.9 0.0 all-gather.5.cloned.1.call-start
  8.0 92.8 %all-gather.3.cloned.1.call-done = bf16[2,1536,256]{2,1,0:T(8,128)(2,1)} async-done(((bf16[2,48,256]{2,1,0:T(8,128)(2,1)}), bf16[2,1536,256]{2,1,0:T(8,128)(2,1)}) %all-gather.3.cloned.1.call-update) | async-done | bytes 1572880 | tf_op jit(solution)/shard_map/all_gather | solution.py:20
  100.8 3.3 fusion.11
  104.1 0.0 copy-start.1
  104.1 0.0 all-gather.5.cloned.1.call-update
  104.1 0.0 all-reduce.3.cloned.1.call-start
  104.1 0.0 copy-done.3
  104.1 1.4 convolution_bitcast_fusion.1
  105.6 82.1 %psum.22 = f32[8]{0:T(128)S(1)} all-reduce(f32[8]{0:T(128)S(1)} %convolution_bitcast_fusion.1), channel_id=1, replica_groups=mesh['chol'=16,'occ'=32] {'occ'}, use_global_device_ids=true, to_apply=%region_1.0 | all-reduce | flops 8 | bytes 64 | tf_op jit(solution)/shard_map/psum | solution.py:27
  187.7 0.0 copy-done.2
  187.7 1.0 multiply_reduce_fusion
  188.7 91.6 %all-gather.5.cloned.1.call-done = bf16[8,2,256,1536]{2,3,0,1:T(8,128)(2,1)} async-done(((bf16[8,2,256,48]{2,3,0,1:T(8,128)(2,1)}), bf16[8,2,256,1536]{2,3,0,1:T(8,128)(2,1)}) %all-gather.5.cloned.1.call-update) | async-done | bytes 12582928 | tf_op jit(solution)/shard_map/all_gather | solution.py:28
  280.3 4.8 %fusion.5 = f32[48,1536]{1,0:T(8,128)S(1)} fusion(bf16[8,2,256,1536]{2,3,0,1:T(8,128)(2,1)} %all-gather.5.cloned.1.call-done, bf16[8,2,256,48]{2,3,0,1:T(8,128)(2,1)} %fusion.11), kind=kOutput, calls=%fused_computation.8 | convolution fusion | flops 301989888 | bytes 6782976 | tf_op jit(solution)/shard_map/pim,pin->mn/dot_general | solution.py:13
  285.1 0.0 copy-done.1
  285.1 0.0 copy-start
  285.2 8.5 %convolution_bitcast_fusion = f32[1,48,1536]{2,1,0:T(8,128)S(1)} fusion(bf16[8,2,256,48]{2,3,0,1:T(8,128)(2,1)S(1)} %copy-done.1, bf16[8,2,256,1536]{2,3,0,1:T(8,128)(2,1)} %all-gather.5.cloned.1.call-done), kind=kOutput, calls=%fused_computation.9 | convolution fusion | flops 603979776 | bytes 13271040 | tf_op jit(solution)/shard_map/pcim,pcin->mn/dot_general | solution.py:8
  293.6 0.0 copy-done
  293.6 1.9 fusion.4
  295.6 0.9 pad_maximum_fusion
  296.5 0.0 all-reduce.3.cloned.1.call-update
  296.5 122.7 %all-reduce.3.cloned.1.call-done = (f32[2,48,1536]{2,1,0:T(8,128)}, f32[1,48,1536]{2,1,0:T(8,128)}) async-done(((f32[2,48,1536]{2,1,0:T(8,128)}, f32[1,48,1536]{2,1,0:T(8,128)}), (f32[2,48,1536]{2,1,0:T(8,128)}, f32[1,48,1536]{2,1,0:T(8,128)})) %all-reduce.3.cloned.1.call-update) | async-done | bytes 884752 | tf_op jit(solution)/shard_map/psum | solution.py:30
  419.2 1.6 constant_dynamic-slice_fusion
  420.8 1.5 dynamic-slice_bitcast_fusion
Async XLA Ops:
  7.2 97.0 %copy-start.3 = (bf16[2,48,256]{2,1,0:T(8,128)(2,1)S(1)}, bf16[2,48,256]{2,1,0:T(8,128)(2,1)}, u32[]{:S(2)}) copy-start(bf16[2,48,256]{2,1,0:T(8,128)(2,1)} %param.3) | copy-start | bytes 147460
  7.2 180.5 %copy-start.2 = (bf16[8,48,1536]{2,1,0:T(8,128)(2,1)S(1)}, bf16[8,48,1536]{2,1,0:T(8,128)(2,1)}, u32[]{:S(2)}) copy-start(bf16[8,48,1536]{2,1,0:T(8,128)(2,1)} %param.2) | copy-start | bytes 3538948
  7.2 93.6 %all-gather.3.cloned.1.call-start = ((), (), s32[]{:S(2)}) async-start(), calls=%async_computation | async-start | bytes 1622016 | tf_op jit(solution)/shard_map/all_gather | solution.py:20
  7.9 272.4 %all-gather.5.cloned.1.call-start = ((), (), s32[]{:S(2)}) async-start(), calls=%async_computation.1 | async-start | bytes 12976128 | tf_op jit(solution)/shard_map/all_gather | solution.py:28
  104.1 181.1 %copy-start.1 = (bf16[8,2,256,48]{2,3,0,1:T(8,128)(2,1)S(1)}, bf16[8,2,256,48]{2,3,0,1:T(8,128)(2,1)}, u32[]{:S(2)}) copy-start(bf16[8,2,256,48]{2,3,0,1:T(8,128)(2,1)} %fusion.11) | copy-start | bytes 1179652
  104.1 315.2 %all-reduce.3.cloned.1.call-start = ((), (), s32[]{:S(2)}) async-start(), calls=%async_computation.2 | async-start | bytes 1769472 | tf_op jit(solution)/shard_map/psum | solution.py:30
  285.1 8.5 %copy-start = (bf16[8,2,256,1536]{2,3,0,1:T(8,128)(2,1)S(1)}, bf16[8,2,256,1536]{2,3,0,1:T(8,128)(2,1)}, u32[]{:S(2)}) copy-start(bf16[8,2,256,1536]{2,3,0,1:T(8,128)(2,1)} %all-gather.5.cloned.1.call-done) | copy-start | bytes 37748740
Sparse Core Ops, SparseCore 0:
  11.1 89.5 all-gather.2
  104.2 176.0 all-gather.4
  296.6 122.5 all-reduce.2
where the time goes:
time: 432 us; the launch traced here: 429 us
  waiting for transfers between devices  308 us (71%)
  blocking collectives  82.1 us (19%)
  matrix products  20 us (5%)
  between operations  13.8 us (3%)
    psum x1, waiting for transfers between devices, on_device(): lax.psum((exchange_part, coulomb_part), 'chol')  123 us
    all_gather x1, waiting for transfers between devices, on_device(): full_coeffs = lax.all_gather(coeffs, 'occ', axis=1, tiled=True)  92.8 us
    all_gather x1, waiting for transfers between devices, on_device(): lax.all_gather(own_slab, 'occ', axis=3, tiled=True)  91.6 us
    psum x1, blocking collectives, on_device(): vector_weight = lax.psum(weight_terms, 'occ')  82.1 us
  transfers between devices with their start and end apart: 3, of which 3 were waited for; matrix products, arithmetic and copies ran while one was open for 1% of the time, Pallas kernels for 0%

commit v1 on v0

v1 whole, which is shorter than its diff:
```python
import jax
import jax.numpy as jnp
from jax import lax
from jax.sharding import Mesh
from jax.sharding import PartitionSpec as P

NEAR = ("zl", "x")
FAR = ("y", "zb", "za")
SUMS = ("y", "za")
SWAP = [(0, 1), (1, 0)]


def to_all(block, axes, count):
    return lax.all_to_all(jnp.broadcast_to(block[None], (count,) + block.shape), axes, 0, 0, tiled=True)


def on_device(vectors, coeffs):
    f32, bf16 = jnp.float32, jnp.bfloat16
    core = lax.axis_index("core")
    zb = lax.axis_index("zb")
    count, rows, nao = vectors.shape
    half = coeffs.shape[2] // 2
    wide = 2 * half

    other_vectors = lax.ppermute(vectors, "core", SWAP)
    own = lax.dynamic_slice_in_dim(coeffs, core * half, half, 2)
    own = jnp.concatenate([own[0], own[1]], axis=1)
    full = to_all(own, FAR, 32).reshape(nao, wide)

    def transform(block):
        return jnp.dot(
            block.reshape(count * rows, nao), full, preferred_element_type=f32
        ).astype(bf16).reshape(count, rows, wide)

    mine, other = transform(vectors), transform(other_vectors)
    first = core == 0
    slab = jnp.concatenate([jnp.where(first, mine, other), jnp.where(first, other, mine)])

    terms = jnp.sum(slab.astype(f32) * own.astype(f32)[None], axis=(1, 2))
    terms = jnp.broadcast_to(terms[:, None], (16, 128))
    weights = jnp.sum(to_all(terms, ("core",) + FAR, 64), axis=0)[:, 0]
    weights = lax.dynamic_slice_in_dim(weights, core * count, count, 0)
    coulomb_part = jnp.sum(vectors.astype(f32) * weights[:, None, None], axis=0)
    coulomb_part = coulomb_part.reshape(rows, 16, nao // 16).transpose(1, 0, 2)
    coulomb = jnp.sum(lax.all_to_all(coulomb_part, NEAR + ("core",), 0, 0, tiled=True), axis=0)

    pieces = jnp.broadcast_to(slab.reshape(8, 1, 2, rows, wide), (8, 2, 2, rows, wide)).reshape(32, rows, wide)
    got = lax.all_to_all(pieces, FAR, 0, 0, tiled=True)
    got_other = lax.ppermute(got, "core", SWAP)

    def parts(block):
        block = block.reshape(8, 2, 2 * rows, wide)
        row_part = lax.dynamic_index_in_dim(block, zb, 1, keepdims=False)
        column_part = lax.dynamic_index_in_dim(block, core, 1, keepdims=False)
        return row_part.reshape(16 * rows, wide), column_part

    row_a, column_a = parts(got)
    row_b, column_b = parts(got_other)
    row_side = jnp.concatenate([row_a, row_b], axis=1)

    def turned(block):
        return jnp.concatenate([-block[..., half:], block[..., :half]], axis=-1)

    real = jnp.concatenate([column_a, column_b], axis=-1)
    imag = jnp.concatenate([turned(column_a), turned(column_b)], axis=-1)
    column_side = jnp.stack([real, imag], axis=1).reshape(32 * rows, 2 * wide)
    exchange = lax.dot_general(
        column_side, row_side, (((1,), (1,)), ((), ())), preferred_element_type=f32
    ).astype(bf16).reshape(8, 4 * rows, 16 * rows)
    exchange = jnp.sum(lax.all_to_all(exchange, NEAR, 0, 0, tiled=True).astype(f32), axis=0)
    exchange = exchange.astype(bf16).T.reshape(16, rows, 4 * rows)
    exchange = jnp.sum(lax.all_to_all(exchange, SUMS, 0, 0, tiled=True).astype(f32), axis=0)
    exchange = exchange.reshape(rows, 2, 2 * rows).transpose(1, 0, 2)
    return exchange, coulomb


def solution(mesh):
    fine = Mesh(mesh.devices.reshape(2, 4, 2, 8, 2, 2), ("zl", "x", "core", "y", "zb", "za"))
    chol = ("zl", "x", "core")
    return jax.shard_map(
        on_device,
        mesh=fine,
        in_specs=(P(chol, FAR, None), P(None, FAR, None)),
        out_specs=(P(None, FAR, chol), P(FAR, chol)),
        check_vma=False,
    )
```

time: 432 us -> 172 us (0.40)
  waiting for transfers between devices: 308 us -> 84.9 us
  blocking collectives: 82.1 us -> 29.7 us
  starting transfers between devices: 0.12 us -> 42 us
  matrix products: 20 us -> 4.08 us
  between operations: 13.8 us -> 0.83 us
    all_gather x2 -> x0, waiting for transfers between devices: 184 us -> none  [the longest x1 92.8 us: on_device(): full_coeffs = lax.all_gather(coeffs, 'occ', axis=1, tiled=True)]
    psum x1 -> x0, waiting for transfers between devices: 123 us -> none  [on_device(): lax.psum((exchange_part, coulomb_part), 'chol')]
    all_to_all x0 -> x5, waiting for transfers between devices: none -> 84.9 us  [the longest x2 37.6 us: to_all(): lax.all_to_all(jnp.broadcast_to(block[None], (count,) + block.shape), axe...]
    psum x1 -> x0, blocking collectives: 82.1 us -> none  [on_device(): vector_weight = lax.psum(weight_terms, 'occ')]
    all_to_all x0 -> x5, starting transfers between devices: none -> 38.2 us  [the longest x2 24.1 us: to_all(): lax.all_to_all(jnp.broadcast_to(block[None], (count,) + block.shape), axe...]
    all_to_all x0 -> x1, blocking collectives: none -> 29.7 us  [on_device(): got = lax.all_to_all(pieces, FAR, 0, 0, tiled=True)]
    dot_general x5 -> x3, matrix products: 20 us -> 4.08 us  [the longest x1 2.84 us: on_device(): lax.dot_general(column_side, row_side, (((1,), (1,)), ((), ())), preferre...]
  transfers between devices with their start and end apart: 3 -> 7, of which waited for: 3 -> 5; matrix products, arithmetic and copies ran while one was open for 1% -> 6% of each run, Pallas kernels for 0% -> 0%
where the time goes in v1:
time: 172 us; the launch traced here: 171 us
  waiting for transfers between devices  84.9 us (49%)
  starting transfers between devices  42 us (24%)
  blocking collectives  29.7 us (17%)
  local copies, waits for them, and re-layouts  5.92 us (3%)
  matrix products  4.08 us (2%)
  other arithmetic  3.46 us (2%)
    all_to_all x2, waiting for transfers between devices, to_all(): lax.all_to_all(jnp.broadcast_to(block[None], (count,) + block.shape), axe...  37.6 us
    all_to_all x1, blocking collectives, on_device(): got = lax.all_to_all(pieces, FAR, 0, 0, tiled=True)  29.7 us
    all_to_all x1, waiting for transfers between devices, on_device(): lax.all_to_all(exchange, NEAR, 0, 0, tiled=True).astype(f32)  25.6 us
    all_to_all x2, starting transfers between devices, to_all(): lax.all_to_all(jnp.broadcast_to(block[None], (count,) + block.shape), axe...  24.1 us
    all_to_all x1, waiting for transfers between devices, on_device(): lax.all_to_all(exchange, SUMS, 0, 0, tiled=True).astype(f32)  15.7 us
    all_to_all x1, waiting for transfers between devices, on_device(): lax.all_to_all(coulomb_part, NEAR + ('core',), 0, 0, tiled=True)  5.96 us
    all_to_all x1, starting transfers between devices, on_device(): lax.all_to_all(coulomb_part, NEAR + ('core',), 0, 0, tiled=True)  4.98 us
    all_to_all x1, starting transfers between devices, on_device(): lax.all_to_all(exchange, NEAR, 0, 0, tiled=True).astype(f32)  4.78 us
  transfers between devices with their start and end apart: 7, of which 5 were waited for; matrix products, arithmetic and copies ran while one was open for 6% of the time, Pallas kernels for 0%

profile of v1, /device:TPU:6, one launch (start us, length us, event | category | flops | bytes accessed | tf_op | source)
XLA Modules:
  0.0 171.0 jit_solution(7814767909497574837)
XLA Ops:
  0.6 0.0 copy-start
  0.6 0.8 dynamic-slice_bitcast_fusion.3
  1.5 0.9 broadcast_in_dim.6
  2.4 16.0 %all-to-all-start = ((bf16[32,48,256]{2,1,0:T(8,128)(2,1)}), bf16[32,48,256]{2,1,0:T(8,128)(2,1)S(1)}, u32[]{:S(2)}, u32[]{:S(2)}) async-start(bf16[32,48,256]{2,1,0:T(8,128)(2,1)} %broadcast_in_dim.6), calls=%async_computation | async-start | bytes 1572864 | tf_op jit(solution)/shard_map/all_to_all | solution.py:14
  18.4 0.0 copy-done
  18.4 1.9 %collective-permute-start = (bf16[8,48,1536]{2,1,0:T(8,128)(2,1)S(1)}, bf16[8,48,1536]{2,1,0:T(8,128)(2,1)S(1)}, u32[]{:S(2)}, u32[]{:S(2)}) collective-permute-start(bf16[8,48,1536]{2,1,0:T(8,128)(2,1)S(1)} %copy-done), channel_id=1, source_target_pairs={{0,32},{32,0},{1,33},{33,1},{2,34},{34,2},{3,35},{35,3},{4,36},{36... | collective-permute-start | bytes 3538952 | tf_op jit(solution)/shard_map/ppermute | solution.py:25
  20.3 21.9 %all-to-all-done = bf16[32,48,256]{2,1,0:T(8,128)(2,1)S(1)} async-done(((bf16[32,48,256]{2,1,0:T(8,128)(2,1)}), bf16[32,48,256]{2,1,0:T(8,128)(2,1)S(1)}, u32[]{:S(2)}, u32[]{:S(2)}) %all-to-all-start) | async-done | bytes 786464 | tf_op jit(solution)/shard_map/all_to_all | solution.py:14
  42.2 0.6 convolution_convert_fusion.2
  42.8 0.0 collective-permute-done
  42.8 0.6 select_bitcast_fusion.1
  43.5 0.1 copy.31
  43.6 0.1 copy.32
  43.8 0.1 broadcast_in_dim.8
  43.9 29.7 %all_to_all.30 = bf16[32,48,256]{2,1,0:T(8,128)(2,1)S(1)} all-to-all(bf16[32,48,256]{2,1,0:T(8,128)(2,1)S(1)} %bitcast.41), channel_id=1, replica_groups=mesh['zl'=2,'x'=4,'core'=2,'y'=8,'zb'=2,'za'=2] {'y','zb','za'}, dimensions={0} | all-to-all | bytes 1572864 | tf_op jit(solution)/shard_map/all_to_all | solution.py:48
  73.6 1.9 %collective-permute-start.1 = (bf16[32,48,256]{2,1,0:T(8,128)(2,1)S(1)}, bf16[32,48,256]{2,1,0:T(8,128)(2,1)S(1)}, u32[]{:S(2)}, u32[]{:S(2)}) collective-permute-start(bf16[32,48,256]{2,1,0:T(8,128)(2,1)S(1)} %all_to_all.30), channel_id=1, source_target_pairs={{0,32},{32,0},{1,33},{33,1},{2,34},{34,2},{3,35},{35,3},{4,36},{36... | collective-permute-start | bytes 2359304 | tf_op jit(solution)/shard_map/ppermute | solution.py:49
  75.6 0.2 multiply_reduce_fusion.1
  75.8 0.9 broadcast_in_dim_broadcast_in_dim_broadcast_in_dim.2
  76.7 8.1 %all-to-all-start.4 = ((f32[64,16,128]{2,1,0:T(8,128)}), f32[64,16,128]{2,1,0:T(8,128)S(1)}, u32[]{:S(2)}, u32[]{:S(2)}) async-start(f32[64,16,128]{2,1,0:T(8,128)} %broadcast_in_dim_broadcast_in_dim_broadcast_in_dim.2), calls=%async_computation.4 | async-start | bytes 1048576 | tf_op jit(solution)/shard_map/all_to_all | solution.py:14
  84.8 0.1 constant_dynamic-slice_fusion.1
  84.9 0.0 collective-permute-done.1
  84.9 0.1 constant_dynamic-slice_fusion
  85.0 0.1 maximum_bitcast_fusion
  85.0 0.1 slice_negate_fusion
  85.1 0.1 maximum_bitcast_fusion.1
  85.2 0.1 pad_maximum_fusion
  85.4 2.8 %convolution_convert_fusion = bf16[1536,768]{1,0:T(8,128)(2,1)} fusion(bf16[1536,512]{1,0:T(8,128)(2,1)S(1)} %bitcast.48, bf16[768,256]{1,0:T(8,128)(2,1)S(1)} %bitcast.57, bf16[768,256]{1,0:T(8,128)(2,1)S(1)} %bitcast.56), kind=kOutput, calls=%fused_computation | convolution fusion | flops 1210712064 | bytes 4718592 | tf_op jit(solution)/shard_map/dot_general | solution.py:67
  88.2 15.8 %all-to-all-done.4 = f32[64,16,128]{2,1,0:T(8,128)S(1)} async-done(((f32[64,16,128]{2,1,0:T(8,128)}), f32[64,16,128]{2,1,0:T(8,128)S(1)}, u32[]{:S(2)}, u32[]{:S(2)}) %all-to-all-start.4) | async-done | bytes 524320 | tf_op jit(solution)/shard_map/all_to_all | solution.py:14
  104.0 4.8 %all-to-all-start.2 = ((bf16[8,192,768]{2,1,0:T(8,128)(2,1)}), bf16[8,192,768]{2,1,0:T(8,128)(2,1)S(1)}, u32[]{:S(2)}, u32[]{:S(2)}) async-start(bf16[8,192,768]{2,1,0:T(8,128)(2,1)} %bitcast.43), calls=%async_computation.2 | async-start | bytes 4718592 | tf_op jit(solution)/shard_map/all_to_all | solution.py:70
  108.8 0.1 reduce_sum.60
  108.9 0.1 dynamic-slice_reduce_fusion
  109.0 1.6 multiply_reduce_fusion
  110.6 0.1 reshape.84
  110.7 0.9 copy.35
  111.6 25.6 %all-to-all-done.2 = bf16[8,192,768]{2,1,0:T(8,128)(2,1)S(1)} async-done(((bf16[8,192,768]{2,1,0:T(8,128)(2,1)}), bf16[8,192,768]{2,1,0:T(8,128)(2,1)S(1)}, u32[]{:S(2)}, u32[]{:S(2)}) %all-to-all-start.2) | async-done | bytes 2359328 | tf_op jit(solution)/shard_map/all_to_all | solution.py:70
  137.2 5.0 %all-to-all-start.5 = ((f32[16,48,96]{2,1,0:T(8,128)}), f32[16,48,96]{2,1,0:T(8,128)S(1)}, u32[]{:S(2)}, u32[]{:S(2)}) async-start(f32[16,48,96]{2,1,0:T(8,128)} %copy.35), calls=%async_computation.5 | async-start | bytes 786432 | tf_op jit(solution)/shard_map/all_to_all | solution.py:45
  142.2 0.4 reduce_sum.57
  142.6 0.9 copy.34
  143.6 6.0 %all-to-all-done.5 = f32[16,48,96]{2,1,0:T(8,128)S(1)} async-done(((f32[16,48,96]{2,1,0:T(8,128)}), f32[16,48,96]{2,1,0:T(8,128)S(1)}, u32[]{:S(2)}, u32[]{:S(2)}) %all-to-all-start.5) | async-done | bytes 294944 | tf_op jit(solution)/shard_map/all_to_all | solution.py:45
  149.5 4.3 %all-to-all-start.3 = ((bf16[16,48,192]{2,1,0:T(8,128)(2,1)}), bf16[16,48,192]{2,1,0:T(8,128)(2,1)S(1)}, u32[]{:S(2)}, u32[]{:S(2)}) async-start(bf16[16,48,192]{2,1,0:T(8,128)(2,1)} %bitcast.23), calls=%async_computation.3 | async-start | bytes 786432 | tf_op jit(solution)/shard_map/all_to_all | solution.py:72
  153.8 0.6 reduce_sum.62
  154.5 15.7 %all-to-all-done.3 = bf16[16,48,192]{2,1,0:T(8,128)(2,1)S(1)} async-done(((bf16[16,48,192]{2,1,0:T(8,128)(2,1)}), bf16[16,48,192]{2,1,0:T(8,128)(2,1)S(1)}, u32[]{:S(2)}, u32[]{:S(2)}) %all-to-all-start.3) | async-done | bytes 294944 | tf_op jit(solution)/shard_map/all_to_all | solution.py:72
  170.2 0.1 convert_reduce_fusion
  170.2 0.1 reshape.83
  170.3 0.6 copy.36
  (2 shorter events, 0.0 us)
Async XLA Ops:
  0.6 17.8 %copy-start = (bf16[8,48,1536]{2,1,0:T(8,128)(2,1)S(1)}, bf16[8,48,1536]{2,1,0:T(8,128)(2,1)}, u32[]{:S(2)}) copy-start(bf16[8,48,1536]{2,1,0:T(8,128)(2,1)} %param.2) | copy-start | bytes 3538948
  2.4 39.8 %all-to-all-start = ((bf16[32,48,256]{2,1,0:T(8,128)(2,1)}), bf16[32,48,256]{2,1,0:T(8,128)(2,1)S(1)}, u32[]{:S(2)}, u32[]{:S(2)}) async-start(bf16[32,48,256]{2,1,0:T(8,128)(2,1)} %broadcast_in_dim.6), calls=%async_computation | async-start | bytes 1572864 | tf_op jit(solution)/shard_map/all_to_all | solution.py:14
  18.4 24.4 %collective-permute-start = (bf16[8,48,1536]{2,1,0:T(8,128)(2,1)S(1)}, bf16[8,48,1536]{2,1,0:T(8,128)(2,1)S(1)}, u32[]{:S(2)}, u32[]{:S(2)}) collective-permute-start(bf16[8,48,1536]{2,1,0:T(8,128)(2,1)S(1)} %copy-done), channel_id=1, source_target_pairs={{0,32},{32,0},{1,33},{33,1},{2,34},{34,2},{3,35},{35,3},{4,36},{36... | collective-permute-start | bytes 3538952 | tf_op jit(solution)/shard_map/ppermute | solution.py:25
  73.6 11.3 %collective-permute-start.1 = (bf16[32,48,256]{2,1,0:T(8,128)(2,1)S(1)}, bf16[32,48,256]{2,1,0:T(8,128)(2,1)S(1)}, u32[]{:S(2)}, u32[]{:S(2)}) collective-permute-start(bf16[32,48,256]{2,1,0:T(8,128)(2,1)S(1)} %all_to_all.30), channel_id=1, source_target_pairs={{0,32},{32,0},{1,33},{33,1},{2,34},{34,2},{3,35},{35,3},{4,36},{36... | collective-permute-start | bytes 2359304 | tf_op jit(solution)/shard_map/ppermute | solution.py:49
  76.7 27.3 %all-to-all-start.4 = ((f32[64,16,128]{2,1,0:T(8,128)}), f32[64,16,128]{2,1,0:T(8,128)S(1)}, u32[]{:S(2)}, u32[]{:S(2)}) async-start(f32[64,16,128]{2,1,0:T(8,128)} %broadcast_in_dim_broadcast_in_dim_broadcast_in_dim.2), calls=%async_computation.4 | async-start | bytes 1048576 | tf_op jit(solution)/shard_map/all_to_all | solution.py:14
  104.0 33.2 %all-to-all-start.2 = ((bf16[8,192,768]{2,1,0:T(8,128)(2,1)}), bf16[8,192,768]{2,1,0:T(8,128)(2,1)S(1)}, u32[]{:S(2)}, u32[]{:S(2)}) async-start(bf16[8,192,768]{2,1,0:T(8,128)(2,1)} %bitcast.43), calls=%async_computation.2 | async-start | bytes 4718592 | tf_op jit(solution)/shard_map/all_to_all | solution.py:70
  137.2 12.3 %all-to-all-start.5 = ((f32[16,48,96]{2,1,0:T(8,128)}), f32[16,48,96]{2,1,0:T(8,128)S(1)}, u32[]{:S(2)}, u32[]{:S(2)}) async-start(f32[16,48,96]{2,1,0:T(8,128)} %copy.35), calls=%async_computation.5 | async-start | bytes 786432 | tf_op jit(solution)/shard_map/all_to_all | solution.py:45
  149.5 20.6 %all-to-all-start.3 = ((bf16[16,48,192]{2,1,0:T(8,128)(2,1)}), bf16[16,48,192]{2,1,0:T(8,128)(2,1)S(1)}, u32[]{:S(2)}, u32[]{:S(2)}) async-start(bf16[16,48,192]{2,1,0:T(8,128)(2,1)} %bitcast.23), calls=%async_computation.3 | async-start | bytes 786432 | tf_op jit(solution)/shard_map/all_to_all | solution.py:72

commit v2 on v1

--- a/solution.py
+++ b/solution.py
@@ -8,14 +8,15 @@
 FAR = ("y", "zb", "za")
 SUMS = ("y", "za")
 SWAP = [(0, 1), (1, 0)]
+f32, bf16 = jnp.float32, jnp.bfloat16
 
 
-def to_all(block, axes, count):
-    return lax.all_to_all(jnp.broadcast_to(block[None], (count,) + block.shape), axes, 0, 0, tiled=True)
+def words(value):
+    high = lax.reduce_precision(value, 8, 7)
+    return high.astype(bf16), (value - high).astype(bf16)
 
 
 def on_device(vectors, coeffs):
-    f32, bf16 = jnp.float32, jnp.bfloat16
     core = lax.axis_index("core")
     zb = lax.axis_index("zb")
     count, rows, nao = vectors.shape
@@ -25,7 +26,8 @@
     other_vectors = lax.ppermute(vectors, "core", SWAP)
     own = lax.dynamic_slice_in_dim(coeffs, core * half, half, 2)
     own = jnp.concatenate([own[0], own[1]], axis=1)
-    full = to_all(own, FAR, 32).reshape(nao, wide)
+    full = lax.all_to_all(jnp.broadcast_to(own[None], (32, rows, wide)), FAR, 0, 0, tiled=True)
+    full = full.reshape(nao, wide)
 
     def transform(block):
         return jnp.dot(
@@ -37,19 +39,31 @@
     slab = jnp.concatenate([jnp.where(first, mine, other), jnp.where(first, other, mine)])
 
     terms = jnp.sum(slab.astype(f32) * own.astype(f32)[None], axis=(1, 2))
-    terms = jnp.broadcast_to(terms[:, None], (16, 128))
-    weights = jnp.sum(to_all(terms, ("core",) + FAR, 64), axis=0)[:, 0]
-    weights = lax.dynamic_slice_in_dim(weights, core * count, count, 0)
-    coulomb_part = jnp.sum(vectors.astype(f32) * weights[:, None, None], axis=0)
-    coulomb_part = coulomb_part.reshape(rows, 16, nao // 16).transpose(1, 0, 2)
-    coulomb = jnp.sum(lax.all_to_all(coulomb_part, NEAR + ("core",), 0, 0, tiled=True), axis=0)
-
-    pieces = jnp.broadcast_to(slab.reshape(8, 1, 2, rows, wide), (8, 2, 2, rows, wide)).reshape(32, rows, wide)
+    high, low = words(terms)
+    terms = jnp.concatenate([high, low, jnp.zeros((wide - 32,), bf16)])
+    terms = jnp.concatenate([terms[None], jnp.zeros((7, wide), bf16)])
+    terms = jnp.broadcast_to(terms[None], (16, 8, wide))
+    pieces = jnp.concatenate([slab, terms], axis=1).reshape(8, 1, 2, rows + 8, wide)
+    pieces = jnp.broadcast_to(pieces, (8, 2, 2, rows + 8, wide)).reshape(32, rows + 8, wide)
     got = lax.all_to_all(pieces, FAR, 0, 0, tiled=True)
     got_other = lax.ppermute(got, "core", SWAP)
 
+    weights = jnp.sum((got[:, rows] + 0.0).astype(f32) + got_other[:, rows].astype(f32), axis=0)
+    weights = weights[:16] + weights[16:32]
+    mine_weights = lax.dynamic_slice_in_dim(weights, core * count, count, 0)
+    other_weights = lax.dynamic_slice_in_dim(weights, (1 - core) * count, count, 0)
+    coulomb = jnp.sum(
+        vectors.astype(f32) * mine_weights[:, None, None]
+        + other_vectors.astype(f32) * other_weights[:, None, None],
+        axis=0,
+    )
+    coulomb = lax.dynamic_index_in_dim(coulomb.reshape(rows, 8, 2, 2 * rows), core, 2, keepdims=False)
+    high, low = words(coulomb)
+    coulomb = jnp.stack([high, low]).transpose(2, 0, 1, 3).reshape(8, 12, 16 * rows)
+    coulomb = jnp.pad(coulomb, ((0, 0), (0, 4), (0, 0)))
+
     def parts(block):
-        block = block.reshape(8, 2, 2 * rows, wide)
+        block = block[:, :rows].reshape(8, 2, 2 * rows, wide)
         row_part = lax.dynamic_index_in_dim(block, zb, 1, keepdims=False)
         column_part = lax.dynamic_index_in_dim(block, core, 1, keepdims=False)
         return row_part.reshape(16 * rows, wide), column_part
@@ -67,8 +81,11 @@
     exchange = lax.dot_general(
         column_side, row_side, (((1,), (1,)), ((), ())), preferred_element_type=f32
     ).astype(bf16).reshape(8, 4 * rows, 16 * rows)
-    exchange = jnp.sum(lax.all_to_all(exchange, NEAR, 0, 0, tiled=True).astype(f32), axis=0)
-    exchange = exchange.astype(bf16).T.reshape(16, rows, 4 * rows)
+    sums = lax.all_to_all(jnp.concatenate([exchange, coulomb], axis=1), NEAR, 0, 0, tiled=True)
+    sums = jnp.sum(sums.astype(f32), axis=0)
+    coulomb = sums[4 * rows : 4 * rows + 12].reshape(2, rows, 2 * rows)
+    coulomb = coulomb[0] + coulomb[1]
+    exchange = sums[: 4 * rows].astype(bf16).T.reshape(16, rows, 4 * rows)
     exchange = jnp.sum(lax.all_to_all(exchange, SUMS, 0, 0, tiled=True).astype(f32), axis=0)
     exchange = exchange.reshape(rows, 2, 2 * rows).transpose(1, 0, 2)
     return exchange, coulomb

time: 172 us -> 153 us (0.89)
  waiting for transfers between devices: 84.9 us -> 38 us
  blocking collectives: 29.7 us -> 67.5 us
  starting transfers between devices: 42 us -> 27 us
  local copies, waits for them, and re-layouts: 5.92 us -> 8.71 us
    all_to_all x4 -> x1, waiting for transfers between devices: 69.2 us -> 21.9 us  [on_device(): lax.all_to_all(jnp.broadcast_to(own[None], (32, rows, wide)), FAR, 0, 0,...]
    all_to_all x0 -> x1, blocking collectives: none -> 35.1 us  [on_device(): lax.all_to_all(jnp.concatenate([exchange, coulomb], axis=1), NEAR, 0, 0,...]
    all_to_all x4 -> x1, starting transfers between devices: 33.9 us -> 16.1 us  [on_device(): lax.all_to_all(jnp.broadcast_to(own[None], (32, rows, wide)), FAR, 0, 0,...]
    all_to_all x1, starting transfers between devices: 4.3 us -> 7.13 us  [on_device(): lax.all_to_all(exchange, SUMS, 0, 0, tiled=True).astype(f32)]
    dot_general x2, matrix products: 1.23 us -> 3.93 us  [transform(): jnp.dot(block.reshape(count * rows, nao), full, preferred_element_type=f32)]
    all_to_all x1, blocking collectives: 29.7 us -> 32.4 us  [on_device(): got = lax.all_to_all(pieces, FAR, 0, 0, tiled=True)]
    ppermute x1, waiting for transfers between devices: 0.01 us -> 2.5 us  [on_device(): got_other = lax.ppermute(got, 'core', SWAP)]
    all_to_all x1, waiting for transfers between devices: 15.7 us -> 13.7 us  [on_device(): lax.all_to_all(exchange, SUMS, 0, 0, tiled=True).astype(f32)]
  transfers between devices with their start and end apart: 7 -> 4, of which waited for: 5 -> 3; matrix products, arithmetic and copies ran while one was open for 6% -> 2% of each run, Pallas kernels for 0% -> 0%
where the time goes in v2:
time: 153 us; the launch traced here: 151 us
  blocking collectives  67.5 us (44%)
  waiting for transfers between devices  38 us (25%)
  starting transfers between devices  27 us (18%)
  local copies, waits for them, and re-layouts  8.71 us (6%)
  matrix products  5.35 us (3%)
  other arithmetic  3.68 us (2%)
    all_to_all x1, blocking collectives, on_device(): lax.all_to_all(jnp.concatenate([exchange, coulomb], axis=1), NEAR, 0, 0,...  35.1 us
    all_to_all x1, blocking collectives, on_device(): got = lax.all_to_all(pieces, FAR, 0, 0, tiled=True)  32.4 us
    all_to_all x1, waiting for transfers between devices, on_device(): lax.all_to_all(jnp.broadcast_to(own[None], (32, rows, wide)), FAR, 0, 0,...  21.9 us
    all_to_all x1, starting transfers between devices, on_device(): lax.all_to_all(jnp.broadcast_to(own[None], (32, rows, wide)), FAR, 0, 0,...  16.1 us
    all_to_all x1, waiting for transfers between devices, on_device(): lax.all_to_all(exchange, SUMS, 0, 0, tiled=True).astype(f32)  13.7 us
    all_to_all x1, starting transfers between devices, on_device(): lax.all_to_all(exchange, SUMS, 0, 0, tiled=True).astype(f32)  7.13 us
    dot_general x2, matrix products, transform(): jnp.dot(block.reshape(count * rows, nao), full, preferred_element_type=f32)  3.93 us
  transfers between devices with their start and end apart: 4, of which 3 were waited for; matrix products, arithmetic and copies ran while one was open for 2% of the time, Pallas kernels for 0%

profile of v2, /device:TPU:6, one launch (start us, length us, event | category | flops | bytes accessed | tf_op | source)
XLA Modules:
  0.0 151.3 jit_solution(15247638586097036602)
XLA Ops:
  0.6 0.0 copy-start
  0.6 0.8 dynamic-slice_bitcast_fusion.3
  1.5 0.9 broadcast_in_dim.12
  2.4 16.1 %all-to-all-start = ((bf16[32,48,256]{2,1,0:T(8,128)(2,1)}), bf16[32,48,256]{2,1,0:T(8,128)(2,1)}, u32[]{:S(2)}, u32[]{:S(2)}) async-start(bf16[32,48,256]{2,1,0:T(8,128)(2,1)} %broadcast_in_dim.12), calls=%async_computation | async-start | bytes 1572864 | tf_op jit(solution)/shard_map/all_to_all | solution.py:29
  18.5 0.0 copy-done
  18.5 1.9 %collective-permute-start = (bf16[8,48,1536]{2,1,0:T(8,128)(2,1)S(1)}, bf16[8,48,1536]{2,1,0:T(8,128)(2,1)S(1)}, u32[]{:S(2)}, u32[]{:S(2)}) collective-permute-start(bf16[8,48,1536]{2,1,0:T(8,128)(2,1)S(1)} %copy-done), channel_id=1, source_target_pairs={{0,32},{32,0},{1,33},{33,1},{2,34},{34,2},{3,35},{35,3},{4,36},{36... | collective-permute-start | bytes 3538952 | tf_op jit(solution)/shard_map/ppermute | solution.py:26
  20.4 21.9 %all-to-all-done = bf16[32,48,256]{2,1,0:T(8,128)(2,1)} async-done(((bf16[32,48,256]{2,1,0:T(8,128)(2,1)}), bf16[32,48,256]{2,1,0:T(8,128)(2,1)}, u32[]{:S(2)}, u32[]{:S(2)}) %all-to-all-start) | async-done | bytes 786464 | tf_op jit(solution)/shard_map/all_to_all | solution.py:29
  42.3 1.7 %convolution_convert_fusion.2 = bf16[256,384]{1,0:T(8,128)(2,1)S(1)} fusion(bf16[1536,256]{1,0:T(8,128)(2,1)} %bitcast.2, bf16[384,1536]{1,0:T(8,128)(2,1)S(1)} %bitcast.55), kind=kOutput, calls=%fused_computation.8 | convolution fusion | flops 302088192 | bytes 2162688 | tf_op jit(solution)/shard_map/dot_general | solution.py:33
  44.1 0.0 collective-permute-done
  44.1 0.0 copy-start.1
  44.1 2.2 %select_bitcast_fusion.1 = (bf16[384,256]{0,1:T(8,128)(2,1)S(1)}, bf16[384,256]{0,1:T(8,128)(2,1)S(1)}) fusion(bf16[256,384]{1,0:T(8,128)(2,1)S(1)} %convolution_convert_fusion.2, pred[]{:T(512)S(6)} %eq.3, bf16[1536,256]{1,0:T(8,128)(2,1)} %bitcast.2, bf16[384,1536]{1,0:T(8,128)(2,1)S(1)} %bitcast.56), kind=kOutput, calls=%fused_computation.28 | convolution fusion | flops 302284800 | bytes 2555905 | tf_op jit(solution)/shard_map/dot_general | solution.py:33
  46.3 0.0 copy-done.1
  46.3 0.1 copy.16
  46.4 0.1 copy.17
  46.6 0.2 multiply_reduce_fusion
  46.8 0.1 pad_maximum_fusion.3
  47.0 0.1 broadcast_in_dim.34
  47.0 32.4 %all_to_all.20 = bf16[32,56,256]{2,1,0:T(8,128)(2,1)S(1)} all-to-all(bf16[32,56,256]{2,1,0:T(8,128)(2,1)S(1)} %bitcast.45), channel_id=1, replica_groups=mesh['zl'=2,'x'=4,'core'=2,'y'=8,'zb'=2,'za'=2] {'y','zb','za'}, dimensions={0} | all-to-all | bytes 1835008 | tf_op jit(solution)/shard_map/all_to_all | solution.py:48
  79.4 1.9 %collective-permute-start.1 = (bf16[32,56,256]{2,1,0:T(8,128)(2,1)S(1)}, bf16[32,56,256]{2,1,0:T(8,128)(2,1)}, u32[]{:S(2)}, u32[]{:S(2)}) collective-permute-start(bf16[32,56,256]{2,1,0:T(8,128)(2,1)S(1)} %all_to_all.20), channel_id=1, source_target_pairs={{0,32},{32,0},{1,33},{33,1},{2,34},{34,2},{3,35},{35,3},{4,36},{36... | collective-permute-start | bytes 2752520 | tf_op jit(solution)/shard_map/ppermute | solution.py:49
  81.4 0.1 slice.66
  81.4 2.5 %collective-permute-done.1 = bf16[32,56,256]{2,1,0:T(8,128)(2,1)} collective-permute-done((bf16[32,56,256]{2,1,0:T(8,128)(2,1)S(1)}, bf16[32,56,256]{2,1,0:T(8,128)(2,1)}, u32[]{:S(2)}, u32[]{:S(2)}) %collective-permute-start.1) | collective-permute-done | bytes 917536 | tf_op jit(solution)/shard_map/ppermute | solution.py:49
  83.9 1.2 slice.67
  85.1 1.0 constant_dynamic-slice_fusion.1
  86.2 0.1 maximum_bitcast_fusion
  86.3 0.7 slice_negate_fusion.1
  87.0 1.0 fusion.8
  88.0 0.1 slice_add_fusion.1
  88.0 0.1 fusion.12
  88.1 0.5 add_reduce_fusion
  88.7 0.5 reshape.123
  89.2 0.2 constant_dynamic-slice_fusion
  89.5 0.2 reshape.124
  89.7 0.0 copy-done.3
  89.7 0.1 maximum_bitcast_fusion.1
  89.8 0.2 pad_maximum_fusion
  90.0 0.8 copy-done.4
  90.8 0.1 copy-done.5
  90.9 1.4 convolution_convert_fusion
  92.3 0.2 fusion.1
  92.5 35.1 %all_to_all.21 = bf16[8,208,768]{2,1,0:T(8,128)(2,1)S(1)} all-to-all(bf16[8,208,768]{2,1,0:T(8,128)(2,1)S(1)} %fusion.1), channel_id=1, replica_groups=mesh['zl'=2,'x'=4,'core'=2,'y'=8,'zb'=2,'za'=2] {'zl','x'}, dimensions={0} | all-to-all | bytes 5111808 | tf_op jit(solution)/shard_map/all_to_all | solution.py:84
  127.7 0.3 convert_reduce_fusion
  128.0 0.9 copy.20
  129.0 7.1 %all-to-all-start.3 = ((bf16[16,48,192]{2,1,0:T(8,128)(2,1)}), bf16[16,48,192]{2,1,0:T(8,128)(2,1)S(1)}, u32[]{:S(2)}, u32[]{:S(2)}) async-start(bf16[16,48,192]{2,1,0:T(8,128)(2,1)} %bitcast.25), calls=%async_computation.3 | async-start | bytes 786432 | tf_op jit(solution)/shard_map/all_to_all | solution.py:89
  136.1 0.7 add.49
  136.8 13.7 %all-to-all-done.3 = bf16[16,48,192]{2,1,0:T(8,128)(2,1)S(1)} async-done(((bf16[16,48,192]{2,1,0:T(8,128)(2,1)}), bf16[16,48,192]{2,1,0:T(8,128)(2,1)S(1)}, u32[]{:S(2)}, u32[]{:S(2)}) %all-to-all-start.3) | async-done | bytes 294944 | tf_op jit(solution)/shard_map/all_to_all | solution.py:89
  150.5 0.1 convert_reduce_fusion.1
  150.5 0.1 reshape.126
  150.6 0.6 copy.21
  (18 shorter events, 0.3 us)
Async XLA Ops:
  0.6 17.9 %copy-start = (bf16[8,48,1536]{2,1,0:T(8,128)(2,1)S(1)}, bf16[8,48,1536]{2,1,0:T(8,128)(2,1)}, u32[]{:S(2)}) copy-start(bf16[8,48,1536]{2,1,0:T(8,128)(2,1)} %param.2) | copy-start | bytes 3538948
  2.4 39.9 %all-to-all-start = ((bf16[32,48,256]{2,1,0:T(8,128)(2,1)}), bf16[32,48,256]{2,1,0:T(8,128)(2,1)}, u32[]{:S(2)}, u32[]{:S(2)}) async-start(bf16[32,48,256]{2,1,0:T(8,128)(2,1)} %broadcast_in_dim.12), calls=%async_computation | async-start | bytes 1572864 | tf_op jit(solution)/shard_map/all_to_all | solution.py:29
  18.5 25.6 %collective-permute-start = (bf16[8,48,1536]{2,1,0:T(8,128)(2,1)S(1)}, bf16[8,48,1536]{2,1,0:T(8,128)(2,1)S(1)}, u32[]{:S(2)}, u32[]{:S(2)}) collective-permute-start(bf16[8,48,1536]{2,1,0:T(8,128)(2,1)S(1)} %copy-done), channel_id=1, source_target_pairs={{0,32},{32,0},{1,33},{33,1},{2,34},{34,2},{3,35},{35,3},{4,36},{36... | collective-permute-start | bytes 3538952 | tf_op jit(solution)/shard_map/ppermute | solution.py:26
  44.1 2.2 %copy-start.1 = (bf16[8,48,1536]{2,1,0:T(8,128)(2,1)}, bf16[8,48,1536]{2,1,0:T(8,128)(2,1)S(1)}, u32[]{:S(2)}) copy-start(bf16[8,48,1536]{2,1,0:T(8,128)(2,1)S(1)} %collective-permute-done) | copy-start | bytes 3538948
  79.4 4.5 %collective-permute-start.1 = (bf16[32,56,256]{2,1,0:T(8,128)(2,1)S(1)}, bf16[32,56,256]{2,1,0:T(8,128)(2,1)}, u32[]{:S(2)}, u32[]{:S(2)}) collective-permute-start(bf16[32,56,256]{2,1,0:T(8,128)(2,1)S(1)} %all_to_all.20), channel_id=1, source_target_pairs={{0,32},{32,0},{1,33},{33,1},{2,34},{34,2},{3,35},{35,3},{4,36},{36... | collective-permute-start | bytes 2752520 | tf_op jit(solution)/shard_map/ppermute | solution.py:49
  86.1 2.0 %copy-start.2 = (bf16[8,48,1536]{2,1,0:T(8,128)(2,1)S(1)}, bf16[8,48,1536]{2,1,0:T(8,128)(2,1)}, u32[]{:S(2)}) copy-start(bf16[8,48,1536]{2,1,0:T(8,128)(2,1)} %copy-done.1) | copy-start | bytes 3538948
  88.7 1.0 copy-start.3
  89.8 1.0 copy-start.4
  89.8 1.1 copy-start.5
  129.0 21.5 %all-to-all-start.3 = ((bf16[16,48,192]{2,1,0:T(8,128)(2,1)}), bf16[16,48,192]{2,1,0:T(8,128)(2,1)S(1)}, u32[]{:S(2)}, u32[]{:S(2)}) async-start(bf16[16,48,192]{2,1,0:T(8,128)(2,1)} %bitcast.25), calls=%async_computation.3 | async-start | bytes 786432 | tf_op jit(solution)/shard_map/all_to_all | solution.py:89

commit v3 on v1

v3 whole, which is shorter than its diff:
```python
import jax
import jax.numpy as jnp
from jax import lax
from jax.experimental import pallas as pl
from jax.experimental.pallas import tpu as pltpu
from jax.sharding import Mesh
from jax.sharding import PartitionSpec as P

NEAR = ("zl", "x")
FAR = ("y", "zb", "za")
SUMS = ("y", "za")
SWAP = [(0, 1), (1, 0)]
f32, bf16 = jnp.float32, jnp.bfloat16
SMEM = pl.BlockSpec(memory_space=pltpu.SMEM)
VMEM = pl.BlockSpec(memory_space=pltpu.VMEM)
PARAMS = pltpu.CompilerParams(vmem_limit_bytes=40 * 2**20)


def words(value):
    high = value.astype(bf16)
    return high, (value - high.astype(f32)).astype(bf16)


def transform_kernel(place, full, mine, other, own, out):
    core = place[0]
    count, rows, nao = mine.shape
    wide = full.shape[1]
    weight = own[...].astype(f32)
    lane = lax.broadcasted_iota(jnp.int32, (1, wide), 1)
    terms = jnp.zeros((1, wide), f32)
    for source, owner in ((mine, core), (other, 1 - core)):
        slab = jnp.dot(
            source[...].reshape(count * rows, nao), full[...], preferred_element_type=f32
        ).astype(bf16)
        for p in range(count):
            block = slab[p * rows : (p + 1) * rows]
            for zb in range(2):
                out[owner * (count // 2) + p // 2, zb, p % 2, 0:rows] = block
            term = jnp.sum(block.astype(f32) * weight, axis=0, keepdims=True)
            term = jnp.sum(term, axis=1, keepdims=True)
            terms += jnp.where(lane == owner * count + p, term, 0.0)
    high, low = words(terms)
    lines = lax.broadcasted_iota(jnp.int32, (16, wide), 0)
    rider = jnp.where(lines == 0, high.astype(f32), jnp.where(lines == 1, low.astype(f32), 0.0))
    rider = rider.astype(bf16)
    for y in range(8):
        for zb in range(2):
            for za in range(2):
                out[y, zb, za, rows : rows + 16] = rider


def exchange_kernel(place, got, got_other, mine, other, out, column_side, row_side):
    core, zb = place[0], place[1]
    count, rows, nao = mine.shape
    wide = got.shape[4]
    half = wide // 2
    for y in range(8):
        for za in range(2):
            for k, source in enumerate((got, got_other)):
                at = pl.ds((2 * y + za) * rows, rows)
                row_side[at, k * wide : (k + 1) * wide] = source[y, zb, za, 0:rows]
                block = source[y, core, za, 0:rows]
                at = pl.ds((4 * y + za) * rows, rows)
                column_side[at, k * wide : (k + 1) * wide] = block
                at = pl.ds((4 * y + 2 + za) * rows, rows)
                column_side[at, k * wide : k * wide + half] = -block[:, half:]
                column_side[at, k * wide + half : (k + 1) * wide] = block[:, :half]

    riders = jnp.zeros((16, wide), f32)
    for y in range(8):
        for b in range(2):
            for za in range(2):
                for source in (got, got_other):
                    riders += source[y, b, za, rows : rows + 16].astype(f32)
    weights = riders[0:1] + riders[1:2]
    lane = lax.broadcasted_iota(jnp.int32, (1, wide), 1)
    for part in range(3):
        at = pl.ds(part * 16, 16)
        total = jnp.zeros((16, nao), f32)
        for source, owner in ((mine, core), (other, 1 - core)):
            for p in range(count):
                weight = jnp.sum(jnp.where(lane == owner * count + p, weights, 0.0), axis=1, keepdims=True)
                total += weight * source[p, at].astype(f32)
        for s in range(8):
            start = s * 4 * rows
            piece = jnp.where(
                core == 0, total[:, start : start + 2 * rows], total[:, start + 2 * rows : start + 4 * rows]
            )
            high, low = words(piece)
            gap = jnp.zeros((16, half - 2 * rows), bf16)
            out[s, 4 * rows : 4 * rows + 16, part * 256 : (part + 1) * 256] = jnp.concatenate(
                [high, gap, low, gap], axis=1
            )

    for n in range(3):
        block = lax.dot_general(
            column_side[...],
            row_side[n * 256 : (n + 1) * 256],
            (((1,), (1,)), ((), ())),
            preferred_element_type=f32,
        ).astype(bf16)
        for s in range(8):
            out[s, 0 : 4 * rows, n * 256 : (n + 1) * 256] = block[s * 4 * rows : (s + 1) * 4 * rows]


def on_device(vectors, coeffs):
    core = lax.axis_index("core")
    zb = lax.axis_index("zb")
    place = jnp.stack([core, zb]).astype(jnp.int32)
    count, rows, nao = vectors.shape
    half = coeffs.shape[2] // 2
    wide = 2 * half
    tall = rows + 16

    other_vectors = lax.ppermute(vectors, "core", SWAP)
    own = lax.dynamic_slice_in_dim(coeffs, core * half, half, 2)
    own = jnp.concatenate([own[0], own[1]], axis=1)
    full = lax.all_to_all(jnp.broadcast_to(own[None], (32, rows, wide)), FAR, 0, 0, tiled=True)

    pieces = pl.pallas_call(
        transform_kernel,
        out_shape=jax.ShapeDtypeStruct((8, 2, 2, tall, wide), bf16),
        in_specs=[SMEM] + [VMEM] * 4,
        out_specs=VMEM,
        compiler_params=PARAMS,
        name="half_transform",
    )(place, full.reshape(nao, wide), vectors, other_vectors, own)
    got = lax.all_to_all(pieces.reshape(32, tall, wide), FAR, 0, 0, tiled=True)
    got_other = lax.ppermute(got, "core", SWAP)

    shape = (8, 2, 2, tall, wide)
    sums = pl.pallas_call(
        exchange_kernel,
        out_shape=jax.ShapeDtypeStruct((8, 4 * rows + 16, 16 * rows), bf16),
        in_specs=[SMEM] + [VMEM] * 4,
        out_specs=VMEM,
        scratch_shapes=[
            pltpu.VMEM((32 * rows, 2 * wide), bf16),
            pltpu.VMEM((16 * rows, 2 * wide), bf16),
        ],
        compiler_params=PARAMS,
        name="exchange_quarter",
    )(place, got.reshape(shape), got_other.reshape(shape), vectors, other_vectors)
    sums = lax.all_to_all(sums, NEAR, 0, 0, tiled=True)
    sums = jnp.sum(sums.astype(f32), axis=0)
    coulomb = sums[4 * rows :].reshape(16, 3, 2, half)[..., : 2 * rows]
    coulomb = (coulomb[:, :, 0] + coulomb[:, :, 1]).transpose(1, 0, 2).reshape(rows, 2 * rows)
    exchange = sums[: 4 * rows].astype(bf16).T.reshape(16, rows, 4 * rows)
    exchange = jnp.sum(lax.all_to_all(exchange, SUMS, 0, 0, tiled=True).astype(f32), axis=0)
    exchange = exchange.reshape(rows, 2, 2 * rows).transpose(1, 0, 2)
    return exchange, coulomb


def solution(mesh):
    fine = Mesh(mesh.devices.reshape(2, 4, 2, 8, 2, 2), ("zl", "x", "core", "y", "zb", "za"))
    chol = ("zl", "x", "core")
    return jax.shard_map(
        on_device,
        mesh=fine,
        in_specs=(P(chol, FAR, None), P(None, FAR, None)),
        out_specs=(P(None, FAR, chol), P(FAR, chol)),
        check_vma=False,
    )
```

time: 172 us -> 145 us (0.84)
  waiting for transfers between devices: 84.9 us -> 38.1 us
  blocking collectives: 29.7 us -> 70.2 us
  starting transfers between devices: 42 us -> 26.7 us
  matrix products: 4.08 us -> 0 us
  Pallas kernels: 0 us -> 3.78 us
  other arithmetic: 3.46 us -> 0.52 us
  local copies, waits for them, and re-layouts: 5.92 us -> 4.1 us
    all_to_all x4 -> x1, waiting for transfers between devices: 69.2 us -> 18.9 us  [on_device(): lax.all_to_all(jnp.broadcast_to(own[None], (32, rows, wide)), FAR, 0, 0,...]
    all_to_all x1 -> x2, blocking collectives: 29.7 us -> 70.2 us  [the longest x1 35.2 us: on_device(): sums = lax.all_to_all(sums, NEAR, 0, 0, tiled=True)]
    all_to_all x4 -> x1, starting transfers between devices: 33.9 us -> 16 us  [on_device(): lax.all_to_all(jnp.broadcast_to(own[None], (32, rows, wide)), FAR, 0, 0,...]
    dot_general x3 -> x0, matrix products: 4.08 us -> none  [the longest x1 2.84 us: on_device(): lax.dot_general(column_side, row_side, (((1,), (1,)), ((), ())), preferre...]
    pallas_call x0 -> x2, Pallas kernels: none -> 3.78 us  [the longest x1 2.31 us: on_device(): pl.pallas_call(exchange_kernel, out_shape=jax.ShapeDtypeStruct((8, 4 * ro...]
    ppermute x1, waiting for transfers between devices: 0.01 us -> 2.94 us  [on_device(): other_vectors = lax.ppermute(vectors, 'core', SWAP)]
    ppermute x1, waiting for transfers between devices: 0.01 us -> 2.63 us  [on_device(): got_other = lax.ppermute(got, 'core', SWAP)]
    reduce_sum x5 -> x1, other arithmetic: 2.95 us -> 0.33 us  [on_device(): sums = jnp.sum(sums.astype(f32), axis=0)]
  transfers between devices with their start and end apart: 7 -> 4, of which waited for: 5 -> 4; matrix products, arithmetic and copies ran while one was open for 6% -> 1% of each run, Pallas kernels for 0% -> 0%
where the time goes in v3:
time: 145 us; the launch traced here: 144 us
  blocking collectives  70.2 us (48%)
  waiting for transfers between devices  38.1 us (26%)
  starting transfers between devices  26.7 us (18%)
  local copies, waits for them, and re-layouts  4.1 us (3%)
  Pallas kernels  3.78 us (3%)
    all_to_all x1, blocking collectives, on_device(): sums = lax.all_to_all(sums, NEAR, 0, 0, tiled=True)  35.2 us
    all_to_all x1, blocking collectives, on_device(): got = lax.all_to_all(pieces.reshape(32, tall, wide), FAR, 0, 0, tiled=True)  35 us
    all_to_all x1, waiting for transfers between devices, on_device(): lax.all_to_all(jnp.broadcast_to(own[None], (32, rows, wide)), FAR, 0, 0,...  18.9 us
    all_to_all x1, starting transfers between devices, on_device(): lax.all_to_all(jnp.broadcast_to(own[None], (32, rows, wide)), FAR, 0, 0,...  16 us
    all_to_all x1, waiting for transfers between devices, on_device(): lax.all_to_all(exchange, SUMS, 0, 0, tiled=True).astype(f32)  13.7 us
    all_to_all x1, starting transfers between devices, on_device(): lax.all_to_all(exchange, SUMS, 0, 0, tiled=True).astype(f32)  6.89 us
    ppermute x1, waiting for transfers between devices, on_device(): other_vectors = lax.ppermute(vectors, 'core', SWAP)  2.94 us
  transfers between devices with their start and end apart: 4, of which 4 were waited for; matrix products, arithmetic and copies ran while one was open for 1% of the time, Pallas kernels for 0%

profile of v3, /device:TPU:6, one launch (start us, length us, event | category | flops | bytes accessed | tf_op | source)
XLA Modules:
  0.0 144.1 jit_solution(4576018058793383386)
XLA Ops:
  0.6 0.0 copy-start
  0.6 0.8 dynamic-slice_bitcast_fusion.1
  1.5 0.9 broadcast_in_dim.2
  2.4 16.0 %all-to-all-start = ((bf16[32,48,256]{2,1,0:T(8,128)(2,1)}), bf16[32,48,256]{2,1,0:T(8,128)(2,1)S(1)}, u32[]{:S(2)}, u32[]{:S(2)}) async-start(bf16[32,48,256]{2,1,0:T(8,128)(2,1)} %broadcast_in_dim.2), calls=%async_computation | async-start | bytes 1572864 | tf_op jit(solution)/shard_map/all_to_all | solution.py:118
  18.4 1.9 %collective-permute-start = (bf16[8,48,1536]{2,1,0:T(8,128)(2,1)}, bf16[8,48,1536]{2,1,0:T(8,128)(2,1)S(1)}, u32[]{:S(2)}, u32[]{:S(2)}) collective-permute-start(bf16[8,48,1536]{2,1,0:T(8,128)(2,1)} %mine.3), channel_id=1, source_target_pairs={{0,32},{32,0},{1,33},{33,1},{2,34},{34,2},{3,35},{35,3},{4,36},{36... | collective-permute-start | bytes 3538952 | tf_op jit(solution)/shard_map/ppermute | solution.py:115
  20.3 0.1 pad_add_fusion.place
  20.4 2.9 %collective-permute-done.other = bf16[8,48,1536]{2,1,0:T(8,128)(2,1)S(1)} collective-permute-done((bf16[8,48,1536]{2,1,0:T(8,128)(2,1)}, bf16[8,48,1536]{2,1,0:T(8,128)(2,1)S(1)}, u32[]{:S(2)}, u32[]{:S(2)}) %collective-permute-start) | collective-permute-done | bytes 1179680 | tf_op jit(solution)/shard_map/ppermute | solution.py:115
  23.3 18.9 %all-to-all-done = bf16[32,48,256]{2,1,0:T(8,128)(2,1)S(1)} async-done(((bf16[32,48,256]{2,1,0:T(8,128)(2,1)}), bf16[32,48,256]{2,1,0:T(8,128)(2,1)S(1)}, u32[]{:S(2)}, u32[]{:S(2)}) %all-to-all-start) | async-done | bytes 786464 | tf_op jit(solution)/shard_map/all_to_all | solution.py:118
  42.2 0.0 copy-done
  42.2 1.5 %half_transform.1 = bf16[8,2,2,64,256]{4,3,2,1,0:T(8,128)(2,1)S(1)} custom-call(s32[2]{0:T(128)S(1)} %pad_add_fusion.place, bf16[1536,256]{1,0:T(8,128)(2,1)S(1)} %bitcast.21, bf16[8,48,1536]{2,1,0:T(8,128)(2,1)S(1)} %copy-done, bf16[8,48,1536]{2,1,0:T(8,128)(2,1)S(1)} %collective-permute-done.other, bf16[48,256]{1,0:T(8,128)(2,1)S(1)} %pad_maximum_fusion.own), custom_call_target="tpu_custom_call" | custom-call | tf_op jit(solution)/shard_map/half_transform/pallas_call | solution.py:120
  43.7 35.0 %all_to_all.20 = bf16[32,64,256]{2,1,0:T(8,128)(2,1)S(1)} all-to-all(bf16[32,64,256]{2,1,0:T(8,128)(2,1)S(1)} %bitcast.19), channel_id=1, replica_groups=mesh['zl'=2,'x'=4,'core'=2,'y'=8,'zb'=2,'za'=2] {'y','zb','za'}, dimensions={0} | all-to-all | bytes 2097152 | tf_op jit(solution)/shard_map/all_to_all | solution.py:128
  78.7 1.9 %collective-permute-start.1 = (bf16[32,64,256]{2,1,0:T(8,128)(2,1)S(1)}, bf16[32,64,256]{2,1,0:T(8,128)(2,1)S(1)}, u32[]{:S(2)}, u32[]{:S(2)}) collective-permute-start(bf16[32,64,256]{2,1,0:T(8,128)(2,1)S(1)} %all_to_all.20), channel_id=1, source_target_pairs={{0,32},{32,0},{1,33},{33,1},{2,34},{34,2},{3,35},{35,3},{4,36},{36... | collective-permute-start | bytes 3145736 | tf_op jit(solution)/shard_map/ppermute | solution.py:129
  80.6 2.6 %collective-permute-done.1 = bf16[32,64,256]{2,1,0:T(8,128)(2,1)S(1)} collective-permute-done((bf16[32,64,256]{2,1,0:T(8,128)(2,1)S(1)}, bf16[32,64,256]{2,1,0:T(8,128)(2,1)S(1)}, u32[]{:S(2)}, u32[]{:S(2)}) %collective-permute-start.1) | collective-permute-done | bytes 1048608 | tf_op jit(solution)/shard_map/ppermute | solution.py:129
  83.3 2.3 %exchange_quarter.1 = bf16[8,208,768]{2,1,0:T(8,128)(2,1)S(1)} custom-call(s32[2]{0:T(128)S(1)} %pad_add_fusion.place, bf16[8,2,2,64,256]{4,3,2,1,0:T(8,128)(2,1)S(1)} %bitcast.20, bf16[8,2,2,64,256]{4,3,2,1,0:T(8,128)(2,1)S(1)} %bitcast.22, bf16[8,48,1536]{2,1,0:T(8,128)(2,1)S(1)} %copy-done, bf16[8,48,1536]{2,1,0:T(8,128)(2,1)S(1)} %collective-permute-done.other), custom_call_target="tpu_custom_call" | custom-call | tf_op jit(solution)/shard_map/exchange_quarter/pallas_call | solution.py:132
  85.6 35.2 %all_to_all.21 = bf16[8,208,768]{2,1,0:T(8,128)(2,1)S(1)} all-to-all(bf16[8,208,768]{2,1,0:T(8,128)(2,1)S(1)} %exchange_quarter.1), channel_id=1, replica_groups=mesh['zl'=2,'x'=4,'core'=2,'y'=8,'zb'=2,'za'=2] {'zl','x'}, dimensions={0} | all-to-all | bytes 5111808 | tf_op jit(solution)/shard_map/all_to_all | solution.py:144
  120.8 0.3 convert_reduce_fusion
  121.1 0.9 copy.9
  122.1 6.9 %all-to-all-start.3 = ((bf16[16,48,192]{2,1,0:T(8,128)(2,1)}), bf16[16,48,192]{2,1,0:T(8,128)(2,1)S(1)}, u32[]{:S(2)}, u32[]{:S(2)}) async-start(bf16[16,48,192]{2,1,0:T(8,128)(2,1)} %bitcast.9), calls=%async_computation.3 | async-start | bytes 786432 | tf_op jit(solution)/shard_map/all_to_all | solution.py:149
  129.1 0.6 copy.10
  129.7 13.7 %all-to-all-done.3 = bf16[16,48,192]{2,1,0:T(8,128)(2,1)S(1)} async-done(((bf16[16,48,192]{2,1,0:T(8,128)(2,1)}), bf16[16,48,192]{2,1,0:T(8,128)(2,1)S(1)}, u32[]{:S(2)}, u32[]{:S(2)}) %all-to-all-start.3) | async-done | bytes 294944 | tf_op jit(solution)/shard_map/all_to_all | solution.py:149
  143.3 0.1 convert_reduce_fusion.1
  143.4 0.1 reshape.35
  143.5 0.6 copy.11
  (5 shorter events, 0.1 us)
Async XLA Ops:
  0.6 41.6 %copy-start = (bf16[8,48,1536]{2,1,0:T(8,128)(2,1)S(1)}, bf16[8,48,1536]{2,1,0:T(8,128)(2,1)}, u32[]{:S(2)}) copy-start(bf16[8,48,1536]{2,1,0:T(8,128)(2,1)} %mine.3) | copy-start | bytes 3538948
  2.4 39.8 %all-to-all-start = ((bf16[32,48,256]{2,1,0:T(8,128)(2,1)}), bf16[32,48,256]{2,1,0:T(8,128)(2,1)S(1)}, u32[]{:S(2)}, u32[]{:S(2)}) async-start(bf16[32,48,256]{2,1,0:T(8,128)(2,1)} %broadcast_in_dim.2), calls=%async_computation | async-start | bytes 1572864 | tf_op jit(solution)/shard_map/all_to_all | solution.py:118
  18.4 5.0 %collective-permute-start = (bf16[8,48,1536]{2,1,0:T(8,128)(2,1)}, bf16[8,48,1536]{2,1,0:T(8,128)(2,1)S(1)}, u32[]{:S(2)}, u32[]{:S(2)}) collective-permute-start(bf16[8,48,1536]{2,1,0:T(8,128)(2,1)} %mine.3), channel_id=1, source_target_pairs={{0,32},{32,0},{1,33},{33,1},{2,34},{34,2},{3,35},{35,3},{4,36},{36... | collective-permute-start | bytes 3538952 | tf_op jit(solution)/shard_map/ppermute | solution.py:115
  78.7 4.5 %collective-permute-start.1 = (bf16[32,64,256]{2,1,0:T(8,128)(2,1)S(1)}, bf16[32,64,256]{2,1,0:T(8,128)(2,1)S(1)}, u32[]{:S(2)}, u32[]{:S(2)}) collective-permute-start(bf16[32,64,256]{2,1,0:T(8,128)(2,1)S(1)} %all_to_all.20), channel_id=1, source_target_pairs={{0,32},{32,0},{1,33},{33,1},{2,34},{34,2},{3,35},{35,3},{4,36},{36... | collective-permute-start | bytes 3145736 | tf_op jit(solution)/shard_map/ppermute | solution.py:129
  122.1 21.3 %all-to-all-start.3 = ((bf16[16,48,192]{2,1,0:T(8,128)(2,1)}), bf16[16,48,192]{2,1,0:T(8,128)(2,1)S(1)}, u32[]{:S(2)}, u32[]{:S(2)}) async-start(bf16[16,48,192]{2,1,0:T(8,128)(2,1)} %bitcast.9), calls=%async_computation.3 | async-start | bytes 786432 | tf_op jit(solution)/shard_map/all_to_all | solution.py:149

commit v4 on v3

v4 whole, which is shorter than its diff:
```python
import jax
import jax.numpy as jnp
from jax import lax
from jax.experimental import pallas as pl
from jax.experimental.pallas import tpu as pltpu
from jax.sharding import Mesh
from jax.sharding import PartitionSpec as P

NEAR = ("zl", "x")
FAR = ("y", "zb", "za")
SUMS = ("y", "za")
SWAP = [(0, 1), (1, 0)]
f32, bf16 = jnp.float32, jnp.bfloat16
SMEM = pl.BlockSpec(memory_space=pltpu.SMEM)
VMEM = pl.BlockSpec(memory_space=pltpu.VMEM)
PARAMS = pltpu.CompilerParams(vmem_limit_bytes=40 * 2**20)


def words(value):
    high = value.astype(bf16)
    return high, (value - high.astype(f32)).astype(bf16)


def spread_kernel(place, coeffs, own, pieces):
    half = coeffs.shape[2] // 2
    for c in range(2):
        low, high = coeffs[c, :, :half], coeffs[c, :, half:]
        part = jnp.where(place[0] == 0, low.astype(f32), high.astype(f32)).astype(bf16)
        own[:, c * half : (c + 1) * half] = part
        for o in range(pieces.shape[0]):
            pieces[o, :, c * half : (c + 1) * half] = part


def transform_kernel(place, full, mine, other, own, out):
    core = place[0]
    count, rows, nao = mine.shape
    wide = full.shape[1]
    half = wide // 2
    weight = own[...].astype(f32)
    lane = lax.broadcasted_iota(jnp.int32, (1, half), 1)
    terms = jnp.zeros((1, half), f32)
    for source, owner in ((mine, core), (other, 1 - core)):
        slab = jnp.dot(
            source[...].reshape(count * rows, nao), full[...], preferred_element_type=f32
        ).astype(bf16)
        for p in range(count):
            block = slab[p * rows : (p + 1) * rows]
            for zb in range(2):
                out[owner * (count // 2) + p // 2, zb, p % 2, 0:rows] = block[:, :half]
                out[owner * (count // 2) + p // 2, zb, p % 2, rows : 2 * rows] = block[:, half:]
            term = jnp.sum(block.astype(f32) * weight, axis=0, keepdims=True)
            term = jnp.sum(term, axis=1, keepdims=True)
            terms += jnp.where(lane == owner * count + p, term, 0.0)
    high, low = words(terms)
    lines = lax.broadcasted_iota(jnp.int32, (8, half), 0)
    rider = jnp.where(lines == 0, high.astype(f32), jnp.where(lines == 1, low.astype(f32), 0.0))
    rider = rider.astype(bf16)
    for y in range(8):
        for zb in range(2):
            for za in range(2):
                out[y, zb, za, 2 * rows : 2 * rows + 8] = rider


def exchange_kernel(place, got, got_other, mine, other, out, column_side, row_side):
    core, zb = place[0], place[1]
    count, rows, nao = mine.shape
    half = got.shape[4]
    wide = 2 * half
    for y in range(8):
        for za in range(2):
            for k, source in enumerate((got, got_other)):
                left = slice(k * wide, k * wide + half)
                right = slice(k * wide + half, (k + 1) * wide)
                at = pl.ds((2 * y + za) * rows, rows)
                row_side[at, left] = source[y, zb, za, 0:rows]
                row_side[at, right] = source[y, zb, za, rows : 2 * rows]
                real = source[y, core, za, 0:rows]
                imag = source[y, core, za, rows : 2 * rows]
                at = pl.ds((4 * y + za) * rows, rows)
                column_side[at, left] = real
                column_side[at, right] = imag
                at = pl.ds((4 * y + 2 + za) * rows, rows)
                column_side[at, left] = -imag
                column_side[at, right] = real

    riders = jnp.zeros((8, half), f32)
    for y in range(8):
        for b in range(2):
            for za in range(2):
                for source in (got, got_other):
                    riders += source[y, b, za, 2 * rows : 2 * rows + 8].astype(f32)
    weights = riders[0:1] + riders[1:2]
    lane = lax.broadcasted_iota(jnp.int32, (1, half), 1)
    for part in range(3):
        at = pl.ds(part * 16, 16)
        total = jnp.zeros((16, nao), f32)
        for source, owner in ((mine, core), (other, 1 - core)):
            for p in range(count):
                weight = jnp.sum(jnp.where(lane == owner * count + p, weights, 0.0), axis=1, keepdims=True)
                total += weight * source[p, at].astype(f32)
        for s in range(8):
            start = s * 4 * rows
            piece = jnp.where(
                core == 0, total[:, start : start + 2 * rows], total[:, start + 2 * rows : start + 4 * rows]
            )
            high, low = words(piece)
            gap = jnp.zeros((16, half - 2 * rows), bf16)
            out[s, 4 * rows : 4 * rows + 16, part * 256 : (part + 1) * 256] = jnp.concatenate(
                [high, gap, low, gap], axis=1
            )

    for n in range(3):
        block = lax.dot_general(
            column_side[...],
            row_side[n * 256 : (n + 1) * 256],
            (((1,), (1,)), ((), ())),
            preferred_element_type=f32,
        ).astype(bf16)
        for s in range(8):
            out[s, 0 : 4 * rows, n * 256 : (n + 1) * 256] = block[s * 4 * rows : (s + 1) * 4 * rows]


def near_sum_kernel(parts, out, coulomb):
    rows = coulomb.shape[0]
    deep = 4 * rows
    tail = jnp.sum(parts[:, deep : deep + 16].astype(f32), axis=0)
    for part in range(3):
        start = part * 256
        coulomb[part * 16 : (part + 1) * 16] = (
            tail[:, start : start + 2 * rows] + tail[:, start + 128 : start + 128 + 2 * rows]
        )
    for n in range(2):
        columns = slice(n * 8 * rows, (n + 1) * 8 * rows)
        turned = jnp.sum(parts[:, 0:deep, columns].astype(f32), axis=0).T
        for j in range(8):
            block = turned[j * rows : (j + 1) * rows]
            rest = jnp.concatenate([block[: rows // 2, 128:], block[rows // 2 :, 128:]], axis=1)
            out[n * 8 + j, 0:rows] = block[:, :128].astype(bf16)
            out[n * 8 + j, rows : rows + rows // 2] = rest.astype(bf16)


def far_sum_kernel(parts, out):
    rows = out.shape[1]
    total = jnp.sum(parts[...].astype(f32), axis=0)
    rest = jnp.concatenate([total[rows:, :64], total[rows:, 64:]], axis=0)
    out[0] = total[:rows, : 2 * rows]
    out[1] = jnp.concatenate([total[:rows, 2 * rows :], rest], axis=1)


def call(kernel, name, outs, inputs, place=None, scratch=()):
    specs = [VMEM] * len(inputs)
    if place is not None:
        specs, inputs = [SMEM] + specs, (place,) + inputs
    return pl.pallas_call(
        kernel,
        out_shape=[jax.ShapeDtypeStruct(shape, dtype) for shape, dtype in outs],
        in_specs=specs,
        out_specs=[VMEM] * len(outs),
        scratch_shapes=scratch,
        compiler_params=PARAMS,
        name=name,
    )(*inputs)


def on_device(vectors, coeffs):
    core = lax.axis_index("core")
    zb = lax.axis_index("zb")
    place = jnp.stack([core, zb]).astype(jnp.int32)
    count, rows, nao = vectors.shape
    half = coeffs.shape[2] // 2
    wide = 2 * half
    tall = 2 * rows + 8
    deep = 4 * rows + 16

    other_vectors = lax.ppermute(vectors, "core", SWAP)
    own, spread = call(
        spread_kernel, "spread", [((rows, wide), bf16), ((32, rows, wide), bf16)], (coeffs,), place
    )
    full = lax.all_to_all(spread, FAR, 0, 0, tiled=True).reshape(nao, wide)

    shape = (8, 2, 2, tall, half)
    (pieces,) = call(
        transform_kernel, "half_transform", [(shape, bf16)], (full, vectors, other_vectors, own), place
    )
    got = lax.all_to_all(pieces.reshape(32, tall, half), FAR, 0, 0, tiled=True)
    got_other = lax.ppermute(got, "core", SWAP)

    scratch = [pltpu.VMEM((32 * rows, 2 * wide), bf16), pltpu.VMEM((16 * rows, 2 * wide), bf16)]
    (parts,) = call(
        exchange_kernel,
        "exchange_quarter",
        [((8, deep, 16 * rows), bf16)],
        (got.reshape(shape), got_other.reshape(shape), vectors, other_vectors),
        place,
        scratch,
    )
    parts = lax.all_to_all(parts, NEAR, 0, 0, tiled=True)
    packed, coulomb = call(
        near_sum_kernel, "near_sum", [((16, rows + rows // 2, 128), bf16), ((rows, 2 * rows), f32)], (parts,)
    )
    packed = lax.all_to_all(packed, SUMS, 0, 0, tiled=True)
    (exchange,) = call(far_sum_kernel, "far_sum", [((2, rows, 2 * rows), f32)], (packed,))
    return exchange, coulomb


def solution(mesh):
    fine = Mesh(mesh.devices.reshape(2, 4, 2, 8, 2, 2), ("zl", "x", "core", "y", "zb", "za"))
    chol = ("zl", "x", "core")
    return jax.shard_map(
        on_device,
        mesh=fine,
        in_specs=(P(chol, FAR, None), P(None, FAR, None)),
        out_specs=(P(None, FAR, chol), P(FAR, chol)),
        check_vma=False,
    )
```

time: 145 us -> 140 us (0.966)
  blocking collectives: 70.2 us -> 85.1 us
  waiting for transfers between devices: 38.1 us -> 24.2 us
  starting transfers between devices: 26.7 us -> 19.8 us
  Pallas kernels: 3.78 us -> 7.19 us
  local copies, waits for them, and re-layouts: 4.1 us -> 2.07 us
    all_to_all x2 -> x3, blocking collectives: 70.2 us -> 85.1 us  [the longest x1 35.2 us: on_device(): parts = lax.all_to_all(parts, NEAR, 0, 0, tiled=True)]
    all_to_all x2 -> x1, waiting for transfers between devices: 32.6 us -> 18.9 us  [on_device(): full = lax.all_to_all(spread, FAR, 0, 0, tiled=True).reshape(nao, wide)]
    all_to_all x2 -> x1, starting transfers between devices: 22.8 us -> 16 us  [on_device(): full = lax.all_to_all(spread, FAR, 0, 0, tiled=True).reshape(nao, wide)]
    pallas_call x2 -> x5, Pallas kernels: 3.78 us -> 7.19 us  [call(): pl.pallas_call(kernel, out_shape=[jax.ShapeDtypeStruct(shape, dtype) for...]
  transfers between devices with their start and end apart: 4 -> 3, of which waited for: 4 -> 3; matrix products, arithmetic and copies ran while one was open for 1% -> 0% of each run, Pallas kernels for 0% -> 0%
where the time goes in v4:
time: 140 us; the launch traced here: 139 us
  blocking collectives  85.1 us (61%)
  waiting for transfers between devices  24.2 us (17%)
  starting transfers between devices  19.8 us (14%)
  Pallas kernels  7.19 us (5%)
  local copies, waits for them, and re-layouts  2.07 us (1%)
    all_to_all x1, blocking collectives, on_device(): parts = lax.all_to_all(parts, NEAR, 0, 0, tiled=True)  35.2 us
    all_to_all x1, blocking collectives, on_device(): got = lax.all_to_all(pieces.reshape(32, tall, half), FAR, 0, 0, tiled=True)  31.1 us
    all_to_all x1, waiting for transfers between devices, on_device(): full = lax.all_to_all(spread, FAR, 0, 0, tiled=True).reshape(nao, wide)  18.9 us
    all_to_all x1, blocking collectives, on_device(): packed = lax.all_to_all(packed, SUMS, 0, 0, tiled=True)  18.8 us
    all_to_all x1, starting transfers between devices, on_device(): full = lax.all_to_all(spread, FAR, 0, 0, tiled=True).reshape(nao, wide)  16 us
    pallas_call x5, Pallas kernels, call(): pl.pallas_call(kernel, out_shape=[jax.ShapeDtypeStruct(shape, dtype) for...  7.19 us
    ppermute x1, waiting for transfers between devices, on_device(): other_vectors = lax.ppermute(vectors, 'core', SWAP)  3.02 us
  transfers between devices with their start and end apart: 3, of which 3 were waited for; matrix products, arithmetic and copies ran while one was open for 0% of the time, Pallas kernels for 0%

profile of v4, /device:TPU:6, one launch (start us, length us, event | category | flops | bytes accessed | tf_op | source)
XLA Modules:
  0.0 139.1 jit_solution(8239288322566928878)
XLA Ops:
  0.6 0.1 pad_add_fusion.place
  0.7 0.0 copy-start.2
  0.7 0.8 copy-done.2
  1.5 1.5 %spread.1 = (bf16[48,256]{1,0:T(8,128)(2,1)S(1)}, bf16[32,48,256]{2,1,0:T(8,128)(2,1)}) custom-call(s32[2]{0:T(128)S(1)} %pad_add_fusion.place, bf16[2,48,256]{2,1,0:T(8,128)(2,1)S(1)} %copy-done.2), custom_call_target="tpu_custom_call" | custom-call | tf_op jit(solution)/shard_map/spread/pallas_call | solution.py:154
  3.0 16.0 %all-to-all-start = ((bf16[32,48,256]{2,1,0:T(8,128)(2,1)}), bf16[32,48,256]{2,1,0:T(8,128)(2,1)S(1)}, u32[]{:S(2)}, u32[]{:S(2)}) async-start(bf16[32,48,256]{2,1,0:T(8,128)(2,1)} %get-tuple-element.6), calls=%async_computation | async-start | bytes 1572864 | tf_op jit(solution)/shard_map/all_to_all | solution.py:179
  19.0 1.9 %collective-permute-start = (bf16[8,48,1536]{2,1,0:T(8,128)(2,1)}, bf16[8,48,1536]{2,1,0:T(8,128)(2,1)S(1)}, u32[]{:S(2)}, u32[]{:S(2)}) collective-permute-start(bf16[8,48,1536]{2,1,0:T(8,128)(2,1)} %mine.3), channel_id=1, source_target_pairs={{0,32},{32,0},{1,33},{33,1},{2,34},{34,2},{3,35},{35,3},{4,36},{36... | collective-permute-start | bytes 3538952 | tf_op jit(solution)/shard_map/ppermute | solution.py:175
  20.9 3.0 %collective-permute-done.other = bf16[8,48,1536]{2,1,0:T(8,128)(2,1)S(1)} collective-permute-done((bf16[8,48,1536]{2,1,0:T(8,128)(2,1)}, bf16[8,48,1536]{2,1,0:T(8,128)(2,1)S(1)}, u32[]{:S(2)}, u32[]{:S(2)}) %collective-permute-start) | collective-permute-done | bytes 1179680 | tf_op jit(solution)/shard_map/ppermute | solution.py:175
  24.0 18.9 %all-to-all-done = bf16[32,48,256]{2,1,0:T(8,128)(2,1)S(1)} async-done(((bf16[32,48,256]{2,1,0:T(8,128)(2,1)}), bf16[32,48,256]{2,1,0:T(8,128)(2,1)S(1)}, u32[]{:S(2)}, u32[]{:S(2)}) %all-to-all-start) | async-done | bytes 786464 | tf_op jit(solution)/shard_map/all_to_all | solution.py:179
  42.8 0.0 copy-start
  42.8 1.3 copy-done
  44.1 0.0 copy-start.1
  44.1 1.4 %half_transform.1 = bf16[8,2,2,104,128]{4,3,2,1,0:T(8,128)(2,1)S(1)} custom-call(s32[2]{0:T(128)S(1)} %pad_add_fusion.place, bf16[1536,256]{1,0:T(8,128)(2,1)S(1)} %bitcast.8, bf16[8,48,1536]{2,1,0:T(8,128)(2,1)S(1)} %copy-done, bf16[8,48,1536]{2,1,0:T(8,128)(2,1)S(1)} %collective-permute-done.other, bf16[48,256]{1,0:T(8,128)(2,1)S(1)} %get-tuple-element.7.own), custom_call_target="tpu_custom_call" | custom-call | tf_op jit(solution)/shard_map/half_transform/pallas_call | solution.py:154
  45.6 31.1 %all_to_all.20 = bf16[32,104,128]{2,1,0:T(8,128)(2,1)S(1)} all-to-all(bf16[32,104,128]{2,1,0:T(8,128)(2,1)S(1)} %bitcast.7), channel_id=1, replica_groups=mesh['zl'=2,'x'=4,'core'=2,'y'=8,'zb'=2,'za'=2] {'y','zb','za'}, dimensions={0} | all-to-all | bytes 1703936 | tf_op jit(solution)/shard_map/all_to_all | solution.py:185
  76.7 1.9 %collective-permute-start.1 = (bf16[32,104,128]{2,1,0:T(8,128)(2,1)S(1)}, bf16[32,104,128]{2,1,0:T(8,128)(2,1)S(1)}, u32[]{:S(2)}, u32[]{:S(2)}) collective-permute-start(bf16[32,104,128]{2,1,0:T(8,128)(2,1)S(1)} %all_to_all.20), channel_id=1, source_target_pairs={{0,32},{32,0},{1,33},{33,1},{2,34},{34,2},{3,35},{35,3},{4,36},{36... | collective-permute-start | bytes 2555912 | tf_op jit(solution)/shard_map/ppermute | solution.py:186
  78.6 2.3 %collective-permute-done.1 = bf16[32,104,128]{2,1,0:T(8,128)(2,1)S(1)} collective-permute-done((bf16[32,104,128]{2,1,0:T(8,128)(2,1)S(1)}, bf16[32,104,128]{2,1,0:T(8,128)(2,1)S(1)}, u32[]{:S(2)}, u32[]{:S(2)}) %collective-permute-start.1) | collective-permute-done | bytes 852000 | tf_op jit(solution)/shard_map/ppermute | solution.py:186
  80.9 0.0 copy-done.1
  80.9 2.4 %exchange_quarter.1 = bf16[8,208,768]{2,1,0:T(8,128)(2,1)S(1)} custom-call(s32[2]{0:T(128)S(1)} %pad_add_fusion.place, bf16[8,2,2,104,128]{4,3,2,1,0:T(8,128)(2,1)S(1)} %bitcast.6, bf16[8,2,2,104,128]{4,3,2,1,0:T(8,128)(2,1)S(1)} %bitcast.9, bf16[8,48,1536]{2,1,0:T(8,128)(2,1)S(1)} %copy-done.1, bf16[8,48,1536]{2,1,0:T(8,128)(2,1)S(1)} %collective-permute-done.other), custom_call_target="tpu_custom_call" | custom-call | tf_op jit(solution)/shard_map/exchange_quarter/pallas_call | solution.py:154
  83.3 35.2 %all_to_all.21.parts = bf16[8,208,768]{2,1,0:T(8,128)(2,1)S(1)} all-to-all(bf16[8,208,768]{2,1,0:T(8,128)(2,1)S(1)} %exchange_quarter.1), channel_id=1, replica_groups=mesh['zl'=2,'x'=4,'core'=2,'y'=8,'zb'=2,'za'=2] {'zl','x'}, dimensions={0} | all-to-all | bytes 5111808 | tf_op jit(solution)/shard_map/all_to_all | solution.py:197
  118.5 1.0 near_sum.1
  119.6 18.8 %all_to_all.22.parts = bf16[16,72,128]{2,1,0:T(8,128)(2,1)S(1)} all-to-all(bf16[16,72,128]{2,1,0:T(8,128)(2,1)S(1)} %get-tuple-element.8), channel_id=1, replica_groups=mesh['zl'=2,'x'=4,'core'=2,'y'=8,'zb'=2,'za'=2] {'y','za'}, dimensions={0} | all-to-all | bytes 589824 | tf_op jit(solution)/shard_map/all_to_all | solution.py:201
  138.3 0.8 far_sum.1
Async XLA Ops:
  0.7 0.8 copy-start.2
  3.0 39.8 %all-to-all-start = ((bf16[32,48,256]{2,1,0:T(8,128)(2,1)}), bf16[32,48,256]{2,1,0:T(8,128)(2,1)S(1)}, u32[]{:S(2)}, u32[]{:S(2)}) async-start(bf16[32,48,256]{2,1,0:T(8,128)(2,1)} %get-tuple-element.6), calls=%async_computation | async-start | bytes 1572864 | tf_op jit(solution)/shard_map/all_to_all | solution.py:179
  19.0 5.0 %collective-permute-start = (bf16[8,48,1536]{2,1,0:T(8,128)(2,1)}, bf16[8,48,1536]{2,1,0:T(8,128)(2,1)S(1)}, u32[]{:S(2)}, u32[]{:S(2)}) collective-permute-start(bf16[8,48,1536]{2,1,0:T(8,128)(2,1)} %mine.3), channel_id=1, source_target_pairs={{0,32},{32,0},{1,33},{33,1},{2,34},{34,2},{3,35},{35,3},{4,36},{36... | collective-permute-start | bytes 3538952 | tf_op jit(solution)/shard_map/ppermute | solution.py:175
  42.8 1.3 copy-start
  44.1 36.8 %copy-start.1 = (bf16[8,48,1536]{2,1,0:T(8,128)(2,1)S(1)}, bf16[8,48,1536]{2,1,0:T(8,128)(2,1)}, u32[]{:S(2)}) copy-start(bf16[8,48,1536]{2,1,0:T(8,128)(2,1)} %mine.3) | copy-start | bytes 3538948
  76.7 4.3 %collective-permute-start.1 = (bf16[32,104,128]{2,1,0:T(8,128)(2,1)S(1)}, bf16[32,104,128]{2,1,0:T(8,128)(2,1)S(1)}, u32[]{:S(2)}, u32[]{:S(2)}) collective-permute-start(bf16[32,104,128]{2,1,0:T(8,128)(2,1)S(1)} %all_to_all.20), channel_id=1, source_target_pairs={{0,32},{32,0},{1,33},{33,1},{2,34},{34,2},{3,35},{35,3},{4,36},{36... | collective-permute-start | bytes 2555912 | tf_op jit(solution)/shard_map/ppermute | solution.py:186

commit v5 on v4

--- a/solution.py
+++ b/solution.py
@@ -13,6 +13,7 @@
 f32, bf16 = jnp.float32, jnp.bfloat16
 SMEM = pl.BlockSpec(memory_space=pltpu.SMEM)
 VMEM = pl.BlockSpec(memory_space=pltpu.VMEM)
+HBM = pl.BlockSpec(memory_space=pltpu.HBM)
 PARAMS = pltpu.CompilerParams(vmem_limit_bytes=40 * 2**20)
 
 
@@ -21,25 +22,29 @@
     return high, (value - high.astype(f32)).astype(bf16)
 
 
-def spread_kernel(place, coeffs, own, pieces):
-    half = coeffs.shape[2] // 2
-    for c in range(2):
-        low, high = coeffs[c, :, :half], coeffs[c, :, half:]
-        part = jnp.where(place[0] == 0, low.astype(f32), high.astype(f32)).astype(bf16)
-        own[:, c * half : (c + 1) * half] = part
-        for o in range(pieces.shape[0]):
-            pieces[o, :, c * half : (c + 1) * half] = part
-
-
-def transform_kernel(place, full, mine, other, own, out):
+def spread_kernel(place, coeffs, pieces, sems):
+    copies = [
+        pltpu.make_async_copy(coeffs.at[place[0]], pieces.at[o], sems.at[o]) for o in range(pieces.shape[0])
+    ]
+    for copy in copies:
+        copy.start()
+    for copy in copies:
+        copy.wait()
+
+
+def transform_kernel(place, full, mine, other, coeffs, out, held, sem):
+    copy = pltpu.make_async_copy(mine, held, sem)
+    copy.start()
     core = place[0]
     count, rows, nao = mine.shape
     wide = full.shape[1]
     half = wide // 2
-    weight = own[...].astype(f32)
+    weight = coeffs[core].astype(f32)
     lane = lax.broadcasted_iota(jnp.int32, (1, half), 1)
     terms = jnp.zeros((1, half), f32)
-    for source, owner in ((mine, core), (other, 1 - core)):
+    for source, owner in ((other, 1 - core), (held, core)):
+        if source is held:
+            copy.wait()
         slab = jnp.dot(
             source[...].reshape(count * rows, nao), full[...], preferred_element_type=f32
         ).astype(bf16)
@@ -66,22 +71,25 @@
     count, rows, nao = mine.shape
     half = got.shape[4]
     wide = 2 * half
+    own_sign = jnp.where(core == 0, 1.0, -1.0).astype(bf16)
+    other_sign = jnp.where(core == 0, -1.0, 1.0).astype(bf16)
     for y in range(8):
         for za in range(2):
-            for k, source in enumerate((got, got_other)):
-                left = slice(k * wide, k * wide + half)
-                right = slice(k * wide + half, (k + 1) * wide)
+            for h in range(2):
+                own_at = slice(h * half, (h + 1) * half)
+                other_at = slice(wide + h * half, wide + (h + 1) * half)
+                part = slice(h * rows, (h + 1) * rows)
                 at = pl.ds((2 * y + za) * rows, rows)
-                row_side[at, left] = source[y, zb, za, 0:rows]
-                row_side[at, right] = source[y, zb, za, rows : 2 * rows]
-                real = source[y, core, za, 0:rows]
-                imag = source[y, core, za, rows : 2 * rows]
+                row_side[at, own_at] = got[y, zb, za, part]
+                row_side[at, other_at] = got_other[y, zb, za, part]
+                own = got[y, core, za, part]
+                other_part = got_other[y, core, za, part]
                 at = pl.ds((4 * y + za) * rows, rows)
-                column_side[at, left] = real
-                column_side[at, right] = imag
+                column_side[at, own_at] = own
+                column_side[at, other_at] = other_part
                 at = pl.ds((4 * y + 2 + za) * rows, rows)
-                column_side[at, left] = -imag
-                column_side[at, right] = real
+                column_side[at, own_at] = other_part * other_sign
+                column_side[at, other_at] = own * own_sign
 
     riders = jnp.zeros((8, half), f32)
     for y in range(8):
@@ -91,13 +99,16 @@
                     riders += source[y, b, za, 2 * rows : 2 * rows + 8].astype(f32)
     weights = riders[0:1] + riders[1:2]
     lane = lax.broadcasted_iota(jnp.int32, (1, half), 1)
+    weighted = []
+    for source, owner in ((mine, core), (other, 1 - core)):
+        for p in range(count):
+            weight = jnp.sum(jnp.where(lane == owner * count + p, weights, 0.0), axis=1, keepdims=True)
+            weighted.append((source, p, weight))
     for part in range(3):
         at = pl.ds(part * 16, 16)
         total = jnp.zeros((16, nao), f32)
-        for source, owner in ((mine, core), (other, 1 - core)):
-            for p in range(count):
-                weight = jnp.sum(jnp.where(lane == owner * count + p, weights, 0.0), axis=1, keepdims=True)
-                total += weight * source[p, at].astype(f32)
+        for source, p, weight in weighted:
+            total += weight * source[p, at].astype(f32)
         for s in range(8):
             start = s * 4 * rows
             piece = jnp.where(
@@ -147,15 +158,15 @@
     out[1] = jnp.concatenate([total[:rows, 2 * rows :], rest], axis=1)
 
 
-def call(kernel, name, outs, inputs, place=None, scratch=()):
-    specs = [VMEM] * len(inputs)
+def call(kernel, name, outs, inputs, place=None, scratch=(), specs=None, out_spec=VMEM):
+    specs = specs or [VMEM] * len(inputs)
     if place is not None:
         specs, inputs = [SMEM] + specs, (place,) + inputs
     return pl.pallas_call(
         kernel,
         out_shape=[jax.ShapeDtypeStruct(shape, dtype) for shape, dtype in outs],
         in_specs=specs,
-        out_specs=[VMEM] * len(outs),
+        out_specs=[out_spec] * len(outs),
         scratch_shapes=scratch,
         compiler_params=PARAMS,
         name=name,
@@ -167,20 +178,33 @@
     zb = lax.axis_index("zb")
     place = jnp.stack([core, zb]).astype(jnp.int32)
     count, rows, nao = vectors.shape
-    half = coeffs.shape[2] // 2
-    wide = 2 * half
+    wide = coeffs.shape[2]
+    half = wide // 2
     tall = 2 * rows + 8
     deep = 4 * rows + 16
 
     other_vectors = lax.ppermute(vectors, "core", SWAP)
-    own, spread = call(
-        spread_kernel, "spread", [((rows, wide), bf16), ((32, rows, wide), bf16)], (coeffs,), place
+    (spread,) = call(
+        spread_kernel,
+        "spread",
+        [((32, rows, wide), bf16)],
+        (coeffs,),
+        place,
+        [pltpu.SemaphoreType.DMA((32,))],
+        [HBM],
+        HBM,
     )
     full = lax.all_to_all(spread, FAR, 0, 0, tiled=True).reshape(nao, wide)
 
     shape = (8, 2, 2, tall, half)
     (pieces,) = call(
-        transform_kernel, "half_transform", [(shape, bf16)], (full, vectors, other_vectors, own), place
+        transform_kernel,
+        "half_transform",
+        [(shape, bf16)],
+        (full, vectors, other_vectors, coeffs),
+        place,
+        [pltpu.VMEM(vectors.shape, bf16), pltpu.SemaphoreType.DMA],
+        [VMEM, HBM, VMEM, VMEM],
     )
     got = lax.all_to_all(pieces.reshape(32, tall, half), FAR, 0, 0, tiled=True)
     got_other = lax.ppermute(got, "core", SWAP)

time: 140 us -> 141 us (level)
  no operation moved by 1% of the time
where the time goes in v5:
time: 141 us; the launch traced here: 140 us
  blocking collectives  85.1 us (60%)
  waiting for transfers between devices  24.2 us (17%)
  starting transfers between devices  19.8 us (14%)
  Pallas kernels  8.38 us (6%)
  local copies, waits for them, and re-layouts  1.68 us (1%)
    all_to_all x1, blocking collectives, on_device(): parts = lax.all_to_all(parts, NEAR, 0, 0, tiled=True)  35.2 us
    all_to_all x1, blocking collectives, on_device(): got = lax.all_to_all(pieces.reshape(32, tall, half), FAR, 0, 0, tiled=True)  31.1 us
    all_to_all x1, waiting for transfers between devices, on_device(): full = lax.all_to_all(spread, FAR, 0, 0, tiled=True).reshape(nao, wide)  18.9 us
    all_to_all x1, blocking collectives, on_device(): packed = lax.all_to_all(packed, SUMS, 0, 0, tiled=True)  18.8 us
    all_to_all x1, starting transfers between devices, on_device(): full = lax.all_to_all(spread, FAR, 0, 0, tiled=True).reshape(nao, wide)  16 us
    pallas_call x5, Pallas kernels, call(): pl.pallas_call(kernel, out_shape=[jax.ShapeDtypeStruct(shape, dtype) for...  8.38 us
    ppermute x1, waiting for transfers between devices, on_device(): other_vectors = lax.ppermute(vectors, 'core', SWAP)  3.02 us
  transfers between devices with their start and end apart: 3, of which 3 were waited for; matrix products, arithmetic and copies ran while one was open for 0% of the time, Pallas kernels for 0%

profile of v5, /device:TPU:6, one launch (start us, length us, event | category | flops | bytes accessed | tf_op | source)
XLA Modules:
  0.0 140.0 jit_solution(7790746704843396756)
XLA Ops:
  0.6 0.0 copy-start
  0.6 0.1 pad_add_fusion.place
  0.7 0.0 copy-start.1
  0.7 0.9 copy-done.1
  1.6 1.7 %spread.1 = bf16[32,48,256]{2,1,0:T(8,128)(2,1)} custom-call(s32[2]{0:T(128)S(1)} %pad_add_fusion.place, bf16[2,48,256]{2,1,0:T(8,128)(2,1)S(1)} %copy-done.1), custom_call_target="tpu_custom_call" | custom-call | tf_op jit(solution)/shard_map/spread/pallas_call | solution.py:165
  3.3 16.0 %all-to-all-start = ((bf16[32,48,256]{2,1,0:T(8,128)(2,1)}), bf16[32,48,256]{2,1,0:T(8,128)(2,1)S(1)}, u32[]{:S(2)}, u32[]{:S(2)}) async-start(bf16[32,48,256]{2,1,0:T(8,128)(2,1)} %spread.1), calls=%async_computation | async-start | bytes 1572864 | tf_op jit(solution)/shard_map/all_to_all | solution.py:197
  19.3 1.9 %collective-permute-start = (bf16[8,48,1536]{2,1,0:T(8,128)(2,1)}, bf16[8,48,1536]{2,1,0:T(8,128)(2,1)S(1)}, u32[]{:S(2)}, u32[]{:S(2)}) collective-permute-start(bf16[8,48,1536]{2,1,0:T(8,128)(2,1)} %mine.3), channel_id=1, source_target_pairs={{0,32},{32,0},{1,33},{33,1},{2,34},{34,2},{3,35},{35,3},{4,36},{36... | collective-permute-start | bytes 3538952 | tf_op jit(solution)/shard_map/ppermute | solution.py:186
  21.2 3.0 %collective-permute-done.other = bf16[8,48,1536]{2,1,0:T(8,128)(2,1)S(1)} collective-permute-done((bf16[8,48,1536]{2,1,0:T(8,128)(2,1)}, bf16[8,48,1536]{2,1,0:T(8,128)(2,1)S(1)}, u32[]{:S(2)}, u32[]{:S(2)}) %collective-permute-start) | collective-permute-done | bytes 1179680 | tf_op jit(solution)/shard_map/ppermute | solution.py:186
  24.3 18.9 %all-to-all-done = bf16[32,48,256]{2,1,0:T(8,128)(2,1)S(1)} async-done(((bf16[32,48,256]{2,1,0:T(8,128)(2,1)}), bf16[32,48,256]{2,1,0:T(8,128)(2,1)S(1)}, u32[]{:S(2)}, u32[]{:S(2)}) %all-to-all-start) | async-done | bytes 786464 | tf_op jit(solution)/shard_map/all_to_all | solution.py:197
  43.1 0.0 copy-done
  43.1 0.0 copy-start.2
  43.1 0.8 copy-done.2
  43.9 2.5 %half_transform.1 = bf16[8,2,2,104,128]{4,3,2,1,0:T(8,128)(2,1)S(1)} custom-call(s32[2]{0:T(128)S(1)} %pad_add_fusion.place, bf16[1536,256]{1,0:T(8,128)(2,1)S(1)} %bitcast.8, bf16[8,48,1536]{2,1,0:T(8,128)(2,1)S(1)} %copy-done, bf16[8,48,1536]{2,1,0:T(8,128)(2,1)S(1)} %collective-permute-done.other, bf16[2,48,256]{2,1,0:T(8,128)(2,1)S(1)} %copy-done.2), custom_call_target="tpu_custom_call" | custom-call | tf_op jit(solution)/shard_map/half_transform/pallas_call | solution.py:165
  46.4 31.1 %all_to_all.20 = bf16[32,104,128]{2,1,0:T(8,128)(2,1)S(1)} all-to-all(bf16[32,104,128]{2,1,0:T(8,128)(2,1)S(1)} %bitcast.7), channel_id=1, replica_groups=mesh['zl'=2,'x'=4,'core'=2,'y'=8,'zb'=2,'za'=2] {'y','zb','za'}, dimensions={0} | all-to-all | bytes 1703936 | tf_op jit(solution)/shard_map/all_to_all | solution.py:209
  77.5 1.9 %collective-permute-start.1 = (bf16[32,104,128]{2,1,0:T(8,128)(2,1)S(1)}, bf16[32,104,128]{2,1,0:T(8,128)(2,1)S(1)}, u32[]{:S(2)}, u32[]{:S(2)}) collective-permute-start(bf16[32,104,128]{2,1,0:T(8,128)(2,1)S(1)} %all_to_all.20), channel_id=1, source_target_pairs={{0,32},{32,0},{1,33},{33,1},{2,34},{34,2},{3,35},{35,3},{4,36},{36... | collective-permute-start | bytes 2555912 | tf_op jit(solution)/shard_map/ppermute | solution.py:210
  79.4 2.3 %collective-permute-done.1 = bf16[32,104,128]{2,1,0:T(8,128)(2,1)S(1)} collective-permute-done((bf16[32,104,128]{2,1,0:T(8,128)(2,1)S(1)}, bf16[32,104,128]{2,1,0:T(8,128)(2,1)S(1)}, u32[]{:S(2)}, u32[]{:S(2)}) %collective-permute-start.1) | collective-permute-done | bytes 852000 | tf_op jit(solution)/shard_map/ppermute | solution.py:210
  81.8 2.4 %exchange_quarter.1 = bf16[8,208,768]{2,1,0:T(8,128)(2,1)S(1)} custom-call(s32[2]{0:T(128)S(1)} %pad_add_fusion.place, bf16[8,2,2,104,128]{4,3,2,1,0:T(8,128)(2,1)S(1)} %bitcast.6, bf16[8,2,2,104,128]{4,3,2,1,0:T(8,128)(2,1)S(1)} %bitcast.9, bf16[8,48,1536]{2,1,0:T(8,128)(2,1)S(1)} %copy-done, bf16[8,48,1536]{2,1,0:T(8,128)(2,1)S(1)} %collective-permute-done.other), custom_call_target="tpu_custom_call" | custom-call | tf_op jit(solution)/shard_map/exchange_quarter/pallas_call | solution.py:165
  84.2 35.2 %all_to_all.21.parts = bf16[8,208,768]{2,1,0:T(8,128)(2,1)S(1)} all-to-all(bf16[8,208,768]{2,1,0:T(8,128)(2,1)S(1)} %exchange_quarter.1), channel_id=1, replica_groups=mesh['zl'=2,'x'=4,'core'=2,'y'=8,'zb'=2,'za'=2] {'zl','x'}, dimensions={0} | all-to-all | bytes 5111808 | tf_op jit(solution)/shard_map/all_to_all | solution.py:221
  119.4 1.0 near_sum.1
  120.4 18.8 %all_to_all.22.parts = bf16[16,72,128]{2,1,0:T(8,128)(2,1)S(1)} all-to-all(bf16[16,72,128]{2,1,0:T(8,128)(2,1)S(1)} %get-tuple-element.4), channel_id=1, replica_groups=mesh['zl'=2,'x'=4,'core'=2,'y'=8,'zb'=2,'za'=2] {'y','za'}, dimensions={0} | all-to-all | bytes 589824 | tf_op jit(solution)/shard_map/all_to_all | solution.py:225
  139.2 0.8 far_sum.1
Async XLA Ops:
  0.6 42.5 %copy-start = (bf16[8,48,1536]{2,1,0:T(8,128)(2,1)S(1)}, bf16[8,48,1536]{2,1,0:T(8,128)(2,1)}, u32[]{:S(2)}) copy-start(bf16[8,48,1536]{2,1,0:T(8,128)(2,1)} %mine.3) | copy-start | bytes 3538948
  0.7 0.9 copy-start.1
  3.3 39.8 %all-to-all-start = ((bf16[32,48,256]{2,1,0:T(8,128)(2,1)}), bf16[32,48,256]{2,1,0:T(8,128)(2,1)S(1)}, u32[]{:S(2)}, u32[]{:S(2)}) async-start(bf16[32,48,256]{2,1,0:T(8,128)(2,1)} %spread.1), calls=%async_computation | async-start | bytes 1572864 | tf_op jit(solution)/shard_map/all_to_all | solution.py:197
  19.3 5.0 %collective-permute-start = (bf16[8,48,1536]{2,1,0:T(8,128)(2,1)}, bf16[8,48,1536]{2,1,0:T(8,128)(2,1)S(1)}, u32[]{:S(2)}, u32[]{:S(2)}) collective-permute-start(bf16[8,48,1536]{2,1,0:T(8,128)(2,1)} %mine.3), channel_id=1, source_target_pairs={{0,32},{32,0},{1,33},{33,1},{2,34},{34,2},{3,35},{35,3},{4,36},{36... | collective-permute-start | bytes 3538952 | tf_op jit(solution)/shard_map/ppermute | solution.py:186
  43.1 0.8 copy-start.2
  77.5 4.3 %collective-permute-start.1 = (bf16[32,104,128]{2,1,0:T(8,128)(2,1)S(1)}, bf16[32,104,128]{2,1,0:T(8,128)(2,1)S(1)}, u32[]{:S(2)}, u32[]{:S(2)}) collective-permute-start(bf16[32,104,128]{2,1,0:T(8,128)(2,1)S(1)} %all_to_all.20), channel_id=1, source_target_pairs={{0,32},{32,0},{1,33},{33,1},{2,34},{34,2},{3,35},{35,3},{4,36},{36... | collective-permute-start | bytes 2555912 | tf_op jit(solution)/shard_map/ppermute | solution.py:210

commit v6 on v5

--- a/solution.py
+++ b/solution.py
@@ -13,8 +13,6 @@
 f32, bf16 = jnp.float32, jnp.bfloat16
 SMEM = pl.BlockSpec(memory_space=pltpu.SMEM)
 VMEM = pl.BlockSpec(memory_space=pltpu.VMEM)
-HBM = pl.BlockSpec(memory_space=pltpu.HBM)
-PARAMS = pltpu.CompilerParams(vmem_limit_bytes=40 * 2**20)
 
 
 def words(value):
@@ -22,29 +20,15 @@
     return high, (value - high.astype(f32)).astype(bf16)
 
 
-def spread_kernel(place, coeffs, pieces, sems):
-    copies = [
-        pltpu.make_async_copy(coeffs.at[place[0]], pieces.at[o], sems.at[o]) for o in range(pieces.shape[0])
-    ]
-    for copy in copies:
-        copy.start()
-    for copy in copies:
-        copy.wait()
-
-
-def transform_kernel(place, full, mine, other, coeffs, out, held, sem):
-    copy = pltpu.make_async_copy(mine, held, sem)
-    copy.start()
+def transform_kernel(place, full, mine, other, own, out):
     core = place[0]
     count, rows, nao = mine.shape
     wide = full.shape[1]
     half = wide // 2
-    weight = coeffs[core].astype(f32)
+    weight = own[...].astype(f32)
     lane = lax.broadcasted_iota(jnp.int32, (1, half), 1)
     terms = jnp.zeros((1, half), f32)
-    for source, owner in ((other, 1 - core), (held, core)):
-        if source is held:
-            copy.wait()
+    for source, owner in ((mine, core), (other, 1 - core)):
         slab = jnp.dot(
             source[...].reshape(count * rows, nao), full[...], preferred_element_type=f32
         ).astype(bf16)
@@ -158,17 +142,17 @@
     out[1] = jnp.concatenate([total[:rows, 2 * rows :], rest], axis=1)
 
 
-def call(kernel, name, outs, inputs, place=None, scratch=(), specs=None, out_spec=VMEM):
-    specs = specs or [VMEM] * len(inputs)
+def call(kernel, name, grant, outs, inputs, place=None, scratch=()):
+    specs = [VMEM] * len(inputs)
     if place is not None:
         specs, inputs = [SMEM] + specs, (place,) + inputs
     return pl.pallas_call(
         kernel,
         out_shape=[jax.ShapeDtypeStruct(shape, dtype) for shape, dtype in outs],
         in_specs=specs,
-        out_specs=[out_spec] * len(outs),
+        out_specs=[VMEM] * len(outs),
         scratch_shapes=scratch,
-        compiler_params=PARAMS,
+        compiler_params=pltpu.CompilerParams(vmem_limit_bytes=grant * 2**20),
         name=name,
     )(*inputs)
 
@@ -184,27 +168,17 @@
     deep = 4 * rows + 16
 
     other_vectors = lax.ppermute(vectors, "core", SWAP)
-    (spread,) = call(
-        spread_kernel,
-        "spread",
-        [((32, rows, wide), bf16)],
-        (coeffs,),
-        place,
-        [pltpu.SemaphoreType.DMA((32,))],
-        [HBM],
-        HBM,
-    )
-    full = lax.all_to_all(spread, FAR, 0, 0, tiled=True).reshape(nao, wide)
+    own = lax.dynamic_index_in_dim(coeffs, core, 0, keepdims=False)
+    full = lax.all_to_all(jnp.broadcast_to(own[None], (32, rows, wide)), FAR, 0, 0, tiled=True).reshape(nao, wide)
 
     shape = (8, 2, 2, tall, half)
     (pieces,) = call(
         transform_kernel,
         "half_transform",
+        16,
         [(shape, bf16)],
-        (full, vectors, other_vectors, coeffs),
+        (full, vectors, other_vectors, own),
         place,
-        [pltpu.VMEM(vectors.shape, bf16), pltpu.SemaphoreType.DMA],
-        [VMEM, HBM, VMEM, VMEM],
     )
     got = lax.all_to_all(pieces.reshape(32, tall, half), FAR, 0, 0, tiled=True)
     got_other = lax.ppermute(got, "core", SWAP)
@@ -213,6 +187,7 @@
     (parts,) = call(
         exchange_kernel,
         "exchange_quarter",
+        24,
         [((8, deep, 16 * rows), bf16)],
         (got.reshape(shape), got_other.reshape(shape), vectors, other_vectors),
         place,
@@ -220,10 +195,10 @@
     )
     parts = lax.all_to_all(parts, NEAR, 0, 0, tiled=True)
     packed, coulomb = call(
-        near_sum_kernel, "near_sum", [((16, rows + rows // 2, 128), bf16), ((rows, 2 * rows), f32)], (parts,)
+        near_sum_kernel, "near_sum", 12, [((16, rows + rows // 2, 128), bf16), ((rows, 2 * rows), f32)], (parts,)
     )
     packed = lax.all_to_all(packed, SUMS, 0, 0, tiled=True)
-    (exchange,) = call(far_sum_kernel, "far_sum", [((2, rows, 2 * rows), f32)], (packed,))
+    (exchange,) = call(far_sum_kernel, "far_sum", 4, [((2, rows, 2 * rows), f32)], (packed,))
     return exchange, coulomb
 
 

time: 141 us -> 138 us (0.979)
  Pallas kernels: 8.38 us -> 5.64 us
    pallas_call x5 -> x4, Pallas kernels: 8.38 us -> 5.64 us  [call(): pl.pallas_call(kernel, out_shape=[jax.ShapeDtypeStruct(shape, dtype) for...]
where the time goes in v6:
time: 138 us; the launch traced here: 137 us
  blocking collectives  85 us (62%)
  waiting for transfers between devices  24.2 us (18%)
  starting transfers between devices  19.8 us (14%)
  Pallas kernels  5.64 us (4%)
  local copies, waits for them, and re-layouts  1.73 us (1%)
    all_to_all x1, blocking collectives, on_device(): parts = lax.all_to_all(parts, NEAR, 0, 0, tiled=True)  35.2 us
    all_to_all x1, blocking collectives, on_device(): got = lax.all_to_all(pieces.reshape(32, tall, half), FAR, 0, 0, tiled=True)  31.1 us
    all_to_all x1, waiting for transfers between devices, on_device(): lax.all_to_all(jnp.broadcast_to(own[None], (32, rows, wide)), FAR, 0, 0,...  18.9 us
    all_to_all x1, blocking collectives, on_device(): packed = lax.all_to_all(packed, SUMS, 0, 0, tiled=True)  18.8 us
    all_to_all x1, starting transfers between devices, on_device(): lax.all_to_all(jnp.broadcast_to(own[None], (32, rows, wide)), FAR, 0, 0,...  16 us
    pallas_call x4, Pallas kernels, call(): pl.pallas_call(kernel, out_shape=[jax.ShapeDtypeStruct(shape, dtype) for...  5.64 us
    ppermute x1, waiting for transfers between devices, on_device(): other_vectors = lax.ppermute(vectors, 'core', SWAP)  2.94 us
  transfers between devices with their start and end apart: 3, of which 3 were waited for; matrix products, arithmetic and copies ran while one was open for 0% of the time, Pallas kernels for 0%

profile of v6, /device:TPU:6, one launch (start us, length us, event | category | flops | bytes accessed | tf_op | source)
XLA Modules:
  0.0 137.1 jit_solution(10598541568685319583)
XLA Ops:
  0.6 0.0 copy-start
  0.6 0.0 copy-start.1
  0.7 0.8 copy-done
  1.4 0.9 broadcast_in_dim.9
  2.4 16.0 %all-to-all-start = ((bf16[32,48,256]{2,1,0:T(8,128)(2,1)}), bf16[32,48,256]{2,1,0:T(8,128)(2,1)S(1)}, u32[]{:S(2)}, u32[]{:S(2)}) async-start(bf16[32,48,256]{2,1,0:T(8,128)(2,1)} %broadcast_in_dim.9), calls=%async_computation | async-start | bytes 1572864 | tf_op jit(solution)/shard_map/all_to_all | solution.py:172
  18.3 1.9 %collective-permute-start = (bf16[8,48,1536]{2,1,0:T(8,128)(2,1)}, bf16[8,48,1536]{2,1,0:T(8,128)(2,1)S(1)}, u32[]{:S(2)}, u32[]{:S(2)}) collective-permute-start(bf16[8,48,1536]{2,1,0:T(8,128)(2,1)} %mine.3), channel_id=1, source_target_pairs={{0,32},{32,0},{1,33},{33,1},{2,34},{34,2},{3,35},{35,3},{4,36},{36... | collective-permute-start | bytes 3538952 | tf_op jit(solution)/shard_map/ppermute | solution.py:170
  20.3 0.1 pad_add_fusion.place
  20.4 2.9 %collective-permute-done.other = bf16[8,48,1536]{2,1,0:T(8,128)(2,1)S(1)} collective-permute-done((bf16[8,48,1536]{2,1,0:T(8,128)(2,1)}, bf16[8,48,1536]{2,1,0:T(8,128)(2,1)S(1)}, u32[]{:S(2)}, u32[]{:S(2)}) %collective-permute-start) | collective-permute-done | bytes 1179680 | tf_op jit(solution)/shard_map/ppermute | solution.py:170
  23.3 18.9 %all-to-all-done = bf16[32,48,256]{2,1,0:T(8,128)(2,1)S(1)} async-done(((bf16[32,48,256]{2,1,0:T(8,128)(2,1)}), bf16[32,48,256]{2,1,0:T(8,128)(2,1)S(1)}, u32[]{:S(2)}, u32[]{:S(2)}) %all-to-all-start) | async-done | bytes 786464 | tf_op jit(solution)/shard_map/all_to_all | solution.py:172
  42.2 0.0 copy-done.1
  42.2 1.4 %half_transform.1 = bf16[8,2,2,104,128]{4,3,2,1,0:T(8,128)(2,1)S(1)} custom-call(s32[2]{0:T(128)S(1)} %pad_add_fusion.place, bf16[1536,256]{1,0:T(8,128)(2,1)S(1)} %bitcast.10, bf16[8,48,1536]{2,1,0:T(8,128)(2,1)S(1)} %copy-done.1, bf16[8,48,1536]{2,1,0:T(8,128)(2,1)S(1)} %collective-permute-done.other, bf16[48,256]{1,0:T(8,128)(2,1)S(1)} %dynamic-slice_bitcast_fusion.own), custom_call_target="tpu_custom_call" | custom-call | tf_op jit(solution)/shard_map/half_transform/pallas_call | solution.py:149
  43.6 31.1 %all_to_all.20 = bf16[32,104,128]{2,1,0:T(8,128)(2,1)S(1)} all-to-all(bf16[32,104,128]{2,1,0:T(8,128)(2,1)S(1)} %bitcast.9), channel_id=1, replica_groups=mesh['zl'=2,'x'=4,'core'=2,'y'=8,'zb'=2,'za'=2] {'y','zb','za'}, dimensions={0} | all-to-all | bytes 1703936 | tf_op jit(solution)/shard_map/all_to_all | solution.py:183
  74.7 1.9 %collective-permute-start.1 = (bf16[32,104,128]{2,1,0:T(8,128)(2,1)S(1)}, bf16[32,104,128]{2,1,0:T(8,128)(2,1)S(1)}, u32[]{:S(2)}, u32[]{:S(2)}) collective-permute-start(bf16[32,104,128]{2,1,0:T(8,128)(2,1)S(1)} %all_to_all.20), channel_id=1, source_target_pairs={{0,32},{32,0},{1,33},{33,1},{2,34},{34,2},{3,35},{35,3},{4,36},{36... | collective-permute-start | bytes 2555912 | tf_op jit(solution)/shard_map/ppermute | solution.py:184
  76.6 2.3 %collective-permute-done.1 = bf16[32,104,128]{2,1,0:T(8,128)(2,1)S(1)} collective-permute-done((bf16[32,104,128]{2,1,0:T(8,128)(2,1)S(1)}, bf16[32,104,128]{2,1,0:T(8,128)(2,1)S(1)}, u32[]{:S(2)}, u32[]{:S(2)}) %collective-permute-start.1) | collective-permute-done | bytes 852000 | tf_op jit(solution)/shard_map/ppermute | solution.py:184
  79.0 2.4 %exchange_quarter.1 = bf16[8,208,768]{2,1,0:T(8,128)(2,1)S(1)} custom-call(s32[2]{0:T(128)S(1)} %pad_add_fusion.place, bf16[8,2,2,104,128]{4,3,2,1,0:T(8,128)(2,1)S(1)} %bitcast.8, bf16[8,2,2,104,128]{4,3,2,1,0:T(8,128)(2,1)S(1)} %bitcast.11, bf16[8,48,1536]{2,1,0:T(8,128)(2,1)S(1)} %copy-done.1, bf16[8,48,1536]{2,1,0:T(8,128)(2,1)S(1)} %collective-permute-done.other), custom_call_target="tpu_custom_call" | custom-call | tf_op jit(solution)/shard_map/exchange_quarter/pallas_call | solution.py:149
  81.4 35.2 %all_to_all.21.parts = bf16[8,208,768]{2,1,0:T(8,128)(2,1)S(1)} all-to-all(bf16[8,208,768]{2,1,0:T(8,128)(2,1)S(1)} %exchange_quarter.1), channel_id=1, replica_groups=mesh['zl'=2,'x'=4,'core'=2,'y'=8,'zb'=2,'za'=2] {'zl','x'}, dimensions={0} | all-to-all | bytes 5111808 | tf_op jit(solution)/shard_map/all_to_all | solution.py:196
  116.6 1.0 near_sum.1
  117.6 18.8 %all_to_all.22.parts = bf16[16,72,128]{2,1,0:T(8,128)(2,1)S(1)} all-to-all(bf16[16,72,128]{2,1,0:T(8,128)(2,1)S(1)} %get-tuple-element.4), channel_id=1, replica_groups=mesh['zl'=2,'x'=4,'core'=2,'y'=8,'zb'=2,'za'=2] {'y','za'}, dimensions={0} | all-to-all | bytes 589824 | tf_op jit(solution)/shard_map/all_to_all | solution.py:200
  136.4 0.8 far_sum.1
  (1 shorter events, 0.0 us)
Async XLA Ops:
  0.6 0.8 copy-start
  0.6 41.5 %copy-start.1 = (bf16[8,48,1536]{2,1,0:T(8,128)(2,1)S(1)}, bf16[8,48,1536]{2,1,0:T(8,128)(2,1)}, u32[]{:S(2)}) copy-start(bf16[8,48,1536]{2,1,0:T(8,128)(2,1)} %mine.3) | copy-start | bytes 3538948
  2.4 39.8 %all-to-all-start = ((bf16[32,48,256]{2,1,0:T(8,128)(2,1)}), bf16[32,48,256]{2,1,0:T(8,128)(2,1)S(1)}, u32[]{:S(2)}, u32[]{:S(2)}) async-start(bf16[32,48,256]{2,1,0:T(8,128)(2,1)} %broadcast_in_dim.9), calls=%async_computation | async-start | bytes 1572864 | tf_op jit(solution)/shard_map/all_to_all | solution.py:172
  18.3 5.0 %collective-permute-start = (bf16[8,48,1536]{2,1,0:T(8,128)(2,1)}, bf16[8,48,1536]{2,1,0:T(8,128)(2,1)S(1)}, u32[]{:S(2)}, u32[]{:S(2)}) collective-permute-start(bf16[8,48,1536]{2,1,0:T(8,128)(2,1)} %mine.3), channel_id=1, source_target_pairs={{0,32},{32,0},{1,33},{33,1},{2,34},{34,2},{3,35},{35,3},{4,36},{36... | collective-permute-start | bytes 3538952 | tf_op jit(solution)/shard_map/ppermute | solution.py:170
  74.7 4.3 %collective-permute-start.1 = (bf16[32,104,128]{2,1,0:T(8,128)(2,1)S(1)}, bf16[32,104,128]{2,1,0:T(8,128)(2,1)S(1)}, u32[]{:S(2)}, u32[]{:S(2)}) collective-permute-start(bf16[32,104,128]{2,1,0:T(8,128)(2,1)S(1)} %all_to_all.20), channel_id=1, source_target_pairs={{0,32},{32,0},{1,33},{33,1},{2,34},{34,2},{3,35},{35,3},{4,36},{36... | collective-permute-start | bytes 2555912 | tf_op jit(solution)/shard_map/ppermute | solution.py:184

commit v7 on v6

--- a/solution.py
+++ b/solution.py
@@ -13,6 +13,7 @@
 f32, bf16 = jnp.float32, jnp.bfloat16
 SMEM = pl.BlockSpec(memory_space=pltpu.SMEM)
 VMEM = pl.BlockSpec(memory_space=pltpu.VMEM)
+ANY = pl.BlockSpec(memory_space=pl.ANY)
 
 
 def words(value):
@@ -20,12 +21,12 @@
     return high, (value - high.astype(f32)).astype(bf16)
 
 
-def transform_kernel(place, full, mine, other, own, out):
+def transform_kernel(place, full, mine, other, coeffs, out):
     core = place[0]
     count, rows, nao = mine.shape
     wide = full.shape[1]
     half = wide // 2
-    weight = own[...].astype(f32)
+    weight = coeffs[core].astype(f32)
     lane = lax.broadcasted_iota(jnp.int32, (1, half), 1)
     terms = jnp.zeros((1, half), f32)
     for source, owner in ((mine, core), (other, 1 - core)):
@@ -50,10 +51,10 @@
                 out[y, zb, za, 2 * rows : 2 * rows + 8] = rider
 
 
-def exchange_kernel(place, got, got_other, mine, other, out, column_side, row_side):
+def exchange_kernel(place, got, got_other, out, column_side, row_side):
     core, zb = place[0], place[1]
-    count, rows, nao = mine.shape
     half = got.shape[4]
+    rows = got.shape[3] // 2 // 16 * 16
     wide = 2 * half
     own_sign = jnp.where(core == 0, 1.0, -1.0).astype(bf16)
     other_sign = jnp.where(core == 0, -1.0, 1.0).astype(bf16)
@@ -75,6 +76,22 @@
                 column_side[at, own_at] = other_part * other_sign
                 column_side[at, other_at] = own * own_sign
 
+    for n in range(3):
+        block = lax.dot_general(
+            column_side[...],
+            row_side[n * 256 : (n + 1) * 256],
+            (((1,), (1,)), ((), ())),
+            preferred_element_type=f32,
+        ).astype(bf16)
+        for s in range(8):
+            out[s, 0 : 4 * rows, n * 256 : (n + 1) * 256] = block[s * 4 * rows : (s + 1) * 4 * rows]
+
+
+def coulomb_kernel(place, got, got_other, mine, other, after, out):
+    del after
+    core = place[0]
+    count, rows, nao = mine.shape
+    half = got.shape[4]
     riders = jnp.zeros((8, half), f32)
     for y in range(8):
         for b in range(2):
@@ -95,38 +112,16 @@
             total += weight * source[p, at].astype(f32)
         for s in range(8):
             start = s * 4 * rows
-            piece = jnp.where(
+            out[s, at] = jnp.where(
                 core == 0, total[:, start : start + 2 * rows], total[:, start + 2 * rows : start + 4 * rows]
             )
-            high, low = words(piece)
-            gap = jnp.zeros((16, half - 2 * rows), bf16)
-            out[s, 4 * rows : 4 * rows + 16, part * 256 : (part + 1) * 256] = jnp.concatenate(
-                [high, gap, low, gap], axis=1
-            )
-
-    for n in range(3):
-        block = lax.dot_general(
-            column_side[...],
-            row_side[n * 256 : (n + 1) * 256],
-            (((1,), (1,)), ((), ())),
-            preferred_element_type=f32,
-        ).astype(bf16)
-        for s in range(8):
-            out[s, 0 : 4 * rows, n * 256 : (n + 1) * 256] = block[s * 4 * rows : (s + 1) * 4 * rows]
-
-
-def near_sum_kernel(parts, out, coulomb):
-    rows = coulomb.shape[0]
-    deep = 4 * rows
-    tail = jnp.sum(parts[:, deep : deep + 16].astype(f32), axis=0)
-    for part in range(3):
-        start = part * 256
-        coulomb[part * 16 : (part + 1) * 16] = (
-            tail[:, start : start + 2 * rows] + tail[:, start + 128 : start + 128 + 2 * rows]
-        )
+
+
+def near_sum_kernel(parts, out):
+    rows = parts.shape[1] // 4
     for n in range(2):
         columns = slice(n * 8 * rows, (n + 1) * 8 * rows)
-        turned = jnp.sum(parts[:, 0:deep, columns].astype(f32), axis=0).T
+        turned = jnp.sum(parts[:, :, columns].astype(f32), axis=0).T
         for j in range(8):
             block = turned[j * rows : (j + 1) * rows]
             rest = jnp.concatenate([block[: rows // 2, 128:], block[rows // 2 :, 128:]], axis=1)
@@ -142,8 +137,8 @@
     out[1] = jnp.concatenate([total[:rows, 2 * rows :], rest], axis=1)
 
 
-def call(kernel, name, grant, outs, inputs, place=None, scratch=()):
-    specs = [VMEM] * len(inputs)
+def call(kernel, name, grant, outs, inputs, place=None, scratch=(), specs=None):
+    specs = specs or [VMEM] * len(inputs)
     if place is not None:
         specs, inputs = [SMEM] + specs, (place,) + inputs
     return pl.pallas_call(
@@ -157,6 +152,20 @@
     )(*inputs)
 
 
+def near_sum(terms):
+    x = lax.axis_index("x")
+    zl = lax.axis_index("zl")
+
+    def pick(block, index, axis):
+        return lax.dynamic_index_in_dim(block, index, axis, keepdims=False)
+
+    for step, axis in ((1, 2), (2, 1)):
+        bit = x // step % 2
+        sent = lax.ppermute(pick(terms, 1 - bit, axis), "x", [(i, i ^ step) for i in range(4)])
+        terms = pick(terms, bit, axis) + sent
+    return pick(terms, zl, 0) + lax.ppermute(pick(terms, 1 - zl, 0), "zl", SWAP)
+
+
 def on_device(vectors, coeffs):
     core = lax.axis_index("core")
     zb = lax.axis_index("zb")
@@ -165,11 +174,10 @@
     wide = coeffs.shape[2]
     half = wide // 2
     tall = 2 * rows + 8
-    deep = 4 * rows + 16
 
     other_vectors = lax.ppermute(vectors, "core", SWAP)
-    own = lax.dynamic_index_in_dim(coeffs, core, 0, keepdims=False)
-    full = lax.all_to_all(jnp.broadcast_to(own[None], (32, rows, wide)), FAR, 0, 0, tiled=True).reshape(nao, wide)
+    spread = jnp.broadcast_to(lax.dynamic_index_in_dim(coeffs, core, 0), (32, rows, wide))
+    full = lax.all_to_all(spread, FAR, 0, 0, tiled=True).reshape(nao, wide)
 
     shape = (8, 2, 2, tall, half)
     (pieces,) = call(
@@ -177,7 +185,7 @@
         "half_transform",
         16,
         [(shape, bf16)],
-        (full, vectors, other_vectors, own),
+        (full, vectors, other_vectors, coeffs),
         place,
     )
     got = lax.all_to_all(pieces.reshape(32, tall, half), FAR, 0, 0, tiled=True)
@@ -188,15 +196,23 @@
         exchange_kernel,
         "exchange_quarter",
         24,
-        [((8, deep, 16 * rows), bf16)],
-        (got.reshape(shape), got_other.reshape(shape), vectors, other_vectors),
+        [((8, 4 * rows, 16 * rows), bf16)],
+        (got.reshape(shape), got_other.reshape(shape)),
         place,
         scratch,
     )
+    (terms,) = call(
+        coulomb_kernel,
+        "coulomb",
+        12,
+        [((8, rows, 2 * rows), f32)],
+        (got.reshape(shape), got_other.reshape(shape), vectors, other_vectors, parts),
+        place,
+        specs=[VMEM] * 4 + [ANY],
+    )
+    coulomb = near_sum(terms.reshape(2, 2, 2, rows, 2 * rows))
     parts = lax.all_to_all(parts, NEAR, 0, 0, tiled=True)
-    packed, coulomb = call(
-        near_sum_kernel, "near_sum", 12, [((16, rows + rows // 2, 128), bf16), ((rows, 2 * rows), f32)], (parts,)
-    )
+    (packed,) = call(near_sum_kernel, "near_sum", 12, [((16, rows + rows // 2, 128), bf16)], (parts,))
     packed = lax.all_to_all(packed, SUMS, 0, 0, tiled=True)
     (exchange,) = call(far_sum_kernel, "far_sum", 4, [((2, rows, 2 * rows), f32)], (packed,))
     return exchange, coulomb

time: 138 us -> 145 us (1.051); the launches traced: 137 us -> 142 us
  blocking collectives: 85 us -> 31.1 us
  waiting for transfers between devices: 24.2 us -> 53.9 us
  starting transfers between devices: 19.8 us -> 41.1 us
  local copies, waits for them, and re-layouts: 1.73 us -> 6.43 us
  Pallas kernels: 5.64 us -> 8.11 us
    all_to_all x2 -> x0, blocking collectives: 54 us -> none  [the longest x1 35.2 us: on_device(): parts = lax.all_to_all(parts, NEAR, 0, 0, tiled=True)]
    ppermute x0 -> x3, waiting for transfers between devices: none -> 23.2 us  [the longest x2 21.2 us: near_sum(): lax.ppermute(pick(terms, 1 - bit, axis), 'x', [(i, i ^ step) for i in ran...]
    all_to_all x1 -> x3, starting transfers between devices: 16 us -> 28.1 us  [the longest x1 16 us: on_device(): full = lax.all_to_all(spread, FAR, 0, 0, tiled=True).reshape(nao, wide)]
    ppermute x0 -> x3, starting transfers between devices: none -> 9.21 us  [the longest x2 5.56 us: near_sum(): lax.ppermute(pick(terms, 1 - bit, axis), 'x', [(i, i ^ step) for i in ran...]
    all_to_all x1 -> x3, waiting for transfers between devices: 18.9 us -> 25.6 us  [the longest x1 19.1 us: on_device(): full = lax.all_to_all(spread, FAR, 0, 0, tiled=True).reshape(nao, wide)]
    unnamed x4 -> x14, local copies, waits for them, and re-layouts: 0.79 us -> 4.6 us
    pallas_call x4 -> x5, Pallas kernels: 5.64 us -> 8.11 us  [call(): pl.pallas_call(kernel, out_shape=[jax.ShapeDtypeStruct(shape, dtype) for...]
  transfers between devices with their start and end apart: 3 -> 8, of which waited for: 3 -> 6; matrix products, arithmetic and copies ran while one was open for 0% -> 1% of each run, Pallas kernels for 0% -> 2%
where the time goes in v7:
time: 145 us; the launch traced here: 142 us
  waiting for transfers between devices  53.9 us (37%)
  starting transfers between devices  41.1 us (28%)
  blocking collectives  31.1 us (21%)
  Pallas kernels  8.11 us (6%)
  local copies, waits for them, and re-layouts  6.43 us (4%)
    all_to_all x1, blocking collectives, on_device(): got = lax.all_to_all(pieces.reshape(32, tall, half), FAR, 0, 0, tiled=True)  31.1 us
    ppermute x2, waiting for transfers between devices, near_sum(): lax.ppermute(pick(terms, 1 - bit, axis), 'x', [(i, i ^ step) for i in ran...  21.2 us
    all_to_all x1, waiting for transfers between devices, on_device(): full = lax.all_to_all(spread, FAR, 0, 0, tiled=True).reshape(nao, wide)  19.1 us
    all_to_all x1, starting transfers between devices, on_device(): full = lax.all_to_all(spread, FAR, 0, 0, tiled=True).reshape(nao, wide)  16 us
    pallas_call x5, Pallas kernels, call(): pl.pallas_call(kernel, out_shape=[jax.ShapeDtypeStruct(shape, dtype) for...  8.11 us
    all_to_all x1, starting transfers between devices, on_device(): packed = lax.all_to_all(packed, SUMS, 0, 0, tiled=True)  6.54 us
    all_to_all x1, waiting for transfers between devices, on_device(): packed = lax.all_to_all(packed, SUMS, 0, 0, tiled=True)  6.51 us
    ppermute x2, starting transfers between devices, near_sum(): lax.ppermute(pick(terms, 1 - bit, axis), 'x', [(i, i ^ step) for i in ran...  5.56 us
  transfers between devices with their start and end apart: 8, of which 6 were waited for; matrix products, arithmetic and copies ran while one was open for 1% of the time, Pallas kernels for 2%

profile of v7, /device:TPU:6, one launch (start us, length us, event | category | flops | bytes accessed | tf_op | source)
XLA Modules:
  0.0 142.2 jit_solution(7874899042021263664)
XLA Ops:
  0.6 0.0 copy-start.6
  0.6 0.0 copy-start
  0.7 0.8 dynamic-slice_bitcast_fusion.3
  1.5 0.9 broadcast_in_dim.8
  2.4 16.0 %all-to-all-start = ((bf16[32,48,256]{2,1,0:T(8,128)(2,1)}), bf16[32,48,256]{2,1,0:T(8,128)(2,1)S(1)}, u32[]{:S(2)}, u32[]{:S(2)}) async-start(bf16[32,48,256]{2,1,0:T(8,128)(2,1)} %broadcast_in_dim.8), calls=%async_computation | async-start | bytes 1572864 | tf_op jit(solution)/shard_map/all_to_all | solution.py:180
  18.4 0.0 copy-done
  18.4 1.9 %collective-permute-start = (bf16[8,48,1536]{2,1,0:T(8,128)(2,1)S(1)}, bf16[8,48,1536]{2,1,0:T(8,128)(2,1)S(1)}, u32[]{:S(2)}, u32[]{:S(2)}) collective-permute-start(bf16[8,48,1536]{2,1,0:T(8,128)(2,1)S(1)} %copy-done), channel_id=1, source_target_pairs={{0,32},{32,0},{1,33},{33,1},{2,34},{34,2},{3,35},{35,3},{4,36},{36... | collective-permute-start | bytes 3538952 | tf_op jit(solution)/shard_map/ppermute | solution.py:178
  20.4 0.1 pad_add_fusion.place
  20.4 2.7 %collective-permute-done.other = bf16[8,48,1536]{2,1,0:T(8,128)(2,1)S(1)} collective-permute-done((bf16[8,48,1536]{2,1,0:T(8,128)(2,1)S(1)}, bf16[8,48,1536]{2,1,0:T(8,128)(2,1)S(1)}, u32[]{:S(2)}, u32[]{:S(2)}) %collective-permute-start) | collective-permute-done | bytes 1179680 | tf_op jit(solution)/shard_map/ppermute | solution.py:178
  23.2 0.0 copy-start.2
  23.2 19.1 %all-to-all-done = bf16[32,48,256]{2,1,0:T(8,128)(2,1)S(1)} async-done(((bf16[32,48,256]{2,1,0:T(8,128)(2,1)}), bf16[32,48,256]{2,1,0:T(8,128)(2,1)S(1)}, u32[]{:S(2)}, u32[]{:S(2)}) %all-to-all-start) | async-done | bytes 786464 | tf_op jit(solution)/shard_map/all_to_all | solution.py:180
  42.2 0.0 copy-done.6
  42.2 1.4 %half_transform.1 = bf16[8,2,2,104,128]{4,3,2,1,0:T(8,128)(2,1)S(1)} custom-call(s32[2]{0:T(128)S(1)} %pad_add_fusion.place, bf16[1536,256]{1,0:T(8,128)(2,1)S(1)} %bitcast.26, bf16[8,48,1536]{2,1,0:T(8,128)(2,1)S(1)} %copy-done, bf16[8,48,1536]{2,1,0:T(8,128)(2,1)S(1)} %collective-permute-done.other, bf16[2,48,256]{2,1,0:T(8,128)(2,1)S(1)} %copy-done.6), custom_call_target="tpu_custom_call" | custom-call | tf_op jit(solution)/shard_map/half_transform/pallas_call | solution.py:144
  43.7 31.1 %all_to_all.20 = bf16[32,104,128]{2,1,0:T(8,128)(2,1)S(1)} all-to-all(bf16[32,104,128]{2,1,0:T(8,128)(2,1)S(1)} %bitcast.25), channel_id=1, replica_groups=mesh['zl'=2,'x'=4,'core'=2,'y'=8,'zb'=2,'za'=2] {'y','zb','za'}, dimensions={0} | all-to-all | bytes 1703936 | tf_op jit(solution)/shard_map/all_to_all | solution.py:191
  74.8 0.0 copy-done.2
  74.8 1.9 %collective-permute-start.1 = (bf16[32,104,128]{2,1,0:T(8,128)(2,1)S(1)}, bf16[32,104,128]{2,1,0:T(8,128)(2,1)S(1)}, u32[]{:S(2)}, u32[]{:S(2)}) collective-permute-start(bf16[32,104,128]{2,1,0:T(8,128)(2,1)S(1)} %all_to_all.20), channel_id=1, source_target_pairs={{0,32},{32,0},{1,33},{33,1},{2,34},{34,2},{3,35},{35,3},{4,36},{36... | collective-permute-start | bytes 2555912 | tf_op jit(solution)/shard_map/ppermute | solution.py:192
  76.7 2.3 %collective-permute-done.1 = bf16[32,104,128]{2,1,0:T(8,128)(2,1)S(1)} collective-permute-done((bf16[32,104,128]{2,1,0:T(8,128)(2,1)S(1)}, bf16[32,104,128]{2,1,0:T(8,128)(2,1)S(1)}, u32[]{:S(2)}, u32[]{:S(2)}) %collective-permute-start.1) | collective-permute-done | bytes 852000 | tf_op jit(solution)/shard_map/ppermute | solution.py:192
  79.0 3.5 %exchange_quarter.1.after = bf16[8,192,768]{2,1,0:T(8,128)(2,1)} custom-call(s32[2]{0:T(128)S(1)} %pad_add_fusion.place, bf16[8,2,2,104,128]{4,3,2,1,0:T(8,128)(2,1)S(1)} %bitcast.21, bf16[8,2,2,104,128]{4,3,2,1,0:T(8,128)(2,1)S(1)} %bitcast.23), custom_call_target="tpu_custom_call" | custom-call | tf_op jit(solution)/shard_map/exchange_quarter/pallas_call | solution.py:144
  82.5 0.0 copy-start.4
  82.5 0.9 copy-done.4
  83.4 5.6 %all-to-all-start.2 = ((bf16[8,192,768]{2,1,0:T(8,128)(2,1)}), bf16[8,192,768]{2,1,0:T(8,128)(2,1)S(1)}, u32[]{:S(2)}, u32[]{:S(2)}) async-start(bf16[8,192,768]{2,1,0:T(8,128)(2,1)} %exchange_quarter.1.after), calls=%async_computation.2 | async-start | bytes 4718592 | tf_op jit(solution)/shard_map/all_to_all | solution.py:214
  89.0 0.0 copy-start.1
  89.0 1.3 copy-done.1
  90.3 0.0 copy-start.3
  90.3 1.3 copy-done.3
  91.5 0.0 copy-start.5
  91.5 1.2 copy-done.5
  92.7 1.3 coulomb.1
  94.0 2.8 %collective-permute-start.2 = (f32[2,2,48,96]{3,2,1,0:T(8,128)S(1)}, f32[2,2,48,96]{3,2,1,0:T(8,128)S(1)}, u32[]{:S(2)}, u32[]{:S(2)}) collective-permute-start(f32[2,2,48,96]{3,2,1,0:T(8,128)S(1)} %dynamic-slice_bitcast_fusion), channel_id=1, source_target_pairs={{0,64},{64,0},{128,192},{192,128},{1,65},{65,1},{129,193},{193,129... | collective-permute-start | bytes 221192 | tf_op jit(solution)/shard_map/ppermute | solution.py:164
  96.8 21.2 %collective-permute-done.2 = f32[2,2,48,96]{3,2,1,0:T(8,128)S(1)} collective-permute-done((f32[2,2,48,96]{3,2,1,0:T(8,128)S(1)}, f32[2,2,48,96]{3,2,1,0:T(8,128)S(1)}, u32[]{:S(2)}, u32[]{:S(2)}) %collective-permute-start.2) | collective-permute-done | bytes 73760 | tf_op jit(solution)/shard_map/ppermute | solution.py:164
  118.0 2.8 %collective-permute-start.3 = (f32[2,48,96]{2,1,0:T(8,128)S(1)}, f32[2,48,96]{2,1,0:T(8,128)S(1)}, u32[]{:S(2)}, u32[]{:S(2)}) collective-permute-start(f32[2,48,96]{2,1,0:T(8,128)S(1)} %dynamic-slice_bitcast_fusion.1), channel_id=1, source_target_pairs={{0,128},{64,192},{128,0},{192,64},{1,129},{65,193},{129,1},{193,65... | collective-permute-start | bytes 110600 | tf_op jit(solution)/shard_map/ppermute | solution.py:164
  120.8 0.0 all-to-all-done.2.parts
  120.8 1.1 near_sum.1
  122.0 6.5 %all-to-all-start.3 = ((bf16[16,72,128]{2,1,0:T(8,128)(2,1)}), bf16[16,72,128]{2,1,0:T(8,128)(2,1)S(1)}, u32[]{:S(2)}, u32[]{:S(2)}) async-start(bf16[16,72,128]{2,1,0:T(8,128)(2,1)} %near_sum.1), calls=%async_computation.3 | async-start | bytes 589824 | tf_op jit(solution)/shard_map/all_to_all | solution.py:216
  128.5 0.0 collective-permute-done.3
  128.6 3.7 %collective-permute-start.4 = (f32[48,96]{1,0:T(8,128)S(1)}, f32[48,96]{1,0:T(8,128)S(1)}, u32[]{:S(2)}, u32[]{:S(2)}) collective-permute-start(f32[48,96]{1,0:T(8,128)S(1)} %dynamic-slice_bitcast_fusion.2), channel_id=1, source_target_pairs={{0,256},{256,0},{1,257},{257,1},{2,258},{258,2},{3,259},{259,3},{4... | collective-permute-start | bytes 55304 | tf_op jit(solution)/shard_map/ppermute | solution.py:166
  132.2 2.1 %collective-permute-done.4 = f32[48,96]{1,0:T(8,128)S(1)} collective-permute-done((f32[48,96]{1,0:T(8,128)S(1)}, f32[48,96]{1,0:T(8,128)S(1)}, u32[]{:S(2)}, u32[]{:S(2)}) %collective-permute-start.4) | collective-permute-done | bytes 18464 | tf_op jit(solution)/shard_map/ppermute | solution.py:166
  134.3 0.6 bitcast_add_fusion.2
  134.9 6.5 %all-to-all-done.3.parts = bf16[16,72,128]{2,1,0:T(8,128)(2,1)S(1)} async-done(((bf16[16,72,128]{2,1,0:T(8,128)(2,1)}), bf16[16,72,128]{2,1,0:T(8,128)(2,1)S(1)}, u32[]{:S(2)}, u32[]{:S(2)}) %all-to-all-start.3) | async-done | bytes 294944 | tf_op jit(solution)/shard_map/all_to_all | solution.py:216
  141.4 0.8 far_sum.1
  (5 shorter events, 0.1 us)
Async XLA Ops:
  0.6 41.6 %copy-start.6 = (bf16[2,48,256]{2,1,0:T(8,128)(2,1)S(1)}, bf16[2,48,256]{2,1,0:T(8,128)(2,1)}, u32[]{:S(2)}) copy-start(bf16[2,48,256]{2,1,0:T(8,128)(2,1)} %coeffs.1) | copy-start | bytes 147460
  0.6 17.8 %copy-start = (bf16[8,48,1536]{2,1,0:T(8,128)(2,1)S(1)}, bf16[8,48,1536]{2,1,0:T(8,128)(2,1)}, u32[]{:S(2)}) copy-start(bf16[8,48,1536]{2,1,0:T(8,128)(2,1)} %mine.3) | copy-start | bytes 3538948
  2.4 39.8 %all-to-all-start = ((bf16[32,48,256]{2,1,0:T(8,128)(2,1)}), bf16[32,48,256]{2,1,0:T(8,128)(2,1)S(1)}, u32[]{:S(2)}, u32[]{:S(2)}) async-start(bf16[32,48,256]{2,1,0:T(8,128)(2,1)} %broadcast_in_dim.8), calls=%async_computation | async-start | bytes 1572864 | tf_op jit(solution)/shard_map/all_to_all | solution.py:180
  18.4 4.7 %collective-permute-start = (bf16[8,48,1536]{2,1,0:T(8,128)(2,1)S(1)}, bf16[8,48,1536]{2,1,0:T(8,128)(2,1)S(1)}, u32[]{:S(2)}, u32[]{:S(2)}) collective-permute-start(bf16[8,48,1536]{2,1,0:T(8,128)(2,1)S(1)} %copy-done), channel_id=1, source_target_pairs={{0,32},{32,0},{1,33},{33,1},{2,34},{34,2},{3,35},{35,3},{4,36},{36... | collective-permute-start | bytes 3538952 | tf_op jit(solution)/shard_map/ppermute | solution.py:178
  23.2 51.6 %copy-start.2 = (bf16[8,48,1536]{2,1,0:T(8,128)(2,1)}, bf16[8,48,1536]{2,1,0:T(8,128)(2,1)S(1)}, u32[]{:S(2)}) copy-start(bf16[8,48,1536]{2,1,0:T(8,128)(2,1)S(1)} %collective-permute-done.other) | copy-start | bytes 3538948
  74.8 4.3 %collective-permute-start.1 = (bf16[32,104,128]{2,1,0:T(8,128)(2,1)S(1)}, bf16[32,104,128]{2,1,0:T(8,128)(2,1)S(1)}, u32[]{:S(2)}, u32[]{:S(2)}) collective-permute-start(bf16[32,104,128]{2,1,0:T(8,128)(2,1)S(1)} %all_to_all.20), channel_id=1, source_target_pairs={{0,32},{32,0},{1,33},{33,1},{2,34},{34,2},{3,35},{35,3},{4,36},{36... | collective-permute-start | bytes 2555912 | tf_op jit(solution)/shard_map/ppermute | solution.py:192
  82.5 0.9 copy-start.4
  83.4 37.4 %all-to-all-start.2 = ((bf16[8,192,768]{2,1,0:T(8,128)(2,1)}), bf16[8,192,768]{2,1,0:T(8,128)(2,1)S(1)}, u32[]{:S(2)}, u32[]{:S(2)}) async-start(bf16[8,192,768]{2,1,0:T(8,128)(2,1)} %exchange_quarter.1.after), calls=%async_computation.2 | async-start | bytes 4718592 | tf_op jit(solution)/shard_map/all_to_all | solution.py:214
  89.0 1.3 copy-start.1
  90.3 1.3 copy-start.3
  91.5 1.2 copy-start.5
  94.0 24.0 %collective-permute-start.2 = (f32[2,2,48,96]{3,2,1,0:T(8,128)S(1)}, f32[2,2,48,96]{3,2,1,0:T(8,128)S(1)}, u32[]{:S(2)}, u32[]{:S(2)}) collective-permute-start(f32[2,2,48,96]{3,2,1,0:T(8,128)S(1)} %dynamic-slice_bitcast_fusion), channel_id=1, source_target_pairs={{0,64},{64,0},{128,192},{192,128},{1,65},{65,1},{129,193},{193,129... | collective-permute-start | bytes 221192 | tf_op jit(solution)/shard_map/ppermute | solution.py:164
  118.0 10.5 %collective-permute-start.3 = (f32[2,48,96]{2,1,0:T(8,128)S(1)}, f32[2,48,96]{2,1,0:T(8,128)S(1)}, u32[]{:S(2)}, u32[]{:S(2)}) collective-permute-start(f32[2,48,96]{2,1,0:T(8,128)S(1)} %dynamic-slice_bitcast_fusion.1), channel_id=1, source_target_pairs={{0,128},{64,192},{128,0},{192,64},{1,129},{65,193},{129,1},{193,65... | collective-permute-start | bytes 110600 | tf_op jit(solution)/shard_map/ppermute | solution.py:164
  122.0 19.4 %all-to-all-start.3 = ((bf16[16,72,128]{2,1,0:T(8,128)(2,1)}), bf16[16,72,128]{2,1,0:T(8,128)(2,1)S(1)}, u32[]{:S(2)}, u32[]{:S(2)}) async-start(bf16[16,72,128]{2,1,0:T(8,128)(2,1)} %near_sum.1), calls=%async_computation.3 | async-start | bytes 589824 | tf_op jit(solution)/shard_map/all_to_all | solution.py:216
  128.6 5.7 %collective-permute-start.4 = (f32[48,96]{1,0:T(8,128)S(1)}, f32[48,96]{1,0:T(8,128)S(1)}, u32[]{:S(2)}, u32[]{:S(2)}) collective-permute-start(f32[48,96]{1,0:T(8,128)S(1)} %dynamic-slice_bitcast_fusion.2), channel_id=1, source_target_pairs={{0,256},{256,0},{1,257},{257,1},{2,258},{258,2},{3,259},{259,3},{4... | collective-permute-start | bytes 55304 | tf_op jit(solution)/shard_map/ppermute | solution.py:166

commit v8 on v6

v8 whole, which is shorter than its diff:
```python
import jax
import jax.numpy as jnp
from jax import lax
from jax.experimental import pallas as pl
from jax.experimental.pallas import tpu as pltpu
from jax.sharding import Mesh
from jax.sharding import PartitionSpec as P

NEAR = ("zl", "x")
FAR = ("y", "zb", "za")
SUMS = ("y",)
SWAP = [(0, 1), (1, 0)]
f32, bf16 = jnp.float32, jnp.bfloat16
SMEM = pl.BlockSpec(memory_space=pltpu.SMEM)
VMEM = pl.BlockSpec(memory_space=pltpu.VMEM)


def words(value):
    high = value.astype(bf16)
    return high, (value - high.astype(f32)).astype(bf16)


def coulomb_place(word):
    return word // 3 * 16, word % 3 * 128


def transform_kernel(place, full, mine, other, own, out):
    core = place[0]
    count, rows, nao = mine.shape
    wide = full.shape[1]
    half = wide // 2
    weight = own[...].astype(f32)
    lane = lax.broadcasted_iota(jnp.int32, (1, half), 1)
    terms = jnp.zeros((1, half), f32)
    for source, owner in ((mine, core), (other, 1 - core)):
        slab = jnp.dot(
            source[...].reshape(count * rows, nao), full[...], preferred_element_type=f32
        ).astype(bf16)
        for p in range(count):
            block = slab[p * rows : (p + 1) * rows]
            for z in range(4):
                for h in range(2):
                    at = pl.ds((p % 2 * 2 + h) * rows, rows)
                    out[owner * (count // 2) + p // 2, z, at] = block[:, h * half : (h + 1) * half]
            term = jnp.sum(block.astype(f32) * weight, axis=0, keepdims=True)
            term = jnp.sum(term, axis=1, keepdims=True)
            terms += jnp.where(lane == owner * count + p, term, 0.0)
    high, low = words(terms)
    lines = lax.broadcasted_iota(jnp.int32, (8, half), 0)
    rider = jnp.where(lines == 0, high.astype(f32), jnp.where(lines == 1, low.astype(f32), 0.0))
    rider = rider.astype(bf16)
    for y in range(8):
        for z in range(4):
            out[y, z, 4 * rows : 4 * rows + 8] = rider


def exchange_kernel(place, got, got_other, mine, other, out, column_side, row_side):
    core, z = place[0], place[1]
    count, rows, nao = mine.shape
    half = got.shape[3]
    wide = 4 * half
    own_sign = jnp.where(core == 0, 1.0, -1.0).astype(bf16)
    other_sign = jnp.where(core == 0, -1.0, 1.0).astype(bf16)
    for y in range(8):
        for h in range(4):
            own_at = slice(h * half, (h + 1) * half)
            other_at = slice(wide + h * half, wide + (h + 1) * half)
            part = slice(h * rows, (h + 1) * rows)
            at = pl.ds(y * rows, rows)
            row_side[at, own_at] = got[y, z, part]
            row_side[at, other_at] = got_other[y, z, part]
            for za in range(2):
                own = got[y, 2 * core + za, part]
                other_part = got_other[y, 2 * core + za, part]
                at = pl.ds((4 * y + za) * rows, rows)
                column_side[at, own_at] = own
                column_side[at, other_at] = other_part
                at = pl.ds((4 * y + 2 + za) * rows, rows)
                column_side[at, own_at] = other_part * other_sign
                column_side[at, other_at] = own * own_sign

    riders = jnp.zeros((8, half), f32)
    for y in range(8):
        for b in range(4):
            for source in (got, got_other):
                riders += source[y, b, 4 * rows : 4 * rows + 8].astype(f32)
    weights = riders[0:1] + riders[1:2]
    lane = lax.broadcasted_iota(jnp.int32, (1, half), 1)
    weighted = []
    for source, owner in ((mine, core), (other, 1 - core)):
        for p in range(count):
            weight = jnp.sum(jnp.where(lane == owner * count + p, weights, 0.0), axis=1, keepdims=True)
            weighted.append((source, p, weight))
    for part in range(3):
        at = pl.ds(part * 16, 16)
        total = jnp.zeros((16, nao), f32)
        for source, p, weight in weighted:
            total += weight * source[p, at].astype(f32)
        for s in range(8):
            start = s * 4 * rows
            piece = jnp.where(
                core == 0, total[:, start : start + 2 * rows], total[:, start + 2 * rows : start + 4 * rows]
            )
            high, low = words(piece)
            gap = jnp.zeros((16, half - 2 * rows), bf16)
            for k, word in enumerate((high, low)):
                row, column = coulomb_place(2 * part + k)
                at_row = pl.ds(4 * rows + row, 16)
                out[s, at_row, column : column + half] = jnp.concatenate([word, gap], axis=1)

    for n in range(2):
        m = slice(n * 16 * rows, (n + 1) * 16 * rows)
        block = lax.dot_general(
            column_side[m], row_side[...], (((1,), (1,)), ((), ())), preferred_element_type=f32
        ).astype(bf16)
        for s in range(4):
            out[n * 4 + s, 0 : 4 * rows] = block[s * 4 * rows : (s + 1) * 4 * rows]


def near_sum_kernel(parts, out, coulomb):
    rows = coulomb.shape[0]
    deep = 4 * rows
    tail = jnp.sum(parts[:, deep : deep + 32].astype(f32), axis=0)
    for part in range(3):
        total = jnp.zeros((16, 2 * rows), f32)
        for k in range(2):
            row, column = coulomb_place(2 * part + k)
            total += tail[row : row + 16, column : column + 2 * rows]
        coulomb[part * 16 : (part + 1) * 16] = total
    turned = jnp.sum(parts[:, 0:deep].astype(f32), axis=0).T
    for j in range(8):
        block = turned[j * rows : (j + 1) * rows]
        rest = jnp.concatenate([block[: rows // 2, 128:], block[rows // 2 :, 128:]], axis=1)
        out[j, 0:rows] = block[:, :128].astype(bf16)
        out[j, rows : rows + rows // 2] = rest.astype(bf16)


def far_sum_kernel(parts, out):
    rows = out.shape[1]
    total = jnp.sum(parts[...].astype(f32), axis=0)
    rest = jnp.concatenate([total[rows:, :64], total[rows:, 64:]], axis=0)
    out[0] = total[:rows, : 2 * rows]
    out[1] = jnp.concatenate([total[:rows, 2 * rows :], rest], axis=1)


def call(kernel, name, grant, outs, inputs, place=None, scratch=()):
    specs = [VMEM] * len(inputs)
    if place is not None:
        specs, inputs = [SMEM] + specs, (place,) + inputs
    return pl.pallas_call(
        kernel,
        out_shape=[jax.ShapeDtypeStruct(shape, dtype) for shape, dtype in outs],
        in_specs=specs,
        out_specs=[VMEM] * len(outs),
        scratch_shapes=scratch,
        compiler_params=pltpu.CompilerParams(vmem_limit_bytes=grant * 2**20),
        name=name,
    )(*inputs)


def on_device(vectors, coeffs):
    core = lax.axis_index("core")
    z = lax.axis_index("zb") * 2 + lax.axis_index("za")
    place = jnp.stack([core, z]).astype(jnp.int32)
    count, rows, nao = vectors.shape
    wide = coeffs.shape[2]
    half = wide // 2
    tall = 4 * rows + 8
    deep = 4 * rows + 32

    other_vectors = lax.ppermute(vectors, "core", SWAP)
    own = lax.dynamic_index_in_dim(coeffs, core, 0, keepdims=False)
    full = lax.all_to_all(jnp.broadcast_to(own[None], (32, rows, wide)), FAR, 0, 0, tiled=True).reshape(nao, wide)

    shape = (8, 4, tall, half)
    (pieces,) = call(
        transform_kernel,
        "half_transform",
        16,
        [(shape, bf16)],
        (full, vectors, other_vectors, own),
        place,
    )
    got = lax.all_to_all(pieces.reshape(32, tall, half), FAR, 0, 0, tiled=True)
    got_other = lax.ppermute(got, "core", SWAP)

    scratch = [pltpu.VMEM((32 * rows, 4 * wide), bf16), pltpu.VMEM((8 * rows, 4 * wide), bf16)]
    (parts,) = call(
        exchange_kernel,
        "exchange_part",
        28,
        [((8, deep, 8 * rows), bf16)],
        (got.reshape(shape), got_other.reshape(shape), vectors, other_vectors),
        place,
        scratch,
    )
    parts = lax.all_to_all(parts, NEAR, 0, 0, tiled=True)
    packed, coulomb = call(
        near_sum_kernel, "near_sum", 12, [((8, rows + rows // 2, 128), bf16), ((rows, 2 * rows), f32)], (parts,)
    )
    packed = lax.all_to_all(packed, SUMS, 0, 0, tiled=True)
    (exchange,) = call(far_sum_kernel, "far_sum", 4, [((2, rows, 2 * rows), f32)], (packed,))
    return exchange, coulomb


def solution(mesh):
    fine = Mesh(mesh.devices.reshape(2, 4, 2, 8, 2, 2), ("zl", "x", "core", "y", "zb", "za"))
    chol = ("zl", "x", "core")
    return jax.shard_map(
        on_device,
        mesh=fine,
        in_specs=(P(chol, FAR, None), P(None, FAR, None)),
        out_specs=(P(None, FAR, chol), P(FAR, chol)),
        check_vma=False,
    )
```

time: 138 us -> 139 us (level)
    all_to_all x1, blocking collectives: 31.1 us -> 48.4 us  [on_device(): got = lax.all_to_all(pieces.reshape(32, tall, half), FAR, 0, 0, tiled=True)]
    all_to_all x1, blocking collectives: 35.2 us -> 22.6 us  [on_device(): parts = lax.all_to_all(parts, NEAR, 0, 0, tiled=True)]
    all_to_all x1, blocking collectives: 18.8 us -> 13.6 us  [on_device(): packed = lax.all_to_all(packed, SUMS, 0, 0, tiled=True)]
where the time goes in v8:
time: 139 us; the launch traced here: 138 us
  blocking collectives  84.5 us (61%)
  waiting for transfers between devices  25.3 us (18%)
  starting transfers between devices  19.8 us (14%)
  Pallas kernels  5.96 us (4%)
  local copies, waits for them, and re-layouts  1.73 us (1%)
    all_to_all x1, blocking collectives, on_device(): got = lax.all_to_all(pieces.reshape(32, tall, half), FAR, 0, 0, tiled=True)  48.4 us
    all_to_all x1, blocking collectives, on_device(): parts = lax.all_to_all(parts, NEAR, 0, 0, tiled=True)  22.6 us
    all_to_all x1, waiting for transfers between devices, on_device(): lax.all_to_all(jnp.broadcast_to(own[None], (32, rows, wide)), FAR, 0, 0,...  19.1 us
    all_to_all x1, starting transfers between devices, on_device(): lax.all_to_all(jnp.broadcast_to(own[None], (32, rows, wide)), FAR, 0, 0,...  16 us
    all_to_all x1, blocking collectives, on_device(): packed = lax.all_to_all(packed, SUMS, 0, 0, tiled=True)  13.6 us
    pallas_call x4, Pallas kernels, call(): pl.pallas_call(kernel, out_shape=[jax.ShapeDtypeStruct(shape, dtype) for...  5.96 us
    ppermute x1, waiting for transfers between devices, on_device(): got_other = lax.ppermute(got, 'core', SWAP)  3.47 us
  transfers between devices with their start and end apart: 3, of which 3 were waited for; matrix products, arithmetic and copies ran while one was open for 0% of the time, Pallas kernels for 0%

profile of v8, /device:TPU:6, one launch (start us, length us, event | category | flops | bytes accessed | tf_op | source)
XLA Modules:
  0.0 138.1 jit_solution(10523935872603345703)
XLA Ops:
  0.6 0.0 copy-start
  0.6 0.0 copy-start.1
  0.7 0.8 copy-done
  1.4 0.9 broadcast_in_dim.9
  2.4 16.0 %all-to-all-start = ((bf16[32,48,256]{2,1,0:T(8,128)(2,1)}), bf16[32,48,256]{2,1,0:T(8,128)(2,1)S(1)}, u32[]{:S(2)}, u32[]{:S(2)}) async-start(bf16[32,48,256]{2,1,0:T(8,128)(2,1)} %broadcast_in_dim.9), calls=%async_computation | async-start | bytes 1572864 | tf_op jit(solution)/shard_map/all_to_all | solution.py:173
  18.3 0.0 copy-done.1
  18.4 1.9 %collective-permute-start = (bf16[8,48,1536]{2,1,0:T(8,128)(2,1)S(1)}, bf16[8,48,1536]{2,1,0:T(8,128)(2,1)S(1)}, u32[]{:S(2)}, u32[]{:S(2)}) collective-permute-start(bf16[8,48,1536]{2,1,0:T(8,128)(2,1)S(1)} %copy-done.1), channel_id=1, source_target_pairs={{0,32},{32,0},{1,33},{33,1},{2,34},{34,2},{3,35},{35,3},{4,36},{36... | collective-permute-start | bytes 3538952 | tf_op jit(solution)/shard_map/ppermute | solution.py:171
  20.3 0.1 pad_add_fusion.place
  20.4 2.7 %collective-permute-done.other = bf16[8,48,1536]{2,1,0:T(8,128)(2,1)S(1)} collective-permute-done((bf16[8,48,1536]{2,1,0:T(8,128)(2,1)S(1)}, bf16[8,48,1536]{2,1,0:T(8,128)(2,1)S(1)}, u32[]{:S(2)}, u32[]{:S(2)}) %collective-permute-start) | collective-permute-done | bytes 1179680 | tf_op jit(solution)/shard_map/ppermute | solution.py:171
  23.1 19.1 %all-to-all-done = bf16[32,48,256]{2,1,0:T(8,128)(2,1)S(1)} async-done(((bf16[32,48,256]{2,1,0:T(8,128)(2,1)}), bf16[32,48,256]{2,1,0:T(8,128)(2,1)S(1)}, u32[]{:S(2)}, u32[]{:S(2)}) %all-to-all-start) | async-done | bytes 786464 | tf_op jit(solution)/shard_map/all_to_all | solution.py:173
  42.2 1.5 %half_transform.1 = bf16[8,4,200,128]{3,2,1,0:T(8,128)(2,1)S(1)} custom-call(s32[2]{0:T(128)S(1)} %pad_add_fusion.place, bf16[1536,256]{1,0:T(8,128)(2,1)S(1)} %bitcast.10, bf16[8,48,1536]{2,1,0:T(8,128)(2,1)S(1)} %copy-done.1, bf16[8,48,1536]{2,1,0:T(8,128)(2,1)S(1)} %collective-permute-done.other, bf16[48,256]{1,0:T(8,128)(2,1)S(1)} %dynamic-slice_bitcast_fusion.own), custom_call_target="tpu_custom_call" | custom-call | tf_op jit(solution)/shard_map/half_transform/pallas_call | solution.py:150
  43.7 48.4 %all_to_all.20 = bf16[32,200,128]{2,1,0:T(8,128)(2,1)S(1)} all-to-all(bf16[32,200,128]{2,1,0:T(8,128)(2,1)S(1)} %bitcast.9), channel_id=1, replica_groups=mesh['zl'=2,'x'=4,'core'=2,'y'=8,'zb'=2,'za'=2] {'y','zb','za'}, dimensions={0} | all-to-all | bytes 3276800 | tf_op jit(solution)/shard_map/all_to_all | solution.py:184
  92.1 1.9 %collective-permute-start.1 = (bf16[32,200,128]{2,1,0:T(8,128)(2,1)S(1)}, bf16[32,200,128]{2,1,0:T(8,128)(2,1)S(1)}, u32[]{:S(2)}, u32[]{:S(2)}) collective-permute-start(bf16[32,200,128]{2,1,0:T(8,128)(2,1)S(1)} %all_to_all.20), channel_id=1, source_target_pairs={{0,32},{32,0},{1,33},{33,1},{2,34},{34,2},{3,35},{35,3},{4,36},{36... | collective-permute-start | bytes 4915208 | tf_op jit(solution)/shard_map/ppermute | solution.py:185
  94.0 3.5 %collective-permute-done.1 = bf16[32,200,128]{2,1,0:T(8,128)(2,1)S(1)} collective-permute-done((bf16[32,200,128]{2,1,0:T(8,128)(2,1)S(1)}, bf16[32,200,128]{2,1,0:T(8,128)(2,1)S(1)}, u32[]{:S(2)}, u32[]{:S(2)}) %collective-permute-start.1) | collective-permute-done | bytes 1638432 | tf_op jit(solution)/shard_map/ppermute | solution.py:185
  97.4 2.8 %exchange_part.1 = bf16[8,224,384]{2,1,0:T(8,128)(2,1)S(1)} custom-call(s32[2]{0:T(128)S(1)} %pad_add_fusion.place, bf16[8,4,200,128]{3,2,1,0:T(8,128)(2,1)S(1)} %bitcast.8, bf16[8,4,200,128]{3,2,1,0:T(8,128)(2,1)S(1)} %bitcast.11, bf16[8,48,1536]{2,1,0:T(8,128)(2,1)S(1)} %copy-done.1, bf16[8,48,1536]{2,1,0:T(8,128)(2,1)S(1)} %collective-permute-done.other), custom_call_target="tpu_custom_call" | custom-call | tf_op jit(solution)/shard_map/exchange_part/pallas_call | solution.py:150
  100.3 22.6 %all_to_all.21.parts = bf16[8,224,384]{2,1,0:T(8,128)(2,1)S(1)} all-to-all(bf16[8,224,384]{2,1,0:T(8,128)(2,1)S(1)} %exchange_part.1), channel_id=1, replica_groups=mesh['zl'=2,'x'=4,'core'=2,'y'=8,'zb'=2,'za'=2] {'zl','x'}, dimensions={0} | all-to-all | bytes 2752512 | tf_op jit(solution)/shard_map/all_to_all | solution.py:197
  122.9 0.9 near_sum.1
  123.7 13.6 %all_to_all.22.parts = bf16[8,72,128]{2,1,0:T(8,128)(2,1)S(1)} all-to-all(bf16[8,72,128]{2,1,0:T(8,128)(2,1)S(1)} %get-tuple-element.4), channel_id=1, replica_groups=mesh['zl'=2,'x'=4,'core'=2,'y'=8,'zb'=2,'za'=2] {'y'}, dimensions={0} | all-to-all | bytes 294912 | tf_op jit(solution)/shard_map/all_to_all | solution.py:201
  137.3 0.8 far_sum.1
  (1 shorter events, 0.0 us)
Async XLA Ops:
  0.6 0.8 copy-start
  0.6 17.7 %copy-start.1 = (bf16[8,48,1536]{2,1,0:T(8,128)(2,1)S(1)}, bf16[8,48,1536]{2,1,0:T(8,128)(2,1)}, u32[]{:S(2)}) copy-start(bf16[8,48,1536]{2,1,0:T(8,128)(2,1)} %mine.3) | copy-start | bytes 3538948
  2.4 39.8 %all-to-all-start = ((bf16[32,48,256]{2,1,0:T(8,128)(2,1)}), bf16[32,48,256]{2,1,0:T(8,128)(2,1)S(1)}, u32[]{:S(2)}, u32[]{:S(2)}) async-start(bf16[32,48,256]{2,1,0:T(8,128)(2,1)} %broadcast_in_dim.9), calls=%async_computation | async-start | bytes 1572864 | tf_op jit(solution)/shard_map/all_to_all | solution.py:173
  18.4 4.7 %collective-permute-start = (bf16[8,48,1536]{2,1,0:T(8,128)(2,1)S(1)}, bf16[8,48,1536]{2,1,0:T(8,128)(2,1)S(1)}, u32[]{:S(2)}, u32[]{:S(2)}) collective-permute-start(bf16[8,48,1536]{2,1,0:T(8,128)(2,1)S(1)} %copy-done.1), channel_id=1, source_target_pairs={{0,32},{32,0},{1,33},{33,1},{2,34},{34,2},{3,35},{35,3},{4,36},{36... | collective-permute-start | bytes 3538952 | tf_op jit(solution)/shard_map/ppermute | solution.py:171
  92.1 5.4 %collective-permute-start.1 = (bf16[32,200,128]{2,1,0:T(8,128)(2,1)S(1)}, bf16[32,200,128]{2,1,0:T(8,128)(2,1)S(1)}, u32[]{:S(2)}, u32[]{:S(2)}) collective-permute-start(bf16[32,200,128]{2,1,0:T(8,128)(2,1)S(1)} %all_to_all.20), channel_id=1, source_target_pairs={{0,32},{32,0},{1,33},{33,1},{2,34},{34,2},{3,35},{35,3},{4,36},{36... | collective-permute-start | bytes 4915208 | tf_op jit(solution)/shard_map/ppermute | solution.py:185

commit v9 on v6

--- a/solution.py
+++ b/solution.py
@@ -11,7 +11,6 @@
 SUMS = ("y", "za")
 SWAP = [(0, 1), (1, 0)]
 f32, bf16 = jnp.float32, jnp.bfloat16
-SMEM = pl.BlockSpec(memory_space=pltpu.SMEM)
 VMEM = pl.BlockSpec(memory_space=pltpu.VMEM)
 
 
@@ -20,14 +19,19 @@
     return high, (value - high.astype(f32)).astype(bf16)
 
 
-def transform_kernel(place, full, mine, other, own, out):
-    core = place[0]
+def vector_lanes(core, count, width):
+    row = lax.broadcasted_iota(jnp.int32, (2 * count, width), 0)
+    lane = lax.broadcasted_iota(jnp.int32, (2 * count, width), 1)
+    return lane == jnp.where(core == 0, row, jnp.where(row < count, row + count, row - count))
+
+
+def transform_kernel(full, mine, other, own, out):
+    core = lax.axis_index("core")
     count, rows, nao = mine.shape
     wide = full.shape[1]
     half = wide // 2
     weight = own[...].astype(f32)
-    lane = lax.broadcasted_iota(jnp.int32, (1, half), 1)
-    terms = jnp.zeros((1, half), f32)
+    terms = []
     for source, owner in ((mine, core), (other, 1 - core)):
         slab = jnp.dot(
             source[...].reshape(count * rows, nao), full[...], preferred_element_type=f32
@@ -37,10 +41,9 @@
             for zb in range(2):
                 out[owner * (count // 2) + p // 2, zb, p % 2, 0:rows] = block[:, :half]
                 out[owner * (count // 2) + p // 2, zb, p % 2, rows : 2 * rows] = block[:, half:]
-            term = jnp.sum(block.astype(f32) * weight, axis=0, keepdims=True)
-            term = jnp.sum(term, axis=1, keepdims=True)
-            terms += jnp.where(lane == owner * count + p, term, 0.0)
-    high, low = words(terms)
+            terms.append(jnp.sum(block.astype(f32) * weight, axis=0, keepdims=True))
+    terms = jnp.sum(jnp.concatenate(terms), axis=1, keepdims=True)
+    high, low = words(jnp.sum(jnp.where(vector_lanes(core, count, half), terms, 0.0), axis=0, keepdims=True))
     lines = lax.broadcasted_iota(jnp.int32, (8, half), 0)
     rider = jnp.where(lines == 0, high.astype(f32), jnp.where(lines == 1, low.astype(f32), 0.0))
     rider = rider.astype(bf16)
@@ -50,8 +53,8 @@
                 out[y, zb, za, 2 * rows : 2 * rows + 8] = rider
 
 
-def exchange_kernel(place, got, got_other, mine, other, out, column_side, row_side):
-    core, zb = place[0], place[1]
+def exchange_kernel(got, got_other, mine, other, out, column_side, row_side):
+    core, zb = lax.axis_index("core"), lax.axis_index("zb")
     count, rows, nao = mine.shape
     half = got.shape[4]
     wide = 2 * half
@@ -82,17 +85,13 @@
                 for source in (got, got_other):
                     riders += source[y, b, za, 2 * rows : 2 * rows + 8].astype(f32)
     weights = riders[0:1] + riders[1:2]
-    lane = lax.broadcasted_iota(jnp.int32, (1, half), 1)
-    weighted = []
-    for source, owner in ((mine, core), (other, 1 - core)):
-        for p in range(count):
-            weight = jnp.sum(jnp.where(lane == owner * count + p, weights, 0.0), axis=1, keepdims=True)
-            weighted.append((source, p, weight))
+    weights = jnp.sum(jnp.where(vector_lanes(core, count, half), weights, 0.0), axis=1, keepdims=True)
     for part in range(3):
         at = pl.ds(part * 16, 16)
         total = jnp.zeros((16, nao), f32)
-        for source, p, weight in weighted:
-            total += weight * source[p, at].astype(f32)
+        for k, source in enumerate((mine, other)):
+            for p in range(count):
+                total += weights[k * count + p : k * count + p + 1] * source[p, at].astype(f32)
         for s in range(8):
             start = s * 4 * rows
             piece = jnp.where(
@@ -142,14 +141,11 @@
     out[1] = jnp.concatenate([total[:rows, 2 * rows :], rest], axis=1)
 
 
-def call(kernel, name, grant, outs, inputs, place=None, scratch=()):
-    specs = [VMEM] * len(inputs)
-    if place is not None:
-        specs, inputs = [SMEM] + specs, (place,) + inputs
+def call(kernel, name, grant, outs, inputs, scratch=()):
     return pl.pallas_call(
         kernel,
         out_shape=[jax.ShapeDtypeStruct(shape, dtype) for shape, dtype in outs],
-        in_specs=specs,
+        in_specs=[VMEM] * len(inputs),
         out_specs=[VMEM] * len(outs),
         scratch_shapes=scratch,
         compiler_params=pltpu.CompilerParams(vmem_limit_bytes=grant * 2**20),
@@ -159,8 +155,6 @@
 
 def on_device(vectors, coeffs):
     core = lax.axis_index("core")
-    zb = lax.axis_index("zb")
-    place = jnp.stack([core, zb]).astype(jnp.int32)
     count, rows, nao = vectors.shape
     wide = coeffs.shape[2]
     half = wide // 2
@@ -178,7 +172,6 @@
         16,
         [(shape, bf16)],
         (full, vectors, other_vectors, own),
-        place,
     )
     got = lax.all_to_all(pieces.reshape(32, tall, half), FAR, 0, 0, tiled=True)
     got_other = lax.ppermute(got, "core", SWAP)
@@ -190,7 +183,6 @@
         24,
         [((8, deep, 16 * rows), bf16)],
         (got.reshape(shape), got_other.reshape(shape), vectors, other_vectors),
-        place,
         scratch,
     )
     parts = lax.all_to_all(parts, NEAR, 0, 0, tiled=True)

time: 138 us -> 137 us (level)
  no operation moved by 1% of the time
where the time goes in v9:
time: 137 us; the launch traced here: 136 us
  blocking collectives  85.1 us (62%)
  waiting for transfers between devices  24.2 us (18%)
  starting transfers between devices  19.8 us (14%)
  Pallas kernels  4.5 us (3%)
  local copies, waits for them, and re-layouts  1.74 us (1%)
    all_to_all x1, blocking collectives, on_device(): parts = lax.all_to_all(parts, NEAR, 0, 0, tiled=True)  35.2 us
    all_to_all x1, blocking collectives, on_device(): got = lax.all_to_all(pieces.reshape(32, tall, half), FAR, 0, 0, tiled=True)  31.1 us
    all_to_all x1, waiting for transfers between devices, on_device(): lax.all_to_all(jnp.broadcast_to(own[None], (32, rows, wide)), FAR, 0, 0,...  18.9 us
    all_to_all x1, blocking collectives, on_device(): packed = lax.all_to_all(packed, SUMS, 0, 0, tiled=True)  18.8 us
    all_to_all x1, starting transfers between devices, on_device(): lax.all_to_all(jnp.broadcast_to(own[None], (32, rows, wide)), FAR, 0, 0,...  16 us
    pallas_call x4, Pallas kernels, call(): pl.pallas_call(kernel, out_shape=[jax.ShapeDtypeStruct(shape, dtype) for...  4.5 us
    ppermute x1, waiting for transfers between devices, on_device(): other_vectors = lax.ppermute(vectors, 'core', SWAP)  3.02 us
  transfers between devices with their start and end apart: 3, of which 3 were waited for; matrix products, arithmetic and copies ran while one was open for 0% of the time, Pallas kernels for 0%

profile of v9, /device:TPU:6, one launch (start us, length us, event | category | flops | bytes accessed | tf_op | source)
XLA Modules:
  0.0 136.1 jit_solution(6046960771372348308)
XLA Ops:
  0.6 0.0 copy-start
  0.6 0.0 copy-start.1
  0.7 0.8 copy-done
  1.4 0.9 broadcast_in_dim.9
  2.4 16.0 %all-to-all-start = ((bf16[32,48,256]{2,1,0:T(8,128)(2,1)}), bf16[32,48,256]{2,1,0:T(8,128)(2,1)S(1)}, u32[]{:S(2)}, u32[]{:S(2)}) async-start(bf16[32,48,256]{2,1,0:T(8,128)(2,1)} %broadcast_in_dim.9), calls=%async_computation | async-start | bytes 1572864 | tf_op jit(solution)/shard_map/all_to_all | solution.py:166
  18.3 1.9 %collective-permute-start = (bf16[8,48,1536]{2,1,0:T(8,128)(2,1)}, bf16[8,48,1536]{2,1,0:T(8,128)(2,1)S(1)}, u32[]{:S(2)}, u32[]{:S(2)}) collective-permute-start(bf16[8,48,1536]{2,1,0:T(8,128)(2,1)} %mine.3), channel_id=1, source_target_pairs={{0,32},{32,0},{1,33},{33,1},{2,34},{34,2},{3,35},{35,3},{4,36},{36... | collective-permute-start | bytes 3538952 | tf_op jit(solution)/shard_map/ppermute | solution.py:164
  20.3 3.0 %collective-permute-done.other = bf16[8,48,1536]{2,1,0:T(8,128)(2,1)S(1)} collective-permute-done((bf16[8,48,1536]{2,1,0:T(8,128)(2,1)}, bf16[8,48,1536]{2,1,0:T(8,128)(2,1)S(1)}, u32[]{:S(2)}, u32[]{:S(2)}) %collective-permute-start) | collective-permute-done | bytes 1179680 | tf_op jit(solution)/shard_map/ppermute | solution.py:164
  23.3 18.9 %all-to-all-done = bf16[32,48,256]{2,1,0:T(8,128)(2,1)S(1)} async-done(((bf16[32,48,256]{2,1,0:T(8,128)(2,1)}), bf16[32,48,256]{2,1,0:T(8,128)(2,1)S(1)}, u32[]{:S(2)}, u32[]{:S(2)}) %all-to-all-start) | async-done | bytes 786464 | tf_op jit(solution)/shard_map/all_to_all | solution.py:166
  42.2 0.0 copy-done.1
  42.2 0.9 half_transform.1
  43.1 31.1 %all_to_all.20 = bf16[32,104,128]{2,1,0:T(8,128)(2,1)S(1)} all-to-all(bf16[32,104,128]{2,1,0:T(8,128)(2,1)S(1)} %bitcast.7), channel_id=1, replica_groups=mesh['zl'=2,'x'=4,'core'=2,'y'=8,'zb'=2,'za'=2] {'y','zb','za'}, dimensions={0} | all-to-all | bytes 1703936 | tf_op jit(solution)/shard_map/all_to_all | solution.py:176
  74.2 1.9 %collective-permute-start.1 = (bf16[32,104,128]{2,1,0:T(8,128)(2,1)S(1)}, bf16[32,104,128]{2,1,0:T(8,128)(2,1)S(1)}, u32[]{:S(2)}, u32[]{:S(2)}) collective-permute-start(bf16[32,104,128]{2,1,0:T(8,128)(2,1)S(1)} %all_to_all.20), channel_id=1, source_target_pairs={{0,32},{32,0},{1,33},{33,1},{2,34},{34,2},{3,35},{35,3},{4,36},{36... | collective-permute-start | bytes 2555912 | tf_op jit(solution)/shard_map/ppermute | solution.py:177
  76.1 2.3 %collective-permute-done.1 = bf16[32,104,128]{2,1,0:T(8,128)(2,1)S(1)} collective-permute-done((bf16[32,104,128]{2,1,0:T(8,128)(2,1)S(1)}, bf16[32,104,128]{2,1,0:T(8,128)(2,1)S(1)}, u32[]{:S(2)}, u32[]{:S(2)}) %collective-permute-start.1) | collective-permute-done | bytes 852000 | tf_op jit(solution)/shard_map/ppermute | solution.py:177
  78.4 1.8 %exchange_quarter.1 = bf16[8,208,768]{2,1,0:T(8,128)(2,1)S(1)} custom-call(bf16[8,2,2,104,128]{4,3,2,1,0:T(8,128)(2,1)S(1)} %bitcast.6, bf16[8,2,2,104,128]{4,3,2,1,0:T(8,128)(2,1)S(1)} %bitcast.9, bf16[8,48,1536]{2,1,0:T(8,128)(2,1)S(1)} %copy-done.1, bf16[8,48,1536]{2,1,0:T(8,128)(2,1)S(1)} %collective-permute-done.other), custom_call_target="tpu_custom_call" | custom-call | tf_op jit(solution)/shard_map/exchange_quarter/pallas_call | solution.py:145
  80.2 35.2 %all_to_all.21.parts = bf16[8,208,768]{2,1,0:T(8,128)(2,1)S(1)} all-to-all(bf16[8,208,768]{2,1,0:T(8,128)(2,1)S(1)} %exchange_quarter.1), channel_id=1, replica_groups=mesh['zl'=2,'x'=4,'core'=2,'y'=8,'zb'=2,'za'=2] {'zl','x'}, dimensions={0} | all-to-all | bytes 5111808 | tf_op jit(solution)/shard_map/all_to_all | solution.py:188
  115.5 1.0 near_sum.1
  116.5 18.8 %all_to_all.22.parts = bf16[16,72,128]{2,1,0:T(8,128)(2,1)S(1)} all-to-all(bf16[16,72,128]{2,1,0:T(8,128)(2,1)S(1)} %get-tuple-element.4), channel_id=1, replica_groups=mesh['zl'=2,'x'=4,'core'=2,'y'=8,'zb'=2,'za'=2] {'y','za'}, dimensions={0} | all-to-all | bytes 589824 | tf_op jit(solution)/shard_map/all_to_all | solution.py:192
  135.3 0.8 far_sum.1
  (1 shorter events, 0.0 us)
Async XLA Ops:
  0.6 0.8 copy-start
  0.6 41.5 %copy-start.1 = (bf16[8,48,1536]{2,1,0:T(8,128)(2,1)S(1)}, bf16[8,48,1536]{2,1,0:T(8,128)(2,1)}, u32[]{:S(2)}) copy-start(bf16[8,48,1536]{2,1,0:T(8,128)(2,1)} %mine.3) | copy-start | bytes 3538948
  2.4 39.8 %all-to-all-start = ((bf16[32,48,256]{2,1,0:T(8,128)(2,1)}), bf16[32,48,256]{2,1,0:T(8,128)(2,1)S(1)}, u32[]{:S(2)}, u32[]{:S(2)}) async-start(bf16[32,48,256]{2,1,0:T(8,128)(2,1)} %broadcast_in_dim.9), calls=%async_computation | async-start | bytes 1572864 | tf_op jit(solution)/shard_map/all_to_all | solution.py:166
  18.3 5.0 %collective-permute-start = (bf16[8,48,1536]{2,1,0:T(8,128)(2,1)}, bf16[8,48,1536]{2,1,0:T(8,128)(2,1)S(1)}, u32[]{:S(2)}, u32[]{:S(2)}) collective-permute-start(bf16[8,48,1536]{2,1,0:T(8,128)(2,1)} %mine.3), channel_id=1, source_target_pairs={{0,32},{32,0},{1,33},{33,1},{2,34},{34,2},{3,35},{35,3},{4,36},{36... | collective-permute-start | bytes 3538952 | tf_op jit(solution)/shard_map/ppermute | solution.py:164
  74.2 4.3 %collective-permute-start.1 = (bf16[32,104,128]{2,1,0:T(8,128)(2,1)S(1)}, bf16[32,104,128]{2,1,0:T(8,128)(2,1)S(1)}, u32[]{:S(2)}, u32[]{:S(2)}) collective-permute-start(bf16[32,104,128]{2,1,0:T(8,128)(2,1)S(1)} %all_to_all.20), channel_id=1, source_target_pairs={{0,32},{32,0},{1,33},{33,1},{2,34},{34,2},{3,35},{35,3},{4,36},{36... | collective-permute-start | bytes 2555912 | tf_op jit(solution)/shard_map/ppermute | solution.py:177

commit v10 on v9

--- a/solution.py
+++ b/solution.py
@@ -114,15 +114,10 @@
             out[s, 0 : 4 * rows, n * 256 : (n + 1) * 256] = block[s * 4 * rows : (s + 1) * 4 * rows]
 
 
-def near_sum_kernel(parts, out, coulomb):
-    rows = coulomb.shape[0]
+def near_sum_kernel(parts, out, tail):
+    rows = parts.shape[2] // 16
     deep = 4 * rows
-    tail = jnp.sum(parts[:, deep : deep + 16].astype(f32), axis=0)
-    for part in range(3):
-        start = part * 256
-        coulomb[part * 16 : (part + 1) * 16] = (
-            tail[:, start : start + 2 * rows] + tail[:, start + 128 : start + 128 + 2 * rows]
-        )
+    tail[...] = jnp.sum(parts[:, deep : deep + 16].astype(f32), axis=0)
     for n in range(2):
         columns = slice(n * 8 * rows, (n + 1) * 8 * rows)
         turned = jnp.sum(parts[:, 0:deep, columns].astype(f32), axis=0).T
@@ -133,8 +128,12 @@
             out[n * 8 + j, rows : rows + rows // 2] = rest.astype(bf16)
 
 
-def far_sum_kernel(parts, out):
+def far_sum_kernel(parts, tail, out, coulomb):
     rows = out.shape[1]
+    for part in range(3):
+        high = slice(part * 256, part * 256 + 2 * rows)
+        low = slice(part * 256 + 128, part * 256 + 128 + 2 * rows)
+        coulomb[part * 16 : (part + 1) * 16] = tail[:, high] + tail[:, low]
     total = jnp.sum(parts[...].astype(f32), axis=0)
     rest = jnp.concatenate([total[rows:, :64], total[rows:, 64:]], axis=0)
     out[0] = total[:rows, : 2 * rows]
@@ -186,12 +185,13 @@
         scratch,
     )
     parts = lax.all_to_all(parts, NEAR, 0, 0, tiled=True)
-    packed, coulomb = call(
-        near_sum_kernel, "near_sum", 12, [((16, rows + rows // 2, 128), bf16), ((rows, 2 * rows), f32)], (parts,)
+    packed, tail = call(
+        near_sum_kernel, "near_sum", 12, [((16, rows + rows // 2, 128), bf16), ((16, 16 * rows), f32)], (parts,)
     )
     packed = lax.all_to_all(packed, SUMS, 0, 0, tiled=True)
-    (exchange,) = call(far_sum_kernel, "far_sum", 4, [((2, rows, 2 * rows), f32)], (packed,))
-    return exchange, coulomb
+    return call(
+        far_sum_kernel, "far_sum", 4, [((2, rows, 2 * rows), f32), ((rows, 2 * rows), f32)], (packed, tail)
+    )
 
 
 def solution(mesh):

time: 137 us -> 137 us (level)
  no operation moved by 1% of the time
where the time goes in v10:
time: 137 us; the launch traced here: 136 us
  blocking collectives  85.1 us (62%)
  waiting for transfers between devices  24.2 us (18%)
  starting transfers between devices  19.8 us (14%)
  Pallas kernels  3.91 us (3%)
  local copies, waits for them, and re-layouts  1.74 us (1%)
    all_to_all x1, blocking collectives, on_device(): parts = lax.all_to_all(parts, NEAR, 0, 0, tiled=True)  35.2 us
    all_to_all x1, blocking collectives, on_device(): got = lax.all_to_all(pieces.reshape(32, tall, half), FAR, 0, 0, tiled=True)  31.1 us
    all_to_all x1, waiting for transfers between devices, on_device(): lax.all_to_all(jnp.broadcast_to(own[None], (32, rows, wide)), FAR, 0, 0,...  18.9 us
    all_to_all x1, blocking collectives, on_device(): packed = lax.all_to_all(packed, SUMS, 0, 0, tiled=True)  18.8 us
    all_to_all x1, starting transfers between devices, on_device(): lax.all_to_all(jnp.broadcast_to(own[None], (32, rows, wide)), FAR, 0, 0,...  16 us
    pallas_call x4, Pallas kernels, call(): pl.pallas_call(kernel, out_shape=[jax.ShapeDtypeStruct(shape, dtype) for...  3.91 us
    ppermute x1, waiting for transfers between devices, on_device(): other_vectors = lax.ppermute(vectors, 'core', SWAP)  3.02 us
  transfers between devices with their start and end apart: 3, of which 3 were waited for; matrix products, arithmetic and copies ran while one was open for 0% of the time, Pallas kernels for 0%

profile of v10, /device:TPU:6, one launch (start us, length us, event | category | flops | bytes accessed | tf_op | source)
XLA Modules:
  0.0 135.5 jit_solution(11356351070452336352)
XLA Ops:
  0.6 0.0 copy-start
  0.6 0.0 copy-start.1
  0.7 0.8 copy-done
  1.4 0.9 broadcast_in_dim.9
  2.4 16.0 %all-to-all-start = ((bf16[32,48,256]{2,1,0:T(8,128)(2,1)}), bf16[32,48,256]{2,1,0:T(8,128)(2,1)S(1)}, u32[]{:S(2)}, u32[]{:S(2)}) async-start(bf16[32,48,256]{2,1,0:T(8,128)(2,1)} %broadcast_in_dim.9), calls=%async_computation | async-start | bytes 1572864 | tf_op jit(solution)/shard_map/all_to_all | solution.py:165
  18.3 1.9 %collective-permute-start = (bf16[8,48,1536]{2,1,0:T(8,128)(2,1)}, bf16[8,48,1536]{2,1,0:T(8,128)(2,1)S(1)}, u32[]{:S(2)}, u32[]{:S(2)}) collective-permute-start(bf16[8,48,1536]{2,1,0:T(8,128)(2,1)} %mine.3), channel_id=1, source_target_pairs={{0,32},{32,0},{1,33},{33,1},{2,34},{34,2},{3,35},{35,3},{4,36},{36... | collective-permute-start | bytes 3538952 | tf_op jit(solution)/shard_map/ppermute | solution.py:163
  20.3 3.0 %collective-permute-done.other = bf16[8,48,1536]{2,1,0:T(8,128)(2,1)S(1)} collective-permute-done((bf16[8,48,1536]{2,1,0:T(8,128)(2,1)}, bf16[8,48,1536]{2,1,0:T(8,128)(2,1)S(1)}, u32[]{:S(2)}, u32[]{:S(2)}) %collective-permute-start) | collective-permute-done | bytes 1179680 | tf_op jit(solution)/shard_map/ppermute | solution.py:163
  23.3 18.9 %all-to-all-done = bf16[32,48,256]{2,1,0:T(8,128)(2,1)S(1)} async-done(((bf16[32,48,256]{2,1,0:T(8,128)(2,1)}), bf16[32,48,256]{2,1,0:T(8,128)(2,1)S(1)}, u32[]{:S(2)}, u32[]{:S(2)}) %all-to-all-start) | async-done | bytes 786464 | tf_op jit(solution)/shard_map/all_to_all | solution.py:165
  42.2 0.0 copy-done.1
  42.2 0.9 half_transform.1
  43.1 31.1 %all_to_all.20 = bf16[32,104,128]{2,1,0:T(8,128)(2,1)S(1)} all-to-all(bf16[32,104,128]{2,1,0:T(8,128)(2,1)S(1)} %bitcast.7), channel_id=1, replica_groups=mesh['zl'=2,'x'=4,'core'=2,'y'=8,'zb'=2,'za'=2] {'y','zb','za'}, dimensions={0} | all-to-all | bytes 1703936 | tf_op jit(solution)/shard_map/all_to_all | solution.py:175
  74.2 1.9 %collective-permute-start.1 = (bf16[32,104,128]{2,1,0:T(8,128)(2,1)S(1)}, bf16[32,104,128]{2,1,0:T(8,128)(2,1)S(1)}, u32[]{:S(2)}, u32[]{:S(2)}) collective-permute-start(bf16[32,104,128]{2,1,0:T(8,128)(2,1)S(1)} %all_to_all.20), channel_id=1, source_target_pairs={{0,32},{32,0},{1,33},{33,1},{2,34},{34,2},{3,35},{35,3},{4,36},{36... | collective-permute-start | bytes 2555912 | tf_op jit(solution)/shard_map/ppermute | solution.py:176
  76.1 2.3 %collective-permute-done.1 = bf16[32,104,128]{2,1,0:T(8,128)(2,1)S(1)} collective-permute-done((bf16[32,104,128]{2,1,0:T(8,128)(2,1)S(1)}, bf16[32,104,128]{2,1,0:T(8,128)(2,1)S(1)}, u32[]{:S(2)}, u32[]{:S(2)}) %collective-permute-start.1) | collective-permute-done | bytes 852000 | tf_op jit(solution)/shard_map/ppermute | solution.py:176
  78.4 1.8 %exchange_quarter.1 = bf16[8,208,768]{2,1,0:T(8,128)(2,1)S(1)} custom-call(bf16[8,2,2,104,128]{4,3,2,1,0:T(8,128)(2,1)S(1)} %bitcast.6, bf16[8,2,2,104,128]{4,3,2,1,0:T(8,128)(2,1)S(1)} %bitcast.9, bf16[8,48,1536]{2,1,0:T(8,128)(2,1)S(1)} %copy-done.1, bf16[8,48,1536]{2,1,0:T(8,128)(2,1)S(1)} %collective-permute-done.other), custom_call_target="tpu_custom_call" | custom-call | tf_op jit(solution)/shard_map/exchange_quarter/pallas_call | solution.py:144
  80.2 35.2 %all_to_all.21.parts = bf16[8,208,768]{2,1,0:T(8,128)(2,1)S(1)} all-to-all(bf16[8,208,768]{2,1,0:T(8,128)(2,1)S(1)} %exchange_quarter.1), channel_id=1, replica_groups=mesh['zl'=2,'x'=4,'core'=2,'y'=8,'zb'=2,'za'=2] {'zl','x'}, dimensions={0} | all-to-all | bytes 5111808 | tf_op jit(solution)/shard_map/all_to_all | solution.py:187
  115.5 0.4 near_sum.1
  115.9 18.8 %all_to_all.22.parts = bf16[16,72,128]{2,1,0:T(8,128)(2,1)S(1)} all-to-all(bf16[16,72,128]{2,1,0:T(8,128)(2,1)S(1)} %get-tuple-element.4), channel_id=1, replica_groups=mesh['zl'=2,'x'=4,'core'=2,'y'=8,'zb'=2,'za'=2] {'y','za'}, dimensions={0} | all-to-all | bytes 589824 | tf_op jit(solution)/shard_map/all_to_all | solution.py:191
  134.7 0.8 far_sum.1
  (1 shorter events, 0.0 us)
Async XLA Ops:
  0.6 0.8 copy-start
  0.6 41.5 %copy-start.1 = (bf16[8,48,1536]{2,1,0:T(8,128)(2,1)S(1)}, bf16[8,48,1536]{2,1,0:T(8,128)(2,1)}, u32[]{:S(2)}) copy-start(bf16[8,48,1536]{2,1,0:T(8,128)(2,1)} %mine.3) | copy-start | bytes 3538948
  2.4 39.8 %all-to-all-start = ((bf16[32,48,256]{2,1,0:T(8,128)(2,1)}), bf16[32,48,256]{2,1,0:T(8,128)(2,1)S(1)}, u32[]{:S(2)}, u32[]{:S(2)}) async-start(bf16[32,48,256]{2,1,0:T(8,128)(2,1)} %broadcast_in_dim.9), calls=%async_computation | async-start | bytes 1572864 | tf_op jit(solution)/shard_map/all_to_all | solution.py:165
  18.3 5.0 %collective-permute-start = (bf16[8,48,1536]{2,1,0:T(8,128)(2,1)}, bf16[8,48,1536]{2,1,0:T(8,128)(2,1)S(1)}, u32[]{:S(2)}, u32[]{:S(2)}) collective-permute-start(bf16[8,48,1536]{2,1,0:T(8,128)(2,1)} %mine.3), channel_id=1, source_target_pairs={{0,32},{32,0},{1,33},{33,1},{2,34},{34,2},{3,35},{35,3},{4,36},{36... | collective-permute-start | bytes 3538952 | tf_op jit(solution)/shard_map/ppermute | solution.py:163
  74.2 4.3 %collective-permute-start.1 = (bf16[32,104,128]{2,1,0:T(8,128)(2,1)S(1)}, bf16[32,104,128]{2,1,0:T(8,128)(2,1)S(1)}, u32[]{:S(2)}, u32[]{:S(2)}) collective-permute-start(bf16[32,104,128]{2,1,0:T(8,128)(2,1)S(1)} %all_to_all.20), channel_id=1, source_target_pairs={{0,32},{32,0},{1,33},{33,1},{2,34},{34,2},{3,35},{35,3},{4,36},{36... | collective-permute-start | bytes 2555912 | tf_op jit(solution)/shard_map/ppermute | solution.py:176

commit v11 on v10

--- a/solution.py
+++ b/solution.py
@@ -8,7 +8,7 @@
 
 NEAR = ("zl", "x")
 FAR = ("y", "zb", "za")
-SUMS = ("y", "za")
+SUMS = ("za", "y")
 SWAP = [(0, 1), (1, 0)]
 f32, bf16 = jnp.float32, jnp.bfloat16
 VMEM = pl.BlockSpec(memory_space=pltpu.VMEM)
@@ -124,8 +124,9 @@
         for j in range(8):
             block = turned[j * rows : (j + 1) * rows]
             rest = jnp.concatenate([block[: rows // 2, 128:], block[rows // 2 :, 128:]], axis=1)
-            out[n * 8 + j, 0:rows] = block[:, :128].astype(bf16)
-            out[n * 8 + j, rows : rows + rows // 2] = rest.astype(bf16)
+            at = j % 2 * 8 + n * 4 + j // 2
+            out[at, 0:rows] = block[:, :128].astype(bf16)
+            out[at, rows : rows + rows // 2] = rest.astype(bf16)
 
 
 def far_sum_kernel(parts, tail, out, coulomb):

time: 137 us -> 136 us (level)
  blocking collectives: 85.1 us -> 83.3 us
    all_to_all x1, blocking collectives: 18.8 us -> 17 us  [on_device(): packed = lax.all_to_all(packed, SUMS, 0, 0, tiled=True)]
where the time goes in v11:
time: 136 us; the launch traced here: 134 us
  blocking collectives  83.3 us (61%)
  waiting for transfers between devices  24.2 us (18%)
  starting transfers between devices  19.8 us (15%)
  Pallas kernels  3.91 us (3%)
  local copies, waits for them, and re-layouts  1.74 us (1%)
    all_to_all x1, blocking collectives, on_device(): parts = lax.all_to_all(parts, NEAR, 0, 0, tiled=True)  35.2 us
    all_to_all x1, blocking collectives, on_device(): got = lax.all_to_all(pieces.reshape(32, tall, half), FAR, 0, 0, tiled=True)  31.1 us
    all_to_all x1, waiting for transfers between devices, on_device(): lax.all_to_all(jnp.broadcast_to(own[None], (32, rows, wide)), FAR, 0, 0,...  18.9 us
    all_to_all x1, blocking collectives, on_device(): packed = lax.all_to_all(packed, SUMS, 0, 0, tiled=True)  17 us
    all_to_all x1, starting transfers between devices, on_device(): lax.all_to_all(jnp.broadcast_to(own[None], (32, rows, wide)), FAR, 0, 0,...  16 us
    pallas_call x4, Pallas kernels, call(): pl.pallas_call(kernel, out_shape=[jax.ShapeDtypeStruct(shape, dtype) for...  3.91 us
    ppermute x1, waiting for transfers between devices, on_device(): other_vectors = lax.ppermute(vectors, 'core', SWAP)  3.02 us
  transfers between devices with their start and end apart: 3, of which 3 were waited for; matrix products, arithmetic and copies ran while one was open for 0% of the time, Pallas kernels for 0%

profile of v11, /device:TPU:6, one launch (start us, length us, event | category | flops | bytes accessed | tf_op | source)
XLA Modules:
  0.0 133.7 jit_solution(16137391922265275513)
XLA Ops:
  0.6 0.0 copy-start
  0.6 0.0 copy-start.1
  0.7 0.8 copy-done
  1.4 0.9 broadcast_in_dim.9
  2.4 16.0 %all-to-all-start = ((bf16[32,48,256]{2,1,0:T(8,128)(2,1)}), bf16[32,48,256]{2,1,0:T(8,128)(2,1)S(1)}, u32[]{:S(2)}, u32[]{:S(2)}) async-start(bf16[32,48,256]{2,1,0:T(8,128)(2,1)} %broadcast_in_dim.9), calls=%async_computation | async-start | bytes 1572864 | tf_op jit(solution)/shard_map/all_to_all | solution.py:166
  18.3 1.9 %collective-permute-start = (bf16[8,48,1536]{2,1,0:T(8,128)(2,1)}, bf16[8,48,1536]{2,1,0:T(8,128)(2,1)S(1)}, u32[]{:S(2)}, u32[]{:S(2)}) collective-permute-start(bf16[8,48,1536]{2,1,0:T(8,128)(2,1)} %mine.3), channel_id=1, source_target_pairs={{0,32},{32,0},{1,33},{33,1},{2,34},{34,2},{3,35},{35,3},{4,36},{36... | collective-permute-start | bytes 3538952 | tf_op jit(solution)/shard_map/ppermute | solution.py:164
  20.3 3.0 %collective-permute-done.other = bf16[8,48,1536]{2,1,0:T(8,128)(2,1)S(1)} collective-permute-done((bf16[8,48,1536]{2,1,0:T(8,128)(2,1)}, bf16[8,48,1536]{2,1,0:T(8,128)(2,1)S(1)}, u32[]{:S(2)}, u32[]{:S(2)}) %collective-permute-start) | collective-permute-done | bytes 1179680 | tf_op jit(solution)/shard_map/ppermute | solution.py:164
  23.3 18.9 %all-to-all-done = bf16[32,48,256]{2,1,0:T(8,128)(2,1)S(1)} async-done(((bf16[32,48,256]{2,1,0:T(8,128)(2,1)}), bf16[32,48,256]{2,1,0:T(8,128)(2,1)S(1)}, u32[]{:S(2)}, u32[]{:S(2)}) %all-to-all-start) | async-done | bytes 786464 | tf_op jit(solution)/shard_map/all_to_all | solution.py:166
  42.2 0.0 copy-done.1
  42.2 0.9 half_transform.1
  43.1 31.1 %all_to_all.20 = bf16[32,104,128]{2,1,0:T(8,128)(2,1)S(1)} all-to-all(bf16[32,104,128]{2,1,0:T(8,128)(2,1)S(1)} %bitcast.7), channel_id=1, replica_groups=mesh['zl'=2,'x'=4,'core'=2,'y'=8,'zb'=2,'za'=2] {'y','zb','za'}, dimensions={0} | all-to-all | bytes 1703936 | tf_op jit(solution)/shard_map/all_to_all | solution.py:176
  74.2 1.9 %collective-permute-start.1 = (bf16[32,104,128]{2,1,0:T(8,128)(2,1)S(1)}, bf16[32,104,128]{2,1,0:T(8,128)(2,1)S(1)}, u32[]{:S(2)}, u32[]{:S(2)}) collective-permute-start(bf16[32,104,128]{2,1,0:T(8,128)(2,1)S(1)} %all_to_all.20), channel_id=1, source_target_pairs={{0,32},{32,0},{1,33},{33,1},{2,34},{34,2},{3,35},{35,3},{4,36},{36... | collective-permute-start | bytes 2555912 | tf_op jit(solution)/shard_map/ppermute | solution.py:177
  76.1 2.3 %collective-permute-done.1 = bf16[32,104,128]{2,1,0:T(8,128)(2,1)S(1)} collective-permute-done((bf16[32,104,128]{2,1,0:T(8,128)(2,1)S(1)}, bf16[32,104,128]{2,1,0:T(8,128)(2,1)S(1)}, u32[]{:S(2)}, u32[]{:S(2)}) %collective-permute-start.1) | collective-permute-done | bytes 852000 | tf_op jit(solution)/shard_map/ppermute | solution.py:177
  78.4 1.8 %exchange_quarter.1 = bf16[8,208,768]{2,1,0:T(8,128)(2,1)S(1)} custom-call(bf16[8,2,2,104,128]{4,3,2,1,0:T(8,128)(2,1)S(1)} %bitcast.6, bf16[8,2,2,104,128]{4,3,2,1,0:T(8,128)(2,1)S(1)} %bitcast.9, bf16[8,48,1536]{2,1,0:T(8,128)(2,1)S(1)} %copy-done.1, bf16[8,48,1536]{2,1,0:T(8,128)(2,1)S(1)} %collective-permute-done.other), custom_call_target="tpu_custom_call" | custom-call | tf_op jit(solution)/shard_map/exchange_quarter/pallas_call | solution.py:145
  80.2 35.2 %all_to_all.21.parts = bf16[8,208,768]{2,1,0:T(8,128)(2,1)S(1)} all-to-all(bf16[8,208,768]{2,1,0:T(8,128)(2,1)S(1)} %exchange_quarter.1), channel_id=1, replica_groups=mesh['zl'=2,'x'=4,'core'=2,'y'=8,'zb'=2,'za'=2] {'zl','x'}, dimensions={0} | all-to-all | bytes 5111808 | tf_op jit(solution)/shard_map/all_to_all | solution.py:188
  115.5 0.4 near_sum.1
  115.9 17.0 %all_to_all.22.parts = bf16[16,72,128]{2,1,0:T(8,128)(2,1)S(1)} all-to-all(bf16[16,72,128]{2,1,0:T(8,128)(2,1)S(1)} %get-tuple-element.4), channel_id=1, replica_groups=mesh['zl'=2,'x'=4,'core'=2,'y'=8,'zb'=2,'za'=2] {'za','y'}, dimensions={0} | all-to-all | bytes 589824 | tf_op jit(solution)/shard_map/all_to_all | solution.py:192
  132.9 0.8 far_sum.1
  (1 shorter events, 0.0 us)
Async XLA Ops:
  0.6 0.8 copy-start
  0.6 41.5 %copy-start.1 = (bf16[8,48,1536]{2,1,0:T(8,128)(2,1)S(1)}, bf16[8,48,1536]{2,1,0:T(8,128)(2,1)}, u32[]{:S(2)}) copy-start(bf16[8,48,1536]{2,1,0:T(8,128)(2,1)} %mine.3) | copy-start | bytes 3538948
  2.4 39.8 %all-to-all-start = ((bf16[32,48,256]{2,1,0:T(8,128)(2,1)}), bf16[32,48,256]{2,1,0:T(8,128)(2,1)S(1)}, u32[]{:S(2)}, u32[]{:S(2)}) async-start(bf16[32,48,256]{2,1,0:T(8,128)(2,1)} %broadcast_in_dim.9), calls=%async_computation | async-start | bytes 1572864 | tf_op jit(solution)/shard_map/all_to_all | solution.py:166
  18.3 5.0 %collective-permute-start = (bf16[8,48,1536]{2,1,0:T(8,128)(2,1)}, bf16[8,48,1536]{2,1,0:T(8,128)(2,1)S(1)}, u32[]{:S(2)}, u32[]{:S(2)}) collective-permute-start(bf16[8,48,1536]{2,1,0:T(8,128)(2,1)} %mine.3), channel_id=1, source_target_pairs={{0,32},{32,0},{1,33},{33,1},{2,34},{34,2},{3,35},{35,3},{4,36},{36... | collective-permute-start | bytes 3538952 | tf_op jit(solution)/shard_map/ppermute | solution.py:164
  74.2 4.3 %collective-permute-start.1 = (bf16[32,104,128]{2,1,0:T(8,128)(2,1)S(1)}, bf16[32,104,128]{2,1,0:T(8,128)(2,1)S(1)}, u32[]{:S(2)}, u32[]{:S(2)}) collective-permute-start(bf16[32,104,128]{2,1,0:T(8,128)(2,1)S(1)} %all_to_all.20), channel_id=1, source_target_pairs={{0,32},{32,0},{1,33},{33,1},{2,34},{34,2},{3,35},{35,3},{4,36},{36... | collective-permute-start | bytes 2555912 | tf_op jit(solution)/shard_map/ppermute | solution.py:177

commit v12 on v11

--- a/solution.py
+++ b/solution.py
@@ -17,6 +17,19 @@
 def words(value):
     high = value.astype(bf16)
     return high, (value - high.astype(f32)).astype(bf16)
+
+
+def packed_words(block):
+    high = block.astype(bf16).astype(f32)
+    both = jnp.concatenate([high, block - high])
+    rest = jnp.concatenate([both[72:, 32 * k : 32 * (k + 1)] for k in range(3)])
+    return jnp.concatenate([both[:72], rest], axis=1).astype(bf16)
+
+
+def unpacked_words(block):
+    rest = jnp.concatenate([block[24 * k : 24 * (k + 1), 96:] for k in range(3)], axis=1)
+    both = jnp.concatenate([block[:, :96], rest])
+    return both[:48] + both[48:]
 
 
 def vector_lanes(core, count, width):
@@ -86,6 +99,7 @@
                     riders += source[y, b, za, 2 * rows : 2 * rows + 8].astype(f32)
     weights = riders[0:1] + riders[1:2]
     weights = jnp.sum(jnp.where(vector_lanes(core, count, half), weights, 0.0), axis=1, keepdims=True)
+    shares = [[] for _ in range(8)]
     for part in range(3):
         at = pl.ds(part * 16, 16)
         total = jnp.zeros((16, nao), f32)
@@ -97,11 +111,9 @@
             piece = jnp.where(
                 core == 0, total[:, start : start + 2 * rows], total[:, start + 2 * rows : start + 4 * rows]
             )
-            high, low = words(piece)
-            gap = jnp.zeros((16, half - 2 * rows), bf16)
-            out[s, 4 * rows : 4 * rows + 16, part * 256 : (part + 1) * 256] = jnp.concatenate(
-                [high, gap, low, gap], axis=1
-            )
+            shares[s].append(piece)
+    for s in range(8):
+        out[s, 24 * rows :] = packed_words(jnp.concatenate(shares[s]))
 
     for n in range(3):
         block = lax.dot_general(
@@ -111,16 +123,20 @@
             preferred_element_type=f32,
         ).astype(bf16)
         for s in range(8):
-            out[s, 0 : 4 * rows, n * 256 : (n + 1) * 256] = block[s * 4 * rows : (s + 1) * 4 * rows]
+            for g in range(2):
+                at = pl.ds((2 * n + g) * 4 * rows, 4 * rows)
+                out[s, at] = block[s * 4 * rows : (s + 1) * 4 * rows, g * 128 : (g + 1) * 128]
 
 
 def near_sum_kernel(parts, out, tail):
-    rows = parts.shape[2] // 16
+    rows = out.shape[1] // 3 * 2
     deep = 4 * rows
-    tail[...] = jnp.sum(parts[:, deep : deep + 16].astype(f32), axis=0)
+    tail[...] = jnp.sum(parts[:, 6 * deep :].astype(f32), axis=0)
     for n in range(2):
-        columns = slice(n * 8 * rows, (n + 1) * 8 * rows)
-        turned = jnp.sum(parts[:, 0:deep, columns].astype(f32), axis=0).T
+        groups = range(3 * n, 3 * n + 3)
+        turned = jnp.concatenate(
+            [jnp.sum(parts[:, g * deep : (g + 1) * deep].astype(f32), axis=0).T for g in groups]
+        )
         for j in range(8):
             block = turned[j * rows : (j + 1) * rows]
             rest = jnp.concatenate([block[: rows // 2, 128:], block[rows // 2 :, 128:]], axis=1)
@@ -131,10 +147,7 @@
 
 def far_sum_kernel(parts, tail, out, coulomb):
     rows = out.shape[1]
-    for part in range(3):
-        high = slice(part * 256, part * 256 + 2 * rows)
-        low = slice(part * 256 + 128, part * 256 + 128 + 2 * rows)
-        coulomb[part * 16 : (part + 1) * 16] = tail[:, high] + tail[:, low]
+    coulomb[...] = unpacked_words(tail[...])
     total = jnp.sum(parts[...].astype(f32), axis=0)
     rest = jnp.concatenate([total[rows:, :64], total[rows:, 64:]], axis=0)
     out[0] = total[:rows, : 2 * rows]
@@ -159,7 +172,7 @@
     wide = coeffs.shape[2]
     half = wide // 2
     tall = 2 * rows + 8
-    deep = 4 * rows + 16
+    deep = 24 * rows + 72
 
     other_vectors = lax.ppermute(vectors, "core", SWAP)
     own = lax.dynamic_index_in_dim(coeffs, core, 0, keepdims=False)
@@ -181,13 +194,13 @@
         exchange_kernel,
         "exchange_quarter",
         24,
-        [((8, deep, 16 * rows), bf16)],
+        [((8, deep, 128), bf16)],
         (got.reshape(shape), got_other.reshape(shape), vectors, other_vectors),
         scratch,
     )
     parts = lax.all_to_all(parts, NEAR, 0, 0, tiled=True)
     packed, tail = call(
-        near_sum_kernel, "near_sum", 12, [((16, rows + rows // 2, 128), bf16), ((16, 16 * rows), f32)], (parts,)
+        near_sum_kernel, "near_sum", 12, [((16, rows + rows // 2, 128), bf16), ((72, 128), f32)], (parts,)
     )
     packed = lax.all_to_all(packed, SUMS, 0, 0, tiled=True)
     return call(

time: 136 us -> 136 us (level)
  no operation moved by 1% of the time
where the time goes in v12:
time: 136 us; the launch traced here: 133 us
  blocking collectives  82.8 us (61%)
  waiting for transfers between devices  24.2 us (18%)
  starting transfers between devices  19.8 us (15%)
  Pallas kernels  4.14 us (3%)
  local copies, waits for them, and re-layouts  1.74 us (1%)
    all_to_all x1, blocking collectives, on_device(): parts = lax.all_to_all(parts, NEAR, 0, 0, tiled=True)  34.8 us
    all_to_all x1, blocking collectives, on_device(): got = lax.all_to_all(pieces.reshape(32, tall, half), FAR, 0, 0, tiled=True)  31.1 us
    all_to_all x1, waiting for transfers between devices, on_device(): lax.all_to_all(jnp.broadcast_to(own[None], (32, rows, wide)), FAR, 0, 0,...  18.9 us
    all_to_all x1, blocking collectives, on_device(): packed = lax.all_to_all(packed, SUMS, 0, 0, tiled=True)  16.9 us
    all_to_all x1, starting transfers between devices, on_device(): lax.all_to_all(jnp.broadcast_to(own[None], (32, rows, wide)), FAR, 0, 0,...  16 us
    pallas_call x4, Pallas kernels, call(): pl.pallas_call(kernel, out_shape=[jax.ShapeDtypeStruct(shape, dtype) for...  4.14 us
    ppermute x1, waiting for transfers between devices, on_device(): other_vectors = lax.ppermute(vectors, 'core', SWAP)  3.02 us
  transfers between devices with their start and end apart: 3, of which 3 were waited for; matrix products, arithmetic and copies ran while one was open for 0% of the time, Pallas kernels for 0%

profile of v12, /device:TPU:6, one launch (start us, length us, event | category | flops | bytes accessed | tf_op | source)
XLA Modules:
  0.0 133.4 jit_solution(7000398022920705489)
XLA Ops:
  0.6 0.0 copy-start
  0.6 0.0 copy-start.1
  0.7 0.8 copy-done
  1.4 0.9 broadcast_in_dim.9
  2.4 16.0 %all-to-all-start = ((bf16[32,48,256]{2,1,0:T(8,128)(2,1)}), bf16[32,48,256]{2,1,0:T(8,128)(2,1)S(1)}, u32[]{:S(2)}, u32[]{:S(2)}) async-start(bf16[32,48,256]{2,1,0:T(8,128)(2,1)} %broadcast_in_dim.9), calls=%async_computation | async-start | bytes 1572864 | tf_op jit(solution)/shard_map/all_to_all | solution.py:179
  18.3 1.9 %collective-permute-start = (bf16[8,48,1536]{2,1,0:T(8,128)(2,1)}, bf16[8,48,1536]{2,1,0:T(8,128)(2,1)S(1)}, u32[]{:S(2)}, u32[]{:S(2)}) collective-permute-start(bf16[8,48,1536]{2,1,0:T(8,128)(2,1)} %mine.3), channel_id=1, source_target_pairs={{0,32},{32,0},{1,33},{33,1},{2,34},{34,2},{3,35},{35,3},{4,36},{36... | collective-permute-start | bytes 3538952 | tf_op jit(solution)/shard_map/ppermute | solution.py:177
  20.3 3.0 %collective-permute-done.other = bf16[8,48,1536]{2,1,0:T(8,128)(2,1)S(1)} collective-permute-done((bf16[8,48,1536]{2,1,0:T(8,128)(2,1)}, bf16[8,48,1536]{2,1,0:T(8,128)(2,1)S(1)}, u32[]{:S(2)}, u32[]{:S(2)}) %collective-permute-start) | collective-permute-done | bytes 1179680 | tf_op jit(solution)/shard_map/ppermute | solution.py:177
  23.3 18.9 %all-to-all-done = bf16[32,48,256]{2,1,0:T(8,128)(2,1)S(1)} async-done(((bf16[32,48,256]{2,1,0:T(8,128)(2,1)}), bf16[32,48,256]{2,1,0:T(8,128)(2,1)S(1)}, u32[]{:S(2)}, u32[]{:S(2)}) %all-to-all-start) | async-done | bytes 786464 | tf_op jit(solution)/shard_map/all_to_all | solution.py:179
  42.2 0.0 copy-done.1
  42.2 0.9 half_transform.1
  43.1 31.1 %all_to_all.20 = bf16[32,104,128]{2,1,0:T(8,128)(2,1)S(1)} all-to-all(bf16[32,104,128]{2,1,0:T(8,128)(2,1)S(1)} %bitcast.7), channel_id=1, replica_groups=mesh['zl'=2,'x'=4,'core'=2,'y'=8,'zb'=2,'za'=2] {'y','zb','za'}, dimensions={0} | all-to-all | bytes 1703936 | tf_op jit(solution)/shard_map/all_to_all | solution.py:189
  74.2 1.9 %collective-permute-start.1 = (bf16[32,104,128]{2,1,0:T(8,128)(2,1)S(1)}, bf16[32,104,128]{2,1,0:T(8,128)(2,1)S(1)}, u32[]{:S(2)}, u32[]{:S(2)}) collective-permute-start(bf16[32,104,128]{2,1,0:T(8,128)(2,1)S(1)} %all_to_all.20), channel_id=1, source_target_pairs={{0,32},{32,0},{1,33},{33,1},{2,34},{34,2},{3,35},{35,3},{4,36},{36... | collective-permute-start | bytes 2555912 | tf_op jit(solution)/shard_map/ppermute | solution.py:190
  76.1 2.3 %collective-permute-done.1 = bf16[32,104,128]{2,1,0:T(8,128)(2,1)S(1)} collective-permute-done((bf16[32,104,128]{2,1,0:T(8,128)(2,1)S(1)}, bf16[32,104,128]{2,1,0:T(8,128)(2,1)S(1)}, u32[]{:S(2)}, u32[]{:S(2)}) %collective-permute-start.1) | collective-permute-done | bytes 852000 | tf_op jit(solution)/shard_map/ppermute | solution.py:190
  78.4 2.0 %exchange_quarter.1 = bf16[8,1224,128]{2,1,0:T(8,128)(2,1)S(1)} custom-call(bf16[8,2,2,104,128]{4,3,2,1,0:T(8,128)(2,1)S(1)} %bitcast.6, bf16[8,2,2,104,128]{4,3,2,1,0:T(8,128)(2,1)S(1)} %bitcast.9, bf16[8,48,1536]{2,1,0:T(8,128)(2,1)S(1)} %copy-done.1, bf16[8,48,1536]{2,1,0:T(8,128)(2,1)S(1)} %collective-permute-done.other), custom_call_target="tpu_custom_call" | custom-call | tf_op jit(solution)/shard_map/exchange_quarter/pallas_call | solution.py:158
  80.5 34.8 %all_to_all.21.parts = bf16[8,1224,128]{2,1,0:T(8,128)(2,1)S(1)} all-to-all(bf16[8,1224,128]{2,1,0:T(8,128)(2,1)S(1)} %exchange_quarter.1), channel_id=1, replica_groups=mesh['zl'=2,'x'=4,'core'=2,'y'=8,'zb'=2,'za'=2] {'zl','x'}, dimensions={0} | all-to-all | bytes 5013504 | tf_op jit(solution)/shard_map/all_to_all | solution.py:201
  115.3 0.4 near_sum.1
  115.7 16.9 %all_to_all.22.parts = bf16[16,72,128]{2,1,0:T(8,128)(2,1)S(1)} all-to-all(bf16[16,72,128]{2,1,0:T(8,128)(2,1)S(1)} %get-tuple-element.4), channel_id=1, replica_groups=mesh['zl'=2,'x'=4,'core'=2,'y'=8,'zb'=2,'za'=2] {'za','y'}, dimensions={0} | all-to-all | bytes 589824 | tf_op jit(solution)/shard_map/all_to_all | solution.py:205
  132.7 0.8 far_sum.1
  (1 shorter events, 0.0 us)
Async XLA Ops:
  0.6 0.8 copy-start
  0.6 41.5 %copy-start.1 = (bf16[8,48,1536]{2,1,0:T(8,128)(2,1)S(1)}, bf16[8,48,1536]{2,1,0:T(8,128)(2,1)}, u32[]{:S(2)}) copy-start(bf16[8,48,1536]{2,1,0:T(8,128)(2,1)} %mine.3) | copy-start | bytes 3538948
  2.4 39.8 %all-to-all-start = ((bf16[32,48,256]{2,1,0:T(8,128)(2,1)}), bf16[32,48,256]{2,1,0:T(8,128)(2,1)S(1)}, u32[]{:S(2)}, u32[]{:S(2)}) async-start(bf16[32,48,256]{2,1,0:T(8,128)(2,1)} %broadcast_in_dim.9), calls=%async_computation | async-start | bytes 1572864 | tf_op jit(solution)/shard_map/all_to_all | solution.py:179
  18.3 5.0 %collective-permute-start = (bf16[8,48,1536]{2,1,0:T(8,128)(2,1)}, bf16[8,48,1536]{2,1,0:T(8,128)(2,1)S(1)}, u32[]{:S(2)}, u32[]{:S(2)}) collective-permute-start(bf16[8,48,1536]{2,1,0:T(8,128)(2,1)} %mine.3), channel_id=1, source_target_pairs={{0,32},{32,0},{1,33},{33,1},{2,34},{34,2},{3,35},{35,3},{4,36},{36... | collective-permute-start | bytes 3538952 | tf_op jit(solution)/shard_map/ppermute | solution.py:177
  74.2 4.3 %collective-permute-start.1 = (bf16[32,104,128]{2,1,0:T(8,128)(2,1)S(1)}, bf16[32,104,128]{2,1,0:T(8,128)(2,1)S(1)}, u32[]{:S(2)}, u32[]{:S(2)}) collective-permute-start(bf16[32,104,128]{2,1,0:T(8,128)(2,1)S(1)} %all_to_all.20), channel_id=1, source_target_pairs={{0,32},{32,0},{1,33},{33,1},{2,34},{34,2},{3,35},{35,3},{4,36},{36... | collective-permute-start | bytes 2555912 | tf_op jit(solution)/shard_map/ppermute | solution.py:190

commit v13 on v12

--- a/solution.py
+++ b/solution.py
@@ -21,15 +21,14 @@
 
 def packed_words(block):
     high = block.astype(bf16).astype(f32)
-    both = jnp.concatenate([high, block - high])
-    rest = jnp.concatenate([both[72:, 32 * k : 32 * (k + 1)] for k in range(3)])
-    return jnp.concatenate([both[:72], rest], axis=1).astype(bf16)
+    low = block - high
+    rest = jnp.concatenate([low[:24, 32:], low[24:, 32:]], axis=1)
+    return jnp.concatenate([jnp.concatenate([high, low[:, :32]], axis=1), rest]).astype(bf16)
 
 
 def unpacked_words(block):
-    rest = jnp.concatenate([block[24 * k : 24 * (k + 1), 96:] for k in range(3)], axis=1)
-    both = jnp.concatenate([block[:, :96], rest])
-    return both[:48] + both[48:]
+    rest = jnp.concatenate([block[48:, :64], block[48:, 64:]])
+    return block[:48, :96] + jnp.concatenate([block[:48, 96:], rest], axis=1)
 
 
 def vector_lanes(core, count, width):
@@ -106,12 +105,9 @@
         for k, source in enumerate((mine, other)):
             for p in range(count):
                 total += weights[k * count + p : k * count + p + 1] * source[p, at].astype(f32)
+        total = jnp.where(core == 0, total, pltpu.roll(total, nao - 2 * rows, 1))
         for s in range(8):
-            start = s * 4 * rows
-            piece = jnp.where(
-                core == 0, total[:, start : start + 2 * rows], total[:, start + 2 * rows : start + 4 * rows]
-            )
-            shares[s].append(piece)
+            shares[s].append(total[:, s * 4 * rows : s * 4 * rows + 2 * rows])
     for s in range(8):
         out[s, 24 * rows :] = packed_words(jnp.concatenate(shares[s]))
 

time: 136 us -> 136 us (level)
  no operation moved by 1% of the time
where the time goes in v13:
time: 136 us; the launch traced here: 133 us
  blocking collectives  82.8 us (61%)
  waiting for transfers between devices  24.2 us (18%)
  starting transfers between devices  19.8 us (15%)
  Pallas kernels  3.88 us (3%)
  local copies, waits for them, and re-layouts  1.74 us (1%)
    all_to_all x1, blocking collectives, on_device(): parts = lax.all_to_all(parts, NEAR, 0, 0, tiled=True)  34.8 us
    all_to_all x1, blocking collectives, on_device(): got = lax.all_to_all(pieces.reshape(32, tall, half), FAR, 0, 0, tiled=True)  31.1 us
    all_to_all x1, waiting for transfers between devices, on_device(): lax.all_to_all(jnp.broadcast_to(own[None], (32, rows, wide)), FAR, 0, 0,...  18.9 us
    all_to_all x1, blocking collectives, on_device(): packed = lax.all_to_all(packed, SUMS, 0, 0, tiled=True)  16.9 us
    all_to_all x1, starting transfers between devices, on_device(): lax.all_to_all(jnp.broadcast_to(own[None], (32, rows, wide)), FAR, 0, 0,...  16 us
    pallas_call x4, Pallas kernels, call(): pl.pallas_call(kernel, out_shape=[jax.ShapeDtypeStruct(shape, dtype) for...  3.88 us
    ppermute x1, waiting for transfers between devices, on_device(): other_vectors = lax.ppermute(vectors, 'core', SWAP)  3.02 us
  transfers between devices with their start and end apart: 3, of which 3 were waited for; matrix products, arithmetic and copies ran while one was open for 0% of the time, Pallas kernels for 0%

profile of v13, /device:TPU:6, one launch (start us, length us, event | category | flops | bytes accessed | tf_op | source)
XLA Modules:
  0.0 133.2 jit_solution(7706181388607522542)
XLA Ops:
  0.6 0.0 copy-start
  0.6 0.0 copy-start.1
  0.7 0.8 copy-done
  1.4 0.9 broadcast_in_dim.9
  2.4 16.0 %all-to-all-start = ((bf16[32,48,256]{2,1,0:T(8,128)(2,1)}), bf16[32,48,256]{2,1,0:T(8,128)(2,1)S(1)}, u32[]{:S(2)}, u32[]{:S(2)}) async-start(bf16[32,48,256]{2,1,0:T(8,128)(2,1)} %broadcast_in_dim.9), calls=%async_computation | async-start | bytes 1572864 | tf_op jit(solution)/shard_map/all_to_all | solution.py:175
  18.3 1.9 %collective-permute-start = (bf16[8,48,1536]{2,1,0:T(8,128)(2,1)}, bf16[8,48,1536]{2,1,0:T(8,128)(2,1)S(1)}, u32[]{:S(2)}, u32[]{:S(2)}) collective-permute-start(bf16[8,48,1536]{2,1,0:T(8,128)(2,1)} %mine.3), channel_id=1, source_target_pairs={{0,32},{32,0},{1,33},{33,1},{2,34},{34,2},{3,35},{35,3},{4,36},{36... | collective-permute-start | bytes 3538952 | tf_op jit(solution)/shard_map/ppermute | solution.py:173
  20.3 3.0 %collective-permute-done.other = bf16[8,48,1536]{2,1,0:T(8,128)(2,1)S(1)} collective-permute-done((bf16[8,48,1536]{2,1,0:T(8,128)(2,1)}, bf16[8,48,1536]{2,1,0:T(8,128)(2,1)S(1)}, u32[]{:S(2)}, u32[]{:S(2)}) %collective-permute-start) | collective-permute-done | bytes 1179680 | tf_op jit(solution)/shard_map/ppermute | solution.py:173
  23.3 18.9 %all-to-all-done = bf16[32,48,256]{2,1,0:T(8,128)(2,1)S(1)} async-done(((bf16[32,48,256]{2,1,0:T(8,128)(2,1)}), bf16[32,48,256]{2,1,0:T(8,128)(2,1)S(1)}, u32[]{:S(2)}, u32[]{:S(2)}) %all-to-all-start) | async-done | bytes 786464 | tf_op jit(solution)/shard_map/all_to_all | solution.py:175
  42.2 0.0 copy-done.1
  42.2 0.9 half_transform.1
  43.1 31.1 %all_to_all.20 = bf16[32,104,128]{2,1,0:T(8,128)(2,1)S(1)} all-to-all(bf16[32,104,128]{2,1,0:T(8,128)(2,1)S(1)} %bitcast.7), channel_id=1, replica_groups=mesh['zl'=2,'x'=4,'core'=2,'y'=8,'zb'=2,'za'=2] {'y','zb','za'}, dimensions={0} | all-to-all | bytes 1703936 | tf_op jit(solution)/shard_map/all_to_all | solution.py:185
  74.2 1.9 %collective-permute-start.1 = (bf16[32,104,128]{2,1,0:T(8,128)(2,1)S(1)}, bf16[32,104,128]{2,1,0:T(8,128)(2,1)S(1)}, u32[]{:S(2)}, u32[]{:S(2)}) collective-permute-start(bf16[32,104,128]{2,1,0:T(8,128)(2,1)S(1)} %all_to_all.20), channel_id=1, source_target_pairs={{0,32},{32,0},{1,33},{33,1},{2,34},{34,2},{3,35},{35,3},{4,36},{36... | collective-permute-start | bytes 2555912 | tf_op jit(solution)/shard_map/ppermute | solution.py:186
  76.1 2.3 %collective-permute-done.1 = bf16[32,104,128]{2,1,0:T(8,128)(2,1)S(1)} collective-permute-done((bf16[32,104,128]{2,1,0:T(8,128)(2,1)S(1)}, bf16[32,104,128]{2,1,0:T(8,128)(2,1)S(1)}, u32[]{:S(2)}, u32[]{:S(2)}) %collective-permute-start.1) | collective-permute-done | bytes 852000 | tf_op jit(solution)/shard_map/ppermute | solution.py:186
  78.4 1.8 %exchange_quarter.1 = bf16[8,1224,128]{2,1,0:T(8,128)(2,1)S(1)} custom-call(bf16[8,2,2,104,128]{4,3,2,1,0:T(8,128)(2,1)S(1)} %bitcast.6, bf16[8,2,2,104,128]{4,3,2,1,0:T(8,128)(2,1)S(1)} %bitcast.9, bf16[8,48,1536]{2,1,0:T(8,128)(2,1)S(1)} %copy-done.1, bf16[8,48,1536]{2,1,0:T(8,128)(2,1)S(1)} %collective-permute-done.other), custom_call_target="tpu_custom_call" | custom-call | tf_op jit(solution)/shard_map/exchange_quarter/pallas_call | solution.py:154
  80.2 34.8 %all_to_all.21.parts = bf16[8,1224,128]{2,1,0:T(8,128)(2,1)S(1)} all-to-all(bf16[8,1224,128]{2,1,0:T(8,128)(2,1)S(1)} %exchange_quarter.1), channel_id=1, replica_groups=mesh['zl'=2,'x'=4,'core'=2,'y'=8,'zb'=2,'za'=2] {'zl','x'}, dimensions={0} | all-to-all | bytes 5013504 | tf_op jit(solution)/shard_map/all_to_all | solution.py:197
  115.0 0.4 near_sum.1
  115.5 16.9 %all_to_all.22.parts = bf16[16,72,128]{2,1,0:T(8,128)(2,1)S(1)} all-to-all(bf16[16,72,128]{2,1,0:T(8,128)(2,1)S(1)} %get-tuple-element.4), channel_id=1, replica_groups=mesh['zl'=2,'x'=4,'core'=2,'y'=8,'zb'=2,'za'=2] {'za','y'}, dimensions={0} | all-to-all | bytes 589824 | tf_op jit(solution)/shard_map/all_to_all | solution.py:201
  132.4 0.8 far_sum.1
  (1 shorter events, 0.0 us)
Async XLA Ops:
  0.6 0.8 copy-start
  0.6 41.5 %copy-start.1 = (bf16[8,48,1536]{2,1,0:T(8,128)(2,1)S(1)}, bf16[8,48,1536]{2,1,0:T(8,128)(2,1)}, u32[]{:S(2)}) copy-start(bf16[8,48,1536]{2,1,0:T(8,128)(2,1)} %mine.3) | copy-start | bytes 3538948
  2.4 39.8 %all-to-all-start = ((bf16[32,48,256]{2,1,0:T(8,128)(2,1)}), bf16[32,48,256]{2,1,0:T(8,128)(2,1)S(1)}, u32[]{:S(2)}, u32[]{:S(2)}) async-start(bf16[32,48,256]{2,1,0:T(8,128)(2,1)} %broadcast_in_dim.9), calls=%async_computation | async-start | bytes 1572864 | tf_op jit(solution)/shard_map/all_to_all | solution.py:175
  18.3 5.0 %collective-permute-start = (bf16[8,48,1536]{2,1,0:T(8,128)(2,1)}, bf16[8,48,1536]{2,1,0:T(8,128)(2,1)S(1)}, u32[]{:S(2)}, u32[]{:S(2)}) collective-permute-start(bf16[8,48,1536]{2,1,0:T(8,128)(2,1)} %mine.3), channel_id=1, source_target_pairs={{0,32},{32,0},{1,33},{33,1},{2,34},{34,2},{3,35},{35,3},{4,36},{36... | collective-permute-start | bytes 3538952 | tf_op jit(solution)/shard_map/ppermute | solution.py:173
  74.2 4.3 %collective-permute-start.1 = (bf16[32,104,128]{2,1,0:T(8,128)(2,1)S(1)}, bf16[32,104,128]{2,1,0:T(8,128)(2,1)S(1)}, u32[]{:S(2)}, u32[]{:S(2)}) collective-permute-start(bf16[32,104,128]{2,1,0:T(8,128)(2,1)S(1)} %all_to_all.20), channel_id=1, source_target_pairs={{0,32},{32,0},{1,33},{33,1},{2,34},{34,2},{3,35},{35,3},{4,36},{36... | collective-permute-start | bytes 2555912 | tf_op jit(solution)/shard_map/ppermute | solution.py:186

commit v14 on v13

--- a/solution.py
+++ b/solution.py
@@ -44,12 +44,11 @@
     half = wide // 2
     weight = own[...].astype(f32)
     terms = []
-    for source, owner in ((mine, core), (other, 1 - core)):
-        slab = jnp.dot(
-            source[...].reshape(count * rows, nao), full[...], preferred_element_type=f32
-        ).astype(bf16)
+    both = jnp.concatenate([source[...].reshape(count * rows, nao) for source in (mine, other)])
+    slab = jnp.dot(both, full[...], preferred_element_type=f32).astype(bf16)
+    for k, owner in enumerate((core, 1 - core)):
         for p in range(count):
-            block = slab[p * rows : (p + 1) * rows]
+            block = slab[(k * count + p) * rows : (k * count + p + 1) * rows]
             for zb in range(2):
                 out[owner * (count // 2) + p // 2, zb, p % 2, 0:rows] = block[:, :half]
                 out[owner * (count // 2) + p // 2, zb, p % 2, rows : 2 * rows] = block[:, half:]

time: 136 us -> 136 us (level)
  no operation moved by 1% of the time
where the time goes in v14:
time: 136 us; the launch traced here: 133 us
  blocking collectives  82.8 us (61%)
  waiting for transfers between devices  24.2 us (18%)
  starting transfers between devices  19.8 us (15%)
  Pallas kernels  3.85 us (3%)
  local copies, waits for them, and re-layouts  1.74 us (1%)
    all_to_all x1, blocking collectives, on_device(): parts = lax.all_to_all(parts, NEAR, 0, 0, tiled=True)  34.8 us
    all_to_all x1, blocking collectives, on_device(): got = lax.all_to_all(pieces.reshape(32, tall, half), FAR, 0, 0, tiled=True)  31.1 us
    all_to_all x1, waiting for transfers between devices, on_device(): lax.all_to_all(jnp.broadcast_to(own[None], (32, rows, wide)), FAR, 0, 0,...  18.9 us
    all_to_all x1, blocking collectives, on_device(): packed = lax.all_to_all(packed, SUMS, 0, 0, tiled=True)  16.9 us
    all_to_all x1, starting transfers between devices, on_device(): lax.all_to_all(jnp.broadcast_to(own[None], (32, rows, wide)), FAR, 0, 0,...  16 us
    pallas_call x4, Pallas kernels, call(): pl.pallas_call(kernel, out_shape=[jax.ShapeDtypeStruct(shape, dtype) for...  3.85 us
    ppermute x1, waiting for transfers between devices, on_device(): other_vectors = lax.ppermute(vectors, 'core', SWAP)  3.02 us
  transfers between devices with their start and end apart: 3, of which 3 were waited for; matrix products, arithmetic and copies ran while one was open for 0% of the time, Pallas kernels for 0%

profile of v14, /device:TPU:6, one launch (start us, length us, event | category | flops | bytes accessed | tf_op | source)
XLA Modules:
  0.0 133.1 jit_solution(12802590521103879693)
XLA Ops:
  0.6 0.0 copy-start
  0.6 0.0 copy-start.1
  0.7 0.8 copy-done
  1.4 0.9 broadcast_in_dim.9
  2.4 16.0 %all-to-all-start = ((bf16[32,48,256]{2,1,0:T(8,128)(2,1)}), bf16[32,48,256]{2,1,0:T(8,128)(2,1)S(1)}, u32[]{:S(2)}, u32[]{:S(2)}) async-start(bf16[32,48,256]{2,1,0:T(8,128)(2,1)} %broadcast_in_dim.9), calls=%async_computation | async-start | bytes 1572864 | tf_op jit(solution)/shard_map/all_to_all | solution.py:174
  18.3 1.9 %collective-permute-start = (bf16[8,48,1536]{2,1,0:T(8,128)(2,1)}, bf16[8,48,1536]{2,1,0:T(8,128)(2,1)S(1)}, u32[]{:S(2)}, u32[]{:S(2)}) collective-permute-start(bf16[8,48,1536]{2,1,0:T(8,128)(2,1)} %mine.3), channel_id=1, source_target_pairs={{0,32},{32,0},{1,33},{33,1},{2,34},{34,2},{3,35},{35,3},{4,36},{36... | collective-permute-start | bytes 3538952 | tf_op jit(solution)/shard_map/ppermute | solution.py:172
  20.3 3.0 %collective-permute-done.other = bf16[8,48,1536]{2,1,0:T(8,128)(2,1)S(1)} collective-permute-done((bf16[8,48,1536]{2,1,0:T(8,128)(2,1)}, bf16[8,48,1536]{2,1,0:T(8,128)(2,1)S(1)}, u32[]{:S(2)}, u32[]{:S(2)}) %collective-permute-start) | collective-permute-done | bytes 1179680 | tf_op jit(solution)/shard_map/ppermute | solution.py:172
  23.3 18.9 %all-to-all-done = bf16[32,48,256]{2,1,0:T(8,128)(2,1)S(1)} async-done(((bf16[32,48,256]{2,1,0:T(8,128)(2,1)}), bf16[32,48,256]{2,1,0:T(8,128)(2,1)S(1)}, u32[]{:S(2)}, u32[]{:S(2)}) %all-to-all-start) | async-done | bytes 786464 | tf_op jit(solution)/shard_map/all_to_all | solution.py:174
  42.2 0.0 copy-done.1
  42.2 0.9 half_transform.1
  43.1 31.1 %all_to_all.20 = bf16[32,104,128]{2,1,0:T(8,128)(2,1)S(1)} all-to-all(bf16[32,104,128]{2,1,0:T(8,128)(2,1)S(1)} %bitcast.7), channel_id=1, replica_groups=mesh['zl'=2,'x'=4,'core'=2,'y'=8,'zb'=2,'za'=2] {'y','zb','za'}, dimensions={0} | all-to-all | bytes 1703936 | tf_op jit(solution)/shard_map/all_to_all | solution.py:184
  74.2 1.9 %collective-permute-start.1 = (bf16[32,104,128]{2,1,0:T(8,128)(2,1)S(1)}, bf16[32,104,128]{2,1,0:T(8,128)(2,1)S(1)}, u32[]{:S(2)}, u32[]{:S(2)}) collective-permute-start(bf16[32,104,128]{2,1,0:T(8,128)(2,1)S(1)} %all_to_all.20), channel_id=1, source_target_pairs={{0,32},{32,0},{1,33},{33,1},{2,34},{34,2},{3,35},{35,3},{4,36},{36... | collective-permute-start | bytes 2555912 | tf_op jit(solution)/shard_map/ppermute | solution.py:185
  76.1 2.3 %collective-permute-done.1 = bf16[32,104,128]{2,1,0:T(8,128)(2,1)S(1)} collective-permute-done((bf16[32,104,128]{2,1,0:T(8,128)(2,1)S(1)}, bf16[32,104,128]{2,1,0:T(8,128)(2,1)S(1)}, u32[]{:S(2)}, u32[]{:S(2)}) %collective-permute-start.1) | collective-permute-done | bytes 852000 | tf_op jit(solution)/shard_map/ppermute | solution.py:185
  78.4 1.8 %exchange_quarter.1 = bf16[8,1224,128]{2,1,0:T(8,128)(2,1)S(1)} custom-call(bf16[8,2,2,104,128]{4,3,2,1,0:T(8,128)(2,1)S(1)} %bitcast.6, bf16[8,2,2,104,128]{4,3,2,1,0:T(8,128)(2,1)S(1)} %bitcast.9, bf16[8,48,1536]{2,1,0:T(8,128)(2,1)S(1)} %copy-done.1, bf16[8,48,1536]{2,1,0:T(8,128)(2,1)S(1)} %collective-permute-done.other), custom_call_target="tpu_custom_call" | custom-call | tf_op jit(solution)/shard_map/exchange_quarter/pallas_call | solution.py:153
  80.2 34.8 %all_to_all.21.parts = bf16[8,1224,128]{2,1,0:T(8,128)(2,1)S(1)} all-to-all(bf16[8,1224,128]{2,1,0:T(8,128)(2,1)S(1)} %exchange_quarter.1), channel_id=1, replica_groups=mesh['zl'=2,'x'=4,'core'=2,'y'=8,'zb'=2,'za'=2] {'zl','x'}, dimensions={0} | all-to-all | bytes 5013504 | tf_op jit(solution)/shard_map/all_to_all | solution.py:196
  115.0 0.4 near_sum.1
  115.4 16.9 %all_to_all.22.parts = bf16[16,72,128]{2,1,0:T(8,128)(2,1)S(1)} all-to-all(bf16[16,72,128]{2,1,0:T(8,128)(2,1)S(1)} %get-tuple-element.4), channel_id=1, replica_groups=mesh['zl'=2,'x'=4,'core'=2,'y'=8,'zb'=2,'za'=2] {'za','y'}, dimensions={0} | all-to-all | bytes 589824 | tf_op jit(solution)/shard_map/all_to_all | solution.py:200
  132.4 0.8 far_sum.1
  (1 shorter events, 0.0 us)
Async XLA Ops:
  0.6 0.8 copy-start
  0.6 41.5 %copy-start.1 = (bf16[8,48,1536]{2,1,0:T(8,128)(2,1)S(1)}, bf16[8,48,1536]{2,1,0:T(8,128)(2,1)}, u32[]{:S(2)}) copy-start(bf16[8,48,1536]{2,1,0:T(8,128)(2,1)} %mine.3) | copy-start | bytes 3538948
  2.4 39.8 %all-to-all-start = ((bf16[32,48,256]{2,1,0:T(8,128)(2,1)}), bf16[32,48,256]{2,1,0:T(8,128)(2,1)S(1)}, u32[]{:S(2)}, u32[]{:S(2)}) async-start(bf16[32,48,256]{2,1,0:T(8,128)(2,1)} %broadcast_in_dim.9), calls=%async_computation | async-start | bytes 1572864 | tf_op jit(solution)/shard_map/all_to_all | solution.py:174
  18.3 5.0 %collective-permute-start = (bf16[8,48,1536]{2,1,0:T(8,128)(2,1)}, bf16[8,48,1536]{2,1,0:T(8,128)(2,1)S(1)}, u32[]{:S(2)}, u32[]{:S(2)}) collective-permute-start(bf16[8,48,1536]{2,1,0:T(8,128)(2,1)} %mine.3), channel_id=1, source_target_pairs={{0,32},{32,0},{1,33},{33,1},{2,34},{34,2},{3,35},{35,3},{4,36},{36... | collective-permute-start | bytes 3538952 | tf_op jit(solution)/shard_map/ppermute | solution.py:172
  74.2 4.3 %collective-permute-start.1 = (bf16[32,104,128]{2,1,0:T(8,128)(2,1)S(1)}, bf16[32,104,128]{2,1,0:T(8,128)(2,1)S(1)}, u32[]{:S(2)}, u32[]{:S(2)}) collective-permute-start(bf16[32,104,128]{2,1,0:T(8,128)(2,1)S(1)} %all_to_all.20), channel_id=1, source_target_pairs={{0,32},{32,0},{1,33},{33,1},{2,34},{34,2},{3,35},{35,3},{4,36},{36... | collective-permute-start | bytes 2555912 | tf_op jit(solution)/shard_map/ppermute | solution.py:185
